TPU v7x, 32 devices: a whole 2x2x4 slice. The times are simulated.
32 devices in a mesh: wide: 16 (over z, x, core), narrow: 2 (over y).
Axes of the slice: x: 2, y: 2, z: 4, core: 2. Of those that a mesh axis runs over, the one named last changes fastest.
Arguments:
- tokens: bfloat16 [16384, 768], P(('wide', 'narrow')), may hold values from -6 to 6
- cotangent: bfloat16 [16384, 768], P(('wide', 'narrow')), may hold values from -6 to 6
- clip_lengths: int32 [32, 3], P(('wide', 'narrow')), may hold values from 0 to 512, as said below
- ln1_gain: bfloat16 [768], P(('wide', 'narrow')), may hold values from 0.099609375 to 1.8984375
- ln1_bias: bfloat16 [768], P(('wide', 'narrow')), may hold values from -3 to 3
- qkv_weight: bfloat16 [768, 2304], P(('wide', 'narrow')), may hold values from -0.21875 to 0.21875
- qv_bias: bfloat16 [1536], P(('wide', 'narrow')), may hold values from -3 to 3
- out_weight: bfloat16 [768, 768], P(('wide', 'narrow')), may hold values from -0.875 to 0.875
- out_bias: bfloat16 [768], P(('wide', 'narrow')), may hold values from -3 to 3
- ln2_gain: bfloat16 [768], P(('wide', 'narrow')), may hold values from 0.099609375 to 1.8984375
- ln2_bias: bfloat16 [768], P(('wide', 'narrow')), may hold values from -3 to 3
- up_weight: bfloat16 [768, 3072], P(('wide', 'narrow')), may hold values from -0.21875 to 0.21875
- up_bias: bfloat16 [3072], P(('wide', 'narrow')), may hold values from -3 to 3
- down_weight: bfloat16 [3072, 768], P(('wide', 'narrow')), may hold values from -0.109375 to 0.109375
- down_bias: bfloat16 [768], P(('wide', 'narrow')), may hold values from -3 to 3
Outputs:
- block_out: bfloat16 [16384, 768], P(('wide', 'narrow'))
- tokens_grad: float32 [16384, 768], P(('wide', 'narrow'))
- ln1_gain_grad: float32 [768], P(('wide', 'narrow'))
- ln1_bias_grad: float32 [768], P(('wide', 'narrow'))
- qkv_weight_grad: float32 [768, 2304], P(('wide', 'narrow'))
- qv_bias_grad: float32 [1536], P(('wide', 'narrow'))
- out_weight_grad: float32 [768, 768], P(('wide', 'narrow'))
- out_bias_grad: float32 [768], P(('wide', 'narrow'))
- ln2_gain_grad: float32 [768], P(('wide', 'narrow'))
- ln2_bias_grad: float32 [768], P(('wide', 'narrow'))
- up_weight_grad: float32 [768, 3072], P(('wide', 'narrow'))
- up_bias_grad: float32 [3072], P(('wide', 'narrow'))
- down_weight_grad: float32 [3072, 768], P(('wide', 'narrow'))
- down_bias_grad: float32 [768], P(('wide', 'narrow'))
Inputs may be any that keep to these rules, and one draw needn't show every extreme that they name: `clip_lengths`: each row is either one clip of 512 tokens followed by empty slots (0), or 3 clips of 129 to 170 tokens each; some row is of the first kind.
All inputs are finite; a program needn't handle non-finite values.
Results may differ from a plain program's by a relative error of at most 0.012.
Values may be sent and summed in bfloat16 or wider, within the bound.
A program may use at most 192 MiB of HBM per device.

v0:
```python
import math

import jax
import jax.numpy as jnp
from jax import lax
from jax.sharding import PartitionSpec as P

H = 12


MASKED_SCORE = -1000000000.0


def layer_norm(inputs, ln_gain, ln_bias):
    row_mean = jnp.mean(inputs, axis=-1, keepdims=True)
    centred = inputs - row_mean
    spread = jnp.mean(centred * centred, axis=-1, keepdims=True)
    return centred * lax.rsqrt(spread + 1e-06) * ln_gain + ln_bias


def gelu_exact(inputs):
    return 0.5 * inputs * (1.0 + lax.erf(inputs * 0.7071067811865476))


def clip_index(lengths, row_count):
    clip_ends = jnp.cumsum(lengths)
    position = jnp.arange(row_count, dtype=jnp.int32)
    return jnp.sum((position[:, None] >= clip_ends[None, :]).astype(jnp.int32), axis=1)


def split_heads(matrix, head_count):
    row_count = matrix.shape[0]
    return matrix.reshape(row_count, head_count, -1).transpose(1, 0, 2)


def join_heads(stacked):
    head_count, row_count, head_size = stacked.shape
    return stacked.transpose(1, 0, 2).reshape(row_count, head_count * head_size)


def attend_forward(queries, key_rows, value_rows, segment, block_rows, score_scale):
    scores = (
        lax.dot_general(
            queries, key_rows, (((1,), (1,)), ((), ())), preferred_element_type=jnp.float32
        )
        * score_scale
    )
    allowed = segment[0:block_rows, None] == segment[None, :]
    scores = jnp.where(allowed, scores, MASKED_SCORE)
    highest = jnp.max(scores, axis=1, keepdims=True)
    raised = jnp.exp(scores - highest)
    denominator = jnp.sum(raised, axis=1, keepdims=True)
    softmax = (raised / denominator).astype(jnp.bfloat16)
    outputs = [jnp.dot(softmax, value_rows, preferred_element_type=jnp.float32)]
    totals = [highest + jnp.log(denominator)]
    return (jnp.concatenate(outputs, 0), jnp.concatenate(totals, 0))


def attend_backward(
    queries, key_rows, value_rows, segment, grad_out, lse_rows, block_rows, score_scale
):
    grad_keys = jnp.zeros(key_rows.shape, jnp.float32)
    grad_values = jnp.zeros(value_rows.shape, jnp.float32)
    g_rows = grad_out[0:block_rows]
    scores = (
        lax.dot_general(
            queries, key_rows, (((1,), (1,)), ((), ())), preferred_element_type=jnp.float32
        )
        * score_scale
    )
    allowed = segment[0:block_rows, None] == segment[None, :]
    softmax = jnp.where(allowed, jnp.exp(scores - lse_rows[0:block_rows]), 0.0)
    grad_values = grad_values + lax.dot_general(
        softmax.astype(jnp.bfloat16),
        g_rows,
        (((0,), (0,)), ((), ())),
        preferred_element_type=jnp.float32,
    )
    grad_probs = lax.dot_general(
        g_rows, value_rows, (((1,), (1,)), ((), ())), preferred_element_type=jnp.float32
    )
    grad_scores = (
        softmax * (grad_probs - jnp.sum(softmax * grad_probs, axis=1, keepdims=True))
    ).astype(jnp.bfloat16)
    grad_queries = [
        jnp.dot(grad_scores, key_rows, preferred_element_type=jnp.float32) * score_scale
    ]
    grad_keys = (
        grad_keys
        + lax.dot_general(
            grad_scores, queries, (((0,), (0,)), ((), ())), preferred_element_type=jnp.float32
        )
        * score_scale
    )
    return (jnp.concatenate(grad_queries, 0), grad_keys, grad_values)


def on_device(
    tokens,
    cotangent,
    clip_lengths,
    ln1_gain,
    ln1_bias,
    qkv_weight,
    qv_bias,
    out_weight,
    out_bias,
    ln2_gain,
    ln2_bias,
    up_weight,
    up_bias,
    down_weight,
    down_bias,
):
    gathered = (
        lax.all_gather(ln1_gain, ("wide", "narrow"), axis=0, tiled=True),
        lax.all_gather(ln1_bias, ("wide", "narrow"), axis=0, tiled=True),
        lax.all_gather(qkv_weight, ("wide", "narrow"), axis=0, tiled=True),
        lax.all_gather(qv_bias, ("wide", "narrow"), axis=0, tiled=True),
        lax.all_gather(out_weight, ("wide", "narrow"), axis=0, tiled=True),
        lax.all_gather(out_bias, ("wide", "narrow"), axis=0, tiled=True),
        lax.all_gather(ln2_gain, ("wide", "narrow"), axis=0, tiled=True),
        lax.all_gather(ln2_bias, ("wide", "narrow"), axis=0, tiled=True),
        lax.all_gather(up_weight, ("wide", "narrow"), axis=0, tiled=True),
        lax.all_gather(up_bias, ("wide", "narrow"), axis=0, tiled=True),
        lax.all_gather(down_weight, ("wide", "narrow"), axis=0, tiled=True),
        lax.all_gather(down_bias, ("wide", "narrow"), axis=0, tiled=True),
    )
    (
        gain_one,
        bias_one,
        merged_weight,
        merged_bias,
        proj_weight,
        proj_bias,
        gain_two,
        bias_two,
        w_up,
        b_up,
        w_down,
        b_down,
    ) = gathered
    inputs = tokens.astype(jnp.float32)
    row_count, model_width = inputs.shape
    head_size = model_width // H
    score_scale = 1.0 / math.sqrt(head_size)
    block_rows = min(512, row_count)
    clip_count = clip_lengths.shape[1]
    segment = clip_index(clip_lengths[0], row_count)
    live_rows = (segment < clip_count).astype(jnp.float32)[:, None]
    normed_one = layer_norm(
        inputs, gain_one.astype(jnp.float32), bias_one.astype(jnp.float32)
    ).astype(jnp.bfloat16)
    bias_float = merged_bias.astype(jnp.float32)
    full_bias = jnp.concatenate(
        [bias_float[:model_width], jnp.zeros((model_width,), jnp.float32), bias_float[model_width:]]
    )
    merged_rows = (
        jnp.dot(normed_one, merged_weight, preferred_element_type=jnp.float32) + full_bias
    ).astype(jnp.bfloat16)
    q_heads = split_heads(merged_rows[:, :model_width], H)
    k_heads = split_heads(merged_rows[:, model_width : 2 * model_width], H)
    v_heads = split_heads(merged_rows[:, 2 * model_width :], H)

    def head_forward(triple):
        return attend_forward(triple[0], triple[1], triple[2], segment, block_rows, score_scale)

    att_heads, lse_heads = lax.map(head_forward, (q_heads, k_heads, v_heads))
    attended = join_heads(att_heads).astype(jnp.bfloat16)
    branch_one = jnp.dot(
        attended, proj_weight, preferred_element_type=jnp.float32
    ) + proj_bias.astype(jnp.float32)
    middle = inputs + live_rows * branch_one
    normed_two = layer_norm(
        middle, gain_two.astype(jnp.float32), bias_two.astype(jnp.float32)
    ).astype(jnp.bfloat16)
    hidden_pre = jnp.dot(normed_two, w_up, preferred_element_type=jnp.float32) + b_up.astype(
        jnp.float32
    )
    activated, gelu_pull = jax.vjp(gelu_exact, hidden_pre)
    activated = activated.astype(jnp.bfloat16)
    branch_two = jnp.dot(activated, w_down, preferred_element_type=jnp.float32) + b_down.astype(
        jnp.float32
    )
    block_out = (middle + live_rows * branch_two).astype(jnp.bfloat16)
    back_gain_one, back_merged, back_proj, back_gain_two, back_up, back_down = (
        lax.all_gather(ln1_gain, ("wide", "narrow"), axis=0, tiled=True),
        lax.all_gather(qkv_weight, ("wide", "narrow"), axis=0, tiled=True),
        lax.all_gather(out_weight, ("wide", "narrow"), axis=0, tiled=True),
        lax.all_gather(ln2_gain, ("wide", "narrow"), axis=0, tiled=True),
        lax.all_gather(up_weight, ("wide", "narrow"), axis=0, tiled=True),
        lax.all_gather(down_weight, ("wide", "narrow"), axis=0, tiled=True),
    )
    upstream = cotangent.astype(jnp.float32)
    grad_two = (live_rows * upstream).astype(jnp.bfloat16)
    grad_b_down = jnp.sum(grad_two.astype(jnp.float32), axis=0)
    grad_w_down = jnp.einsum("tf,td->fd", activated, grad_two, preferred_element_type=jnp.float32)
    grad_act = jnp.einsum("td,fd->tf", grad_two, back_down, preferred_element_type=jnp.float32)
    grad_hidden = gelu_pull(grad_act)[0].astype(jnp.bfloat16)
    grad_b_up = jnp.sum(grad_hidden.astype(jnp.float32), axis=0)
    grad_w_up = jnp.einsum("td,tf->df", normed_two, grad_hidden, preferred_element_type=jnp.float32)
    grad_normed_two = jnp.einsum(
        "tf,df->td", grad_hidden, back_up, preferred_element_type=jnp.float32
    )
    _, norm_pull_two = jax.vjp(
        layer_norm, middle, back_gain_two.astype(jnp.float32), bias_two.astype(jnp.float32)
    )
    grad_middle_norm, grad_gain_two, grad_bias_two = norm_pull_two(grad_normed_two)
    grad_middle = upstream + grad_middle_norm
    grad_one = (live_rows * grad_middle).astype(jnp.bfloat16)
    grad_b_proj = jnp.sum(grad_one.astype(jnp.float32), axis=0)
    grad_w_proj = jnp.einsum("te,td->ed", attended, grad_one, preferred_element_type=jnp.float32)
    grad_att = jnp.einsum(
        "td,ed->te", grad_one, back_proj, preferred_element_type=jnp.float32
    ).astype(jnp.bfloat16)
    grad_att_heads = split_heads(grad_att, H)

    def head_backward(members):
        return attend_backward(
            members[0],
            members[1],
            members[2],
            segment,
            members[3],
            members[4],
            block_rows,
            score_scale,
        )

    grad_q, grad_k, grad_v = lax.map(
        head_backward, (q_heads, k_heads, v_heads, grad_att_heads, lse_heads)
    )
    grad_merged = jnp.concatenate(
        [join_heads(grad_q), join_heads(grad_k), join_heads(grad_v)], 1
    ).astype(jnp.bfloat16)
    column_sums = jnp.sum(grad_merged.astype(jnp.float32), axis=0)
    grad_merged_bias = jnp.concatenate([column_sums[:model_width], column_sums[2 * model_width :]])
    grad_w_merged = jnp.einsum(
        "te,tf->ef", normed_one, grad_merged, preferred_element_type=jnp.float32
    )
    grad_normed_one = jnp.einsum(
        "tf,ef->te", grad_merged, back_merged, preferred_element_type=jnp.float32
    )
    _, norm_pull_one = jax.vjp(
        layer_norm, inputs, back_gain_one.astype(jnp.float32), bias_one.astype(jnp.float32)
    )
    grad_input_norm, grad_gain_one, grad_bias_one = norm_pull_one(grad_normed_one)
    tokens_grad = grad_middle + grad_input_norm
    shares = (
        lax.psum_scatter(grad_gain_one, ("wide", "narrow"), scatter_dimension=0, tiled=True),
        lax.psum_scatter(grad_bias_one, ("wide", "narrow"), scatter_dimension=0, tiled=True),
        lax.psum_scatter(grad_w_merged, ("wide", "narrow"), scatter_dimension=0, tiled=True),
        lax.psum_scatter(grad_merged_bias, ("wide", "narrow"), scatter_dimension=0, tiled=True),
        lax.psum_scatter(grad_w_proj, ("wide", "narrow"), scatter_dimension=0, tiled=True),
        lax.psum_scatter(grad_b_proj, ("wide", "narrow"), scatter_dimension=0, tiled=True),
        lax.psum_scatter(grad_gain_two, ("wide", "narrow"), scatter_dimension=0, tiled=True),
        lax.psum_scatter(grad_bias_two, ("wide", "narrow"), scatter_dimension=0, tiled=True),
        lax.psum_scatter(grad_w_up, ("wide", "narrow"), scatter_dimension=0, tiled=True),
        lax.psum_scatter(grad_b_up, ("wide", "narrow"), scatter_dimension=0, tiled=True),
        lax.psum_scatter(grad_w_down, ("wide", "narrow"), scatter_dimension=0, tiled=True),
        lax.psum_scatter(grad_b_down, ("wide", "narrow"), scatter_dimension=0, tiled=True),
    )
    return (
        block_out,
        tokens_grad,
        shares[0],
        shares[1],
        shares[2],
        shares[3],
        shares[4],
        shares[5],
        shares[6],
        shares[7],
        shares[8],
        shares[9],
        shares[10],
        shares[11],
    )


def solution(mesh):
    return jax.shard_map(
        on_device,
        mesh=mesh,
        in_specs=(
            P(("wide", "narrow"), None),
            P(("wide", "narrow"), None),
            P(("wide", "narrow"), None),
            P(("wide", "narrow")),
            P(("wide", "narrow")),
            P(("wide", "narrow"), None),
            P(("wide", "narrow")),
            P(("wide", "narrow"), None),
            P(("wide", "narrow")),
            P(("wide", "narrow")),
            P(("wide", "narrow")),
            P(("wide", "narrow"), None),
            P(("wide", "narrow")),
            P(("wide", "narrow"), None),
            P(("wide", "narrow")),
        ),
        out_specs=(
            P(("wide", "narrow"), None),
            P(("wide", "narrow"), None),
            P(("wide", "narrow")),
            P(("wide", "narrow")),
            P(("wide", "narrow"), None),
            P(("wide", "narrow")),
            P(("wide", "narrow"), None),
            P(("wide", "narrow")),
            P(("wide", "narrow")),
            P(("wide", "narrow")),
            P(("wide", "narrow"), None),
            P(("wide", "narrow")),
            P(("wide", "narrow"), None),
            P(("wide", "narrow")),
        ),
        check_vma=False,
    )
```

profile of v0, /device:TPU:0, one launch (start us, length us, event | category | flops | bytes accessed | tf_op | source)
XLA Modules:
  0.0 800.3 jit_solution(938956678701963232)
XLA Ops:
  16.8 42.5 %all-reduce.17 = (bf16[1536]{0:T(1024)(128)(2,1)S(1)}, bf16[768]{0:T(1024)(128)(2,1)S(1)}, bf16[768]{0:T(1024)(128)(2,1)S(1)}, bf16[768]{0:T(1024)(128)(2,1)S(1)...) all-reduce(bf16[1536]{0:T(1024)(128)(2,1)S(1)} %dynamic-update-slic, ...), channel_id=1, replica_groups=mesh['wide'=16,'narrow'=2] {'wide','narrow'}, use_global_device_ids=true, to_apply=%add.2 | all-reduce | flops 9216 | bytes 36864
  62.0 11.9 %all-gather.5.cloned.1.call-done = bf16[768,2304]{1,0:T(8,128)(2,1)} async-done(((bf16[24,2304]{1,0:T(8,128)(2,1)}), bf16[768,2304]{1,0:T(8,128)(2,1)}) %all-gather.5.cloned.1.call-update) | async-done | bytes 3538960 | tf_op jit(solution)/shard_map/all_gather | solution.py:118
  73.9 4.2 fusion.42
  80.2 1.8 copy.58
  82.0 2.3 copy.56
  84.3 2.4 copy.59
  87.9 2.5 copy.60
  90.4 32.2 %while.26 = (s32[]{:T(128)}, bf16[12,512,64]{1,2,0:T(8,128)(2,1)S(1)}, f32[12,512,1]{1,2,0:T(1,128)S(1)}, s32[512]{0:T(512)S(1)}, bf16[12,512,64]{2,1,0:T(8,128)...) while((s32[]{:T(128)}, bf16[12,512,64]{1,2,0:T(8,128)(2,1)S(1)}, ...), condition=%wide.region_7.8_spmd, body=%wide.region_4.7_spmd.sunk | while | flops 69467648 | bytes 3696737 | solution.py:168
  122.7 7.2 all-gather.7.cloned.1.call-done
  129.9 2.2 fusion.76
  132.5 62.9 %all-gather.9.cloned.1.call-done = bf16[768,3072]{1,0:T(8,128)(2,1)} async-done(((bf16[24,3072]{1,0:T(8,128)(2,1)}), bf16[768,3072]{1,0:T(8,128)(2,1)}) %all-gather.9.cloned.1.call-update) | async-done | bytes 4718608 | tf_op jit(solution)/shard_map/all_gather | solution.py:124
  195.4 8.2 %multiply_convert_fusion.1 = (bf16[512,3072]{1,0:T(8,128)(2,1)}, f32[512,3072]{1,0:T(8,128)}) fusion(f32[3072]{0:T(1024)S(1)} %convert_element_type.115, bf16[768,3072]{1,0:T(8,128)(2,1)} %all-gather.9.cloned.1.call-done, f32[512,768]{1,0:T(8,128)S(1)} %get-tuple-element.236, f32[768]{0:T(1024)S(1)} %convert_element_type.113, ...), kind=kOutput, calls=%fused_computation.57 | convolution fusion | flops 2427322368 | bytes 15751168 | tf_op jit(solution)/shard_map/dot_general | solution.py:177
  203.6 57.1 %all-gather.11.cloned.1.call-done = bf16[3072,768]{1,0:T(8,128)(2,1)} async-done(((bf16[96,768]{1,0:T(8,128)(2,1)}), bf16[3072,768]{1,0:T(8,128)(2,1)}) %all-gather.11.cloned.1.call-update) | async-done | bytes 4718608 | tf_op jit(solution)/shard_map/all_gather | solution.py:126
  260.7 8.1 %convert_reduce_fusion = (f32[3072]{0:T(1024)S(1)}, bf16[512,3072]{1,0:T(8,128)(2,1)S(1)}) fusion(bf16[3072,768]{1,0:T(8,128)(2,1)} %all-gather.11.cloned.1.call-done, bf16[512,768]{1,0:T(8,128)(2,1)S(1)} %copy-done.5, f32[512]{0:T(512)S(1)} %compare_convert_fusion, f32[512,3072]{1,0:T(8,128)} %get-tuple-element.238, f32[3072]{0:T(1024)S(1)} %convert_element_type.115), kind=kOutput, calls=%fused_computation.55 | convolution fusion | flops 2442261504 | bytes 14968832 | tf_op jit(solution)/shard_map/td,fd->tf/dot_general | solution.py:198
  268.8 3.0 multiply_reduce_fusion.1
  271.8 2.0 fusion.71
  275.2 2.2 fusion.77
  277.4 3.2 convolution_convert_fusion
  280.5 2.3 copy.61
  285.8 98.7 %while.27 = (s32[]{:T(128)}, bf16[12,512,64]{1,2,0:T(8,128)(2,1)}, bf16[12,512,64]{1,2,0:T(8,128)(2,1)}, bf16[12,512,64]{1,2,0:T(8,128)(2,1)}, s32[512]{0:T(512)...) while((s32[]{:T(128)}, bf16[12,512,64]{1,2,0:T(8,128)(2,1)}, ...), condition=%wide.region_14.15_spmd, body=%wide.region_12.14_spmd.sunk | while | flops 170458624 | bytes 9063545 | solution.py:230
  288.7 1.8 fusion.125
  290.5 1.8 fusion.126
  292.3 1.7 fusion.127
  296.9 1.8 fusion.125
  298.7 1.8 fusion.126
  300.5 1.7 fusion.127
  305.2 1.8 fusion.125
  307.0 1.8 fusion.126
  308.8 1.7 fusion.127
  313.4 1.8 fusion.125
  315.2 1.8 fusion.126
  317.0 1.7 fusion.127
  321.7 1.8 fusion.125
  323.4 1.8 fusion.126
  325.3 1.7 fusion.127
  329.9 1.8 fusion.125
  331.7 1.8 fusion.126
  338.1 1.8 fusion.125
  339.9 1.8 fusion.126
  341.7 1.7 fusion.127
  346.3 1.8 fusion.125
  348.1 1.8 fusion.126
  349.9 1.7 fusion.127
  354.6 1.8 fusion.125
  356.3 1.8 fusion.126
  362.8 1.8 fusion.125
  364.6 1.8 fusion.126
  371.0 1.8 fusion.125
  372.8 1.8 fusion.126
  374.6 1.7 fusion.127
  379.2 1.8 fusion.125
  381.0 1.8 fusion.126
  382.8 1.7 fusion.127
  384.6 6.8 fusion.63
  391.5 8.9 %fusion.68 = f32[768,3072]{1,0:T(8,128)} fusion(bf16[512,3072]{1,0:T(8,128)(2,1)} %copy-done.14, f32[512,768]{1,0:T(8,128)} %copy-done.1, f32[768]{0:T(1024)S(1)} %convert_element_type.113, f32[768]{0:T(1024)S(1)} %convert_element_type.112, f32[512]{0:T(512)S(1)} %fusion.56, f32[512]{0:T(512)S(1)} %broadcast_multiply_fusion), kind=kOutput, calls=%fused_computation.112 | convolution fusion | flops 2417885184 | bytes 14166016 | tf_op jit(solution)/shard_map/td,tf->df/dot_general | solution.py:201
  400.6 8.4 %fusion.57 = f32[3072,768]{1,0:T(8,128)} fusion(bf16[512,3072]{1,0:T(8,128)(2,1)} %get-tuple-element.237, bf16[512,768]{1,0:T(8,128)(2,1)S(1)} %copy-done.5, f32[512]{0:T(512)S(1)} %compare_convert_fusion), kind=kOutput, calls=%fused_computation.107 | convolution fusion | flops 2417098752 | bytes 13371392 | tf_op jit(solution)/shard_map/tf,td->fd/dot_general | solution.py:197
  409.1 2.2 convert_reduce_fusion.1
  411.5 4.4 fusion.70
  417.9 41.4 %all-reduce.16 = (f32[768]{0:T(1024)S(1)}, f32[768]{0:T(1024)S(1)}, f32[1536]{0:T(1024)S(1)}, f32[768]{0:T(1024)S(1)}, f32[768]{0:T(1024)S(1)}, /*index=5*/f32[7...) all-reduce(f32[768]{0:T(1024)S(1)} %get-tuple-element.164, ...), channel_id=2, replica_groups=mesh['wide'=16,'narrow'=2] {'wide','narrow'}, use_global_device_ids=true, to_apply=%region_18.19.clone | all-reduce | flops 9216 | bytes 73728
  464.1 3.5 add_add_fusion.2
  467.5 5.9 add_convert_fusion.1
  473.4 36.8 %reduce-scatter.5.cloned.1.call-done = f32[24,2304]{1,0:T(8,128)} async-done(((f32[768,2304]{1,0:T(8,128)}), f32[24,2304]{1,0:T(8,128)}) %reduce-scatter.5.cloned.1.call-update) | async-done | bytes 221200 | tf_op jit(solution)/shard_map/reduce_scatter | solution.py:252
  510.2 141.5 %reduce-scatter.9.cloned.1.call-done = f32[24,3072]{1,0:T(8,128)} async-done(((f32[768,3072]{1,0:T(8,128)}), f32[24,3072]{1,0:T(8,128)}) %reduce-scatter.9.cloned.1.call-update) | async-done | bytes 294928 | tf_op jit(solution)/shard_map/reduce_scatter | solution.py:258
  651.7 141.8 %reduce-scatter.11.cloned.1.call-done = f32[96,768]{1,0:T(8,128)} async-done(((f32[3072,768]{1,0:T(8,128)}), f32[96,768]{1,0:T(8,128)}) %reduce-scatter.11.cloned.1.call-update) | async-done | bytes 294928 | tf_op jit(solution)/shard_map/reduce_scatter | solution.py:260
  (218 shorter events, 98.8 us)
Async XLA Ops:
  7.2 54.4 %copy-start = (bf16[512,768]{1,0:T(8,128)(2,1)S(1)}, bf16[512,768]{1,0:T(8,128)(2,1)}, u32[]{:S(2)}) copy-start(bf16[512,768]{1,0:T(8,128)(2,1)} %param.19) | copy-start | bytes 2359300
  7.2 66.7 %all-gather.5.cloned.1.call-start = ((), (), s32[]{:S(2)}) async-start(), calls=%async_computation.4 | async-start | bytes 3649536 | tf_op jit(solution)/shard_map/all_gather | solution.py:118
  7.9 122.0 %all-gather.7.cloned.1.call-start = ((), (), s32[]{:S(2)}) async-start(), calls=%async_computation.5 | async-start | bytes 1216512 | tf_op jit(solution)/shard_map/all_gather | solution.py:120
  8.7 186.7 %all-gather.9.cloned.1.call-start = ((), (), s32[]{:S(2)}) async-start(), calls=%async_computation.6 | async-start | bytes 4866048 | tf_op jit(solution)/shard_map/all_gather | solution.py:124
  9.4 251.3 %all-gather.11.cloned.1.call-start = ((), (), s32[]{:S(2)}) async-start(), calls=%async_computation.7 | async-start | bytes 4866048 | tf_op jit(solution)/shard_map/all_gather | solution.py:126
  10.0 463.4 %reduce-scatter.7.cloned.1.call-start = ((), (), s32[]{:S(2)}) async-start(), calls=%async_computation.9 | async-start | bytes 2433024 | tf_op jit(solution)/shard_map/reduce_scatter | solution.py:254
  122.7 7.2 copy-start.4
  122.7 9.5 %copy-start.10 = (bf16[12,512,64]{1,2,0:T(8,128)(2,1)}, bf16[12,512,64]{1,2,0:T(8,128)(2,1)S(1)}, u32[]{:S(2)}) copy-start(bf16[12,512,64]{1,2,0:T(8,128)(2,1)S(1)} %get-tuple-element.106) | copy-start | bytes 2359300
  132.2 136.6 %copy-start.1 = (f32[512,768]{1,0:T(8,128)}, f32[512,768]{1,0:T(8,128)S(1)}, u32[]{:S(2)}) copy-start(f32[512,768]{1,0:T(8,128)S(1)} %get-tuple-element.236) | copy-start | bytes 4718596
  132.5 128.2 %copy-start.5 = (bf16[512,768]{1,0:T(8,128)(2,1)S(1)}, bf16[512,768]{1,0:T(8,128)(2,1)}, u32[]{:S(2)}) copy-start(bf16[512,768]{1,0:T(8,128)(2,1)} %param.20) | copy-start | bytes 2359300
  260.7 8.1 %copy-start.12 = (bf16[768,3072]{1,0:T(8,128)(2,1)S(1)}, bf16[768,3072]{1,0:T(8,128)(2,1)}, u32[]{:S(2)}) copy-start(bf16[768,3072]{1,0:T(8,128)(2,1)} %all-gather.9.cloned.1.call-done) | copy-start | bytes 14155780
  268.7 3.0 copy-start.14
  273.8 1.4 copy-start.11
  274.3 0.9 copy-start.9
  282.9 227.3 %reduce-scatter.5.cloned.1.call-start = ((), (), s32[]{:S(2)}) async-start(), calls=%async_computation.8 | async-start | bytes 7299072 | tf_op jit(solution)/shard_map/reduce_scatter | solution.py:252
  391.4 260.2 %reduce-scatter.9.cloned.1.call-start = ((), (), s32[]{:S(2)}) async-start(), calls=%async_computation.10 | async-start | bytes 9732096 | tf_op jit(solution)/shard_map/reduce_scatter | solution.py:258
  400.4 393.1 %reduce-scatter.11.cloned.1.call-start = ((), (), s32[]{:S(2)}) async-start(), calls=%async_computation.11 | async-start | bytes 9732096 | tf_op jit(solution)/shard_map/reduce_scatter | solution.py:260
  409.1 2.3 copy-start.6
  409.1 2.3 copy-start.7
  409.1 2.5 copy-start.8
  416.0 1.1 copy-start.3
  464.1 3.5 copy-start.2
  464.1 3.5 copy-start.13
Sparse Core Ops, SparseCore 0:
  10.9 62.8 all-gather.4
  76.8 53.0 all-gather.6
  132.8 62.5 all-gather.8
  198.2 62.4 all-gather.10
  283.0 97.8 reduce-scatter.6
  391.5 118.6 reduce-scatter.4
  516.7 134.9 reduce-scatter.8
  659.1 134.3 reduce-scatter.10
where the time goes:
time: 803 us; the launch traced here: 800 us
  waiting for transfers between devices  462 us (58%)
  matrix products  190 us (24%)
  blocking collectives  83.9 us (10%)
  local copies, waits for them, and re-layouts  31.5 us (4%)
  other arithmetic  17.5 us (2%)
  between operations  14.5 us (2%)
    reduce_scatter x1, waiting for transfers between devices, on_device(): lax.psum_scatter(grad_w_down, ('wide', 'narrow'), scatter_dimension=0, ti...  142 us
    reduce_scatter x1, waiting for transfers between devices, on_device(): lax.psum_scatter(grad_w_up, ('wide', 'narrow'), scatter_dimension=0, tile...  141 us
    unnamed x2, blocking collectives  83.9 us
    all_gather x1, waiting for transfers between devices, on_device(): lax.all_gather(up_weight, ('wide', 'narrow'), axis=0, tiled=True)  62.9 us
    all_gather x1, waiting for transfers between devices, on_device(): lax.all_gather(down_weight, ('wide', 'narrow'), axis=0, tiled=True)  57.1 us
    reduce_scatter x1, waiting for transfers between devices, on_device(): lax.psum_scatter(grad_w_merged, ('wide', 'narrow'), scatter_dimension=0,...  36.8 us
    dot_general x12, matrix products, attend_backward(): lax.dot_general(grad_scores, queries, (((0,), (0,)), ((), ())), preferred...  21.7 us
    dot_general x12, matrix products, attend_backward(): jnp.dot(grad_scores, key_rows, preferred_element_type=jnp.float32)  21.5 us
  transfers between devices with their start and end apart: 8, of which 7 were waited for; matrix products, arithmetic and copies ran while one was open for 27% of the time, Pallas kernels for 0%

commit v1 on v0

--- a/solution.py
+++ b/solution.py
@@ -1,14 +1,20 @@
+import functools
 import math
 
 import jax
 import jax.numpy as jnp
 from jax import lax
+from jax.experimental import pallas as pl
+from jax.experimental.pallas import tpu as pltpu
 from jax.sharding import PartitionSpec as P
 
 H = 12
-
-
 MASKED_SCORE = -1000000000.0
+MESH = pl.DeviceIdType.MESH
+F32 = jnp.float32
+BF16 = jnp.bfloat16
+ALL = slice(None)
+CHUNK = 64
 
 
 def layer_norm(inputs, ln_gain, ln_bias):
@@ -95,7 +101,7 @@
     return (jnp.concatenate(grad_queries, 0), grad_keys, grad_values)
 
 
-def on_device(
+def by_collectives(
     tokens,
     cotangent,
     clip_lengths,
@@ -278,42 +284,755 @@
     )
 
 
+def nt_dot(left, right):
+    return lax.dot_general(left, right, (((1,), (1,)), ((), ())), preferred_element_type=F32)
+
+
+def nn_dot(left, right):
+    return jnp.dot(left, right, preferred_element_type=F32)
+
+
+def rows_of(step, size=CHUNK):
+    return pl.ds(pl.multiple_of(step * size, size), size)
+
+
+def norm_parts(values):
+    centred = values - jnp.mean(values, axis=-1, keepdims=True)
+    scale = lax.rsqrt(jnp.mean(centred * centred, axis=-1, keepdims=True) + 1e-06)
+    return centred * scale, scale
+
+
+def fold_rows(values):
+    return jnp.sum(values.reshape(-1, 8, values.shape[-1]), axis=0)
+
+
+def gelu_both(u):
+    tail = 0.5 * (1.0 + lax.erf(u * 0.7071067811865476))
+    return u * tail, tail + u * jnp.exp(-0.5 * u * u) * 0.3989422804014327
+
+
+def spread_maps(width, columns):
+    column = lax.broadcasted_iota(jnp.int32, (1, columns), 1).astype(F32)
+    group = jnp.floor((column + 0.5) * (1.0 / width))
+    place = column - group * width
+    lane = lax.broadcasted_iota(jnp.int32, (128, columns), 0).astype(F32)
+    picks = jnp.where(lane == place, 1.0, 0.0).astype(BF16)
+    owners = columns // width
+    owner = lax.broadcasted_iota(jnp.int32, (owners, 8, columns), 0).astype(F32)
+    mine = owner == group.reshape(1, 1, columns)
+    return picks, mine
+
+
+def spread(pieces, width, columns):
+    picks, mine = spread_maps(width, columns)
+    wide_rows = nn_dot(pieces.reshape(-1, 128).astype(BF16), picks)
+    return jnp.sum(jnp.where(mine, wide_rows.reshape(-1, 8, columns), 0.0), axis=0)
+
+
+def gather_back(vectors, width):
+    columns = vectors.shape[-1]
+    picks, mine = spread_maps(width, columns)
+    rest = jnp.where(mine, vectors[None], 0.0).reshape(-1, columns)
+    total = None
+    for _ in range(3):
+        part = rest.astype(BF16)
+        rest = rest - part.astype(F32)
+        term = nt_dot(part, picks)
+        total = term if total is None else total + term
+    return total.reshape(-1, 8, 128)
+
+
+def layer_kernel(
+    clip_ref, tok_ref, cot_ref, small_ref, wqkv_ref, wout_ref, wup_ref, wdown_ref,
+    out_ref, tgrad_ref, gqkv_ref, gout_ref, gup_ref, gdown_ref, gsmall_ref,
+    slabs, downs, smalls, gsmalls, weights, w_up,
+    row_c, row_2, row_3, row_z, down_c, down_2, down_3, down_z, sm_c, sm_2, sm_3, sm_z,
+    qkv, n1t, n1, att_t, middle, n2, n2t, g2, acc_out, acc_grad, act, grad_h, pre, grad_act,
+    tok, cot, bias, lse, dq_t, vec24, vec48, vec96, sums, up_sums, block_out,
+    ag_send, ag_recv, rs_send, rs_recv, local,
+):
+    n_z, width = slabs.shape[1], slabs.shape[-1]
+    count = tok.shape[0]
+    pairs = width // 128
+    chunks = count // CHUNK
+    wide_at, y = lax.axis_index("wide"), lax.axis_index("narrow")
+    core = lax.rem(wide_at, 2)
+    x = lax.rem(lax.div(wide_at, 2), 2)
+    z = lax.div(wide_at, 4)
+    own = {"z": z, "x": x, "c": core, "y": y}
+
+    def device(z_at, x_at, c_at, y_at):
+        return ((z_at * 2 + x_at) * 2 + c_at, y_at)
+
+    def others(axis):
+        if axis == "z":
+            return [(step, device(lax.rem(z + step, n_z), x, core, y)) for step in range(1, n_z)]
+        if axis == "x":
+            return [(n_z, device(z, 1 - x, core, y))]
+        if axis == "y":
+            return [(n_z + 1, device(z, x, core, 1 - y))]
+        return [(n_z + 2, device(z, x, 1 - core, y))]
+
+    def index(held, **fixed):
+        return tuple(fixed.get(a, ALL if a in held else own[a]) for a in "zxcy")
+
+    def row_view(block, columns=ALL):
+        def view(at):
+            if isinstance(columns, slice):
+                return slabs.at[(block, *at)]
+            return slabs.at[(block, *at, ALL, columns)]
+        return view
+
+    def down_view(tile):
+        def view(at):
+            return downs.at[(tile, *at[1:])]
+        return view
+
+    def small_view(ref):
+        def view(at):
+            return ref.at[at]
+        return view
+
+    def ag_copies(unit, phase):
+        view, order, row = unit
+        axis = order[phase]
+        at = index(order[:phase])
+        return [
+            pltpu.make_async_remote_copy(
+                src_ref=view(at), dst_ref=view(at), send_sem=ag_send.at[row, sem], recv_sem=ag_recv.at[row, sem],
+                device_id=to, device_id_type=MESH,
+            )
+            for sem, to in others(axis)
+        ]
+
+    def ag_start(unit, phase):
+        for copy in ag_copies(unit, phase):
+            copy.start()
+
+    def ag_arrived(unit, phase):
+        for copy in ag_copies(unit, phase):
+            copy.wait_recv()
+
+    def ag_sent(unit):
+        for phase in range(len(unit[1])):
+            for copy in ag_copies(unit, phase):
+                copy.wait_send()
+
+    half = width // 2
+    left, right = pl.ds(0, half), pl.ds(half, half)
+    small_unit = (small_view(smalls), "zxyc", 0)
+    gather_groups = [[small_unit, (row_view(0, left), "zxyc", 1), (row_view(0, right), "zyxc", 2)]]
+    for block in (1, 2, 3):
+        gather_groups.append(
+            [(row_view(block, left), "zxyc", 2 * block + 1), (row_view(block, right), "zyxc", 2 * block + 2)]
+        )
+    for tile in range(n_z):
+        gather_groups.append(
+            [(row_view(4 + tile), "zxyc", 9 + tile), (down_view(tile), "yxc", 9 + n_z + tile)]
+        )
+    down_first = (lambda at: downs.at[(at[0], *at[1:])], "z", 9 + 2 * n_z)
+
+    def ag_stage(unit, stage):
+        order = unit[1]
+        phase = stage - (4 - len(order))
+        if phase > 0:
+            ag_arrived(unit, phase - 1)
+        if 0 <= phase < len(order):
+            ag_start(unit, phase)
+        if stage == 4:
+            ag_sent(unit)
+
+    def ag_slot(slot):
+        for stage in (4, 3, 2, 1, 0):
+            group = slot - stage
+            if 0 <= group < len(gather_groups):
+                if group == 4 and stage == 1:
+                    ag_arrived(down_first, 0)
+                    ag_sent(down_first)
+                for unit in gather_groups[group]:
+                    ag_stage(unit, stage)
+                if group == 2 and stage == 0:
+                    ag_start(down_first, 0)
+
+    def rs_index(order, phase, partner):
+        done = order[:phase]
+        at = []
+        for a in "zxcy":
+            if a in done:
+                at.append(own[a])
+            elif a == order[phase]:
+                at.append(1 - own[a] if partner else own[a])
+            else:
+                at.append(ALL)
+        return tuple(at)
+
+    def rs_copies(unit, phase):
+        view, order, row, landing = unit
+        axis = order[phase]
+        if axis == "z":
+            copies = []
+            for sem, to in others("z"):
+                at = (lax.rem(z + sem, n_z), x, core, y)
+                copies.append((view(at), landing[phase].at[sem - 1], sem, to))
+        else:
+            sem, to = others(axis)[0]
+            copies = [(view(rs_index(order, phase, True)), landing[phase], sem, to)]
+        return [
+            pltpu.make_async_remote_copy(
+                src_ref=src, dst_ref=dst, send_sem=rs_send.at[row, sem], recv_sem=rs_recv.at[row, sem],
+                device_id=to, device_id_type=MESH,
+            )
+            for src, dst, sem, to in copies
+        ]
+
+    def rs_start(unit, phase):
+        for copy in rs_copies(unit, phase):
+            copy.start()
+
+    def rs_arrived(unit, phase):
+        for copy in rs_copies(unit, phase):
+            copy.wait_recv()
+
+    def rs_sent(unit):
+        for phase in range(len(unit[1])):
+            for copy in rs_copies(unit, phase):
+                copy.wait_send()
+
+    def add_into(target, source):
+        total = target[...].astype(F32) + source[...].astype(F32)
+        target[...] = total.astype(target.dtype)
+
+    def rs_add(unit, phase):
+        view, order, _, landing = unit
+        at = rs_index(order, phase, False)
+        target, source = view(at), landing[phase]
+        free = len(target.shape) - 2
+        if free == 0:
+            add_into(target, source)
+            return
+        inner = target.shape[1:free]
+
+        def step(i, carry):
+            places = [()]
+            for extent in inner:
+                places = [place + (k,) for place in places for k in range(extent)]
+            for place in places:
+                add_into(target.at[(i, *place)], source.at[(i, *place)])
+            return carry
+
+        lax.fori_loop(0, target.shape[0], step, 0)
+
+    def rs_final(unit, phase, result):
+        view, _, _, landing = unit
+        total = view((z, x, core, y))[...].astype(F32)
+        for sem in range(n_z - 1):
+            total = total + landing[phase].at[sem][...].astype(F32)
+        result[...] = total
+
+    def row_unit(block, order, row):
+        return (row_view(block), order, row, (row_c.at[block], row_2.at[block], row_3.at[block], row_z.at[block]))
+
+    def down_unit(tile, order, row):
+        return (down_view(tile), order, row, (down_c.at[tile], down_2.at[tile], down_3.at[tile]))
+
+    def block_columns(block):
+        return pl.ds(block * width, width)
+
+    up_units = [row_unit(4 + t, "cyxz", t) for t in range(n_z)]
+    down_units = [down_unit(t, "cxy", n_z + t) for t in range(n_z)]
+    out_unit = row_unit(3, "cyxz", 2 * n_z)
+    v_unit = row_unit(2, "cxyz", 2 * n_z + 1)
+    k_unit = row_unit(1, "cyxz", 2 * n_z + 2)
+    q_unit = row_unit(0, "cxyz", 2 * n_z + 3)
+    small_grad_unit = (small_view(gsmalls), "cyxz", 2 * n_z + 4, (sm_c, sm_2, sm_3, sm_z))
+    down_last = (lambda at: downs.at[at], "z", 2 * n_z + 5, (down_z,))
+
+    def rs_stage(unit, stage):
+        order = unit[1]
+        if 0 < stage <= len(order) and order[stage - 1] != "z":
+            rs_arrived(unit, stage - 1)
+            rs_add(unit, stage - 1)
+        if stage < len(order):
+            rs_start(unit, stage)
+
+    def rs_end(unit, result):
+        phase = len(unit[1]) - 1
+        rs_arrived(unit, phase)
+        rs_final(unit, phase, result)
+
+    def local_copies():
+        pairs_of = [(tok_ref, tok), (cot_ref, cot), (small_ref, smalls.at[z, x, core, y])]
+        for block in range(3):
+            pairs_of.append((wqkv_ref.at[:, block_columns(block)], slabs.at[block, z, x, core, y]))
+        pairs_of.append((wout_ref, slabs.at[3, z, x, core, y]))
+        for tile in range(n_z):
+            pairs_of.append((wup_ref.at[:, block_columns(tile)], slabs.at[4 + tile, z, x, core, y]))
+        pairs_of.append((wdown_ref, downs.at[z, x, core, y]))
+        return [pltpu.make_async_copy(src, dst, local.at[k]) for k, (src, dst) in enumerate(pairs_of)]
+
+    starts = local_copies()
+    for copy in starts:
+        copy.start()
+    barrier = pltpu.get_barrier_semaphore()
+    partners = [to for axis in "zxyc" for _, to in others(axis)]
+    for to in partners:
+        pl.semaphore_signal(barrier, inc=1, device_id=to, device_id_type=MESH)
+    for copy in starts:
+        copy.wait()
+    pl.semaphore_wait(barrier, len(partners))
+    ag_slot(0)
+
+    ends = []
+    for k in range(clip_ref.shape[1]):
+        ends.append(clip_ref[0, k] + (ends[-1] if ends else 0))
+
+    def segment_of(position):
+        total = jnp.zeros(position.shape, jnp.int32)
+        for end in ends:
+            total = total + jnp.where(position >= end, 1, 0)
+        return total
+
+    across = segment_of(lax.broadcasted_iota(jnp.int32, (CHUNK, count), 1))
+
+    def live_of(step):
+        position = lax.broadcasted_iota(jnp.int32, (CHUNK, 1), 0) + step * CHUNK
+        return jnp.where(position < ends[-1], 1.0, 0.0)
+
+    def mask_step(i, total):
+        down = segment_of(lax.broadcasted_iota(jnp.int32, (CHUNK, count), 0) + i * CHUNK)
+        bias[rows_of(i), :] = jnp.where(down == across, 0.0, -1e30)
+        grad = (live_of(i) * cot[rows_of(i), :].astype(F32)).astype(BF16)
+        g2[rows_of(i), :] = grad
+        return total + fold_rows(grad.astype(F32))
+
+    down_bias_sum = lax.fori_loop(0, chunks, mask_step, jnp.zeros((8, width), F32))
+    sums[...] = jnp.zeros_like(sums)
+    sums[0, 7:8, :] = jnp.sum(down_bias_sum, axis=0, keepdims=True)
+
+    ag_slot(1)
+    ag_slot(2)
+    ag_slot(3)
+    ag_slot(4)
+
+    vec24[...] = spread(smalls[...], 24, width)
+    for k in range(2):
+        vec48[k] = spread(smalls[k * n_z // 2 : (k + 1) * n_z // 2], 48, width)
+    for k in range(n_z):
+        vec96[k] = spread(smalls[k], 96, width)
+
+    def norm_one(i, carry):
+        normed, _ = norm_parts(tok[rows_of(i), :].astype(F32))
+        n1[rows_of(i), :] = (normed * vec24[0:1, :] + vec24[1:2, :]).astype(BF16)
+        return carry
+
+    lax.fori_loop(0, chunks, norm_one, 0)
+
+    def turn(source, target):
+        def step(i, carry):
+            at = rows_of(i, 128)
+            target[at, :] = source[:, at].T
+            return carry
+
+        lax.fori_loop(0, pairs, step, 0)
+
+    turn(n1, n1t)
+
+    def assemble(block, target):
+        def step(z_at, carry):
+            for x_at in range(2):
+                for c_at in range(2):
+                    two = slabs[block, z_at, x_at, c_at].astype(F32)
+                    size = 2 * two.shape[1]
+                    first = pl.multiple_of(((z_at * 2 + x_at) * 2 + c_at) * size, 16)
+                    target[pl.ds(first, size), :] = two.reshape(size, width).astype(BF16)
+            return carry
+
+        lax.fori_loop(0, n_z, step, 0)
+
+    def project(block, add):
+        assemble(block, weights.at[block])
+        total = nn_dot(n1[...], weights[block])
+        qkv[block] = (total if add is None else total + add).astype(BF16)
+
+    project(0, vec48[0, 2:3, :])
+    ag_slot(5)
+    project(1, None)
+    ag_slot(6)
+    project(2, vec48[1, 2:3, :])
+
+    lane = lax.broadcasted_iota(jnp.int32, (count, 128), 1)
+
+    def one_head(values, head):
+        keep = lane < 64 if head == 0 else lane >= 64
+        return jnp.where(keep, values, jnp.zeros_like(values))
+
+    q_block = 256
+    parts = count // q_block
+
+    def attend(p, carry):
+        for when, slot in ((0, 7), (2, 8), (4, 9)):
+            @pl.when(p == when)
+            def _():
+                ag_slot(slot)
+        at = rows_of(p, 128)
+        keys = qkv[1, :, at]
+        queries = qkv[0, :, at] * 0.125
+        values_t = qkv[2, :, at].T
+        for head in range(2):
+            mine = one_head(queries, head)
+            for part in range(parts):
+                span = slice(part * q_block, (part + 1) * q_block)
+                scores = nt_dot(keys, mine[span]) + bias[:, span]
+                highest = jnp.max(scores, axis=0, keepdims=True)
+                raised = jnp.exp(scores - highest)
+                total = jnp.sum(raised, axis=0, keepdims=True)
+                chances = (raised * (1.0 / total)).astype(BF16)
+                lse[p, head : head + 1, span] = highest + jnp.log(total)
+                result = nn_dot(values_t[64 * head : 64 * head + 64], chances)
+                att_t[pl.ds(pl.multiple_of(p * 128 + 64 * head, 64), 64), span] = result.astype(BF16)
+        return carry
+
+    lax.fori_loop(0, pairs, attend, 0)
+    att = n1
+    def turn_back(p, carry):
+        at = rows_of(p, 128)
+        att[:, at] = att_t[at, :].T
+        return carry
+    lax.fori_loop(0, pairs, turn_back, 0)
+
+    assemble(3, weights.at[3])
+    pre[...] = nn_dot(att[...], weights[3])
+
+    def norm_two(i, carry):
+        at = rows_of(i)
+        branch = pre[at, :] + vec24[3:4, :]
+        mid = tok[at, :].astype(F32) + live_of(i) * branch
+        middle[at, :] = mid
+        normed, _ = norm_parts(mid)
+        n2[at, :] = (normed * vec24[4:5, :] + vec24[5:6, :]).astype(BF16)
+        return carry
+
+    lax.fori_loop(0, chunks, norm_two, 0)
+    turn(n2, n2t)
+    acc_out[...] = jnp.zeros_like(acc_out)
+    acc_grad[...] = jnp.zeros_like(acc_grad)
+
+    def store_rows(block, lhs_t, rhs):
+        deep = width // n_z
+        size = slabs.shape[-2]
+
+        def step(z_at, carry):
+            total = nn_dot(lhs_t[rows_of(z_at, deep), :], rhs)
+            for x_at in range(2):
+                for c_at in range(2):
+                    for y_at in range(2):
+                        first = ((x_at * 2 + c_at) * 2 + y_at) * size
+                        slabs[block, z_at, x_at, c_at, y_at] = total[first : first + size].astype(BF16)
+            return carry
+
+        lax.fori_loop(0, n_z, step, 0)
+
+    def feed(t, carry):
+        for when in range(n_z):
+            @pl.when(t == when)
+            def _():
+                if when + 10 < len(gather_groups) + 4:
+                    ag_slot(when + 10)
+                if when >= 1:
+                    rs_stage(up_units[when - 1], 1)
+                    rs_stage(down_units[when - 1], 1)
+                if when >= 2:
+                    rs_stage(up_units[when - 2], 2)
+                    rs_stage(down_units[when - 2], 2)
+                if when >= 3:
+                    rs_stage(up_units[when - 3], 3)
+                    rs_stage(down_units[when - 3], 3)
+        assemble(4 + t, w_up)
+        pre[...] = nn_dot(n2[...], w_up[...])
+        w_down = downs[t].reshape(width, width)
+        grad_act[...] = nt_dot(g2[...], w_down)
+        up_bias = vec96[t, 6:7, :]
+
+        def gelu_step(i, total):
+            at = rows_of(i, 32)
+            active, slope = gelu_both(pre[at, :] + up_bias)
+            act[at, :] = active.astype(BF16)
+            grad = (grad_act[at, :] * slope).astype(BF16)
+            grad_h[at, :] = grad
+            return total + fold_rows(grad.astype(F32))
+
+        total = lax.fori_loop(0, count // 32, gelu_step, jnp.zeros((8, width), F32))
+        up_sums[t, 6:7, :] = jnp.sum(total, axis=0, keepdims=True)
+        acc_out[...] += nn_dot(act[...], w_down)
+        acc_grad[...] += nt_dot(grad_h[...], w_up[...])
+        store_rows(4 + t, n2t, grad_h[...])
+        for j in range(pairs):
+            span = slice(j * 128, (j + 1) * 128)
+            piece = nn_dot(act[:, span].T, g2[...]).astype(BF16)
+            size = downs.shape[-2]
+            at = j * 128
+            while at < (j + 1) * 128:
+                owner, inside = at // size, at % size
+                length = min(size - inside, (j + 1) * 128 - at)
+                downs[t, owner // 4, owner // 2 % 2, owner % 2, inside : inside + length, :] = piece[at - j * 128 : at - j * 128 + length]
+                at += length
+        for when in range(n_z):
+            @pl.when(t == when)
+            def _():
+                rs_stage(up_units[when], 0)
+                rs_stage(down_units[when], 0)
+        return carry
+
+    up_sums[...] = jnp.zeros_like(up_sums)
+    lax.fori_loop(0, n_z, feed, 0)
+
+    def norm_two_back(i, carry):
+        gain_sum, bias_sum, one_sum = carry
+        at = rows_of(i)
+        alive = live_of(i)
+        mid = middle[at, :]
+        block_out[at, :] = (mid + alive * (acc_out[at, :] + vec24[7:8, :])).astype(BF16)
+        normed, scale = norm_parts(mid)
+        e = acc_grad[at, :]
+        scaled = e * vec24[4:5, :]
+        inner = scaled - jnp.mean(scaled, axis=-1, keepdims=True) - normed * jnp.mean(scaled * normed, axis=-1, keepdims=True)
+        grad_mid = cot[at, :].astype(F32) + inner * scale
+        acc_grad[at, :] = grad_mid
+        one = (alive * grad_mid).astype(BF16)
+        g2[at, :] = one
+        return (gain_sum + fold_rows(e * normed), bias_sum + fold_rows(e), one_sum + fold_rows(one.astype(F32)))
+
+    zero = jnp.zeros((8, width), F32)
+    gain_sum, bias_sum, one_sum = lax.fori_loop(0, chunks, norm_two_back, (zero, zero, zero))
+    sums[0, 4:5, :] = jnp.sum(gain_sum, axis=0, keepdims=True)
+    sums[0, 5:6, :] = jnp.sum(bias_sum, axis=0, keepdims=True)
+    sums[0, 3:4, :] = jnp.sum(one_sum, axis=0, keepdims=True)
+    out_copy = pltpu.make_async_copy(block_out, out_ref, local.at[0])
+    out_copy.start()
+
+    def rs_points(points):
+        for unit, stage in points:
+            rs_stage(unit, stage)
+
+    rs_points([(up_units[3], 1), (down_units[3], 1), (up_units[2], 2), (down_units[2], 2), (up_units[1], 3), (down_units[1], 3)])
+    store_rows(3, att_t, g2[...])
+    rs_stage(out_unit, 0)
+    grad_att = n2
+    grad_att[...] = nt_dot(g2[...], weights[3]).astype(BF16)
+
+    back_points = {
+        0: [(up_units[3], 2), (down_units[3], 2), (up_units[2], 3), (down_units[2], 3), (out_unit, 1)],
+        2: [(up_units[3], 3), (down_units[3], 3), (down_last, 0), (out_unit, 2)],
+        4: [(out_unit, 3)],
+    }
+
+    def attend_back(p, carry):
+        for when in sorted(back_points):
+            @pl.when(p == when)
+            def _():
+                rs_points(back_points[when])
+        at = rows_of(p, 128)
+        keys = qkv[1, :, at]
+        values = qkv[2, :, at]
+        queries = qkv[0, :, at] * 0.125
+        grads = grad_att[:, at]
+        keys_t = keys.T
+        grad_keys = jnp.zeros((count, 128), F32)
+        grad_values = jnp.zeros((count, 128), F32)
+        for head in range(2):
+            my_queries, my_grads = one_head(queries, head), one_head(grads, head)
+            for part in range(parts):
+                span = slice(part * q_block, (part + 1) * q_block)
+                scores = nt_dot(keys, my_queries[span]) + bias[:, span]
+                chances = jnp.exp(scores - lse[p, head : head + 1, span])
+                slopes = nt_dot(values, my_grads[span])
+                level = jnp.sum(chances * slopes, axis=0, keepdims=True)
+                grad_scores = (chances * (slopes - level)).astype(BF16)
+                grad_values += nn_dot(chances.astype(BF16), my_grads[span])
+                grad_keys += nn_dot(grad_scores, my_queries[span])
+                dq_t[64 * head : 64 * head + 64, span] = nn_dot(keys_t[64 * head : 64 * head + 64], grad_scores) * 0.125
+        qkv[0, :, at] = dq_t[...].T.astype(BF16)
+        qkv[1, :, at] = grad_keys.astype(BF16)
+        qkv[2, :, at] = grad_values.astype(BF16)
+        return carry
+
+    lax.fori_loop(0, pairs, attend_back, 0)
+
+    store_rows(2, n1t, qkv[2])
+    rs_stage(v_unit, 0)
+    store_rows(1, n1t, qkv[1])
+    rs_points([(k_unit, 0), (v_unit, 1)])
+    store_rows(0, n1t, qkv[0])
+    rs_points([(q_unit, 0), (k_unit, 1), (v_unit, 2)])
+    pre[...] = nt_dot(qkv[2], weights[2])
+    rs_points([(q_unit, 1), (k_unit, 2), (v_unit, 3)])
+    pre[...] += nt_dot(qkv[1], weights[1])
+    rs_points([(q_unit, 2), (k_unit, 3)])
+    pre[...] += nt_dot(qkv[0], weights[0])
+
+    def norm_one_back(i, carry):
+        gain_sum, bias_sum, q_sum, v_sum = carry
+        at = rows_of(i)
+        normed, scale = norm_parts(tok[at, :].astype(F32))
+        e = pre[at, :]
+        scaled = e * vec24[0:1, :]
+        inner = scaled - jnp.mean(scaled, axis=-1, keepdims=True) - normed * jnp.mean(scaled * normed, axis=-1, keepdims=True)
+        acc_grad[at, :] = acc_grad[at, :] + inner * scale
+        return (
+            gain_sum + fold_rows(e * normed), bias_sum + fold_rows(e),
+            q_sum + fold_rows(qkv[0, at, :].astype(F32)), v_sum + fold_rows(qkv[2, at, :].astype(F32)),
+        )
+
+    gain_sum, bias_sum, q_sum, v_sum = lax.fori_loop(0, chunks, norm_one_back, (zero, zero, zero, zero))
+    tgrad_copy = pltpu.make_async_copy(acc_grad, tgrad_ref, local.at[1])
+    tgrad_copy.start()
+    sums[0, 0:1, :] = jnp.sum(gain_sum, axis=0, keepdims=True)
+    sums[0, 1:2, :] = jnp.sum(bias_sum, axis=0, keepdims=True)
+    sums[1, 2:3, :] = jnp.sum(q_sum, axis=0, keepdims=True)
+    sums[2, 2:3, :] = jnp.sum(v_sum, axis=0, keepdims=True)
+    gsmalls[...] = gather_back(sums[0], 24).reshape(gsmalls.shape)
+    for k in range(2):
+        part = gather_back(sums[1 + k], 48)
+        span = slice(k * n_z // 2, (k + 1) * n_z // 2)
+        gsmalls[span] = gsmalls[span] + part.reshape(n_z // 2, 2, 2, 2, 8, 128)
+    for k in range(n_z):
+        gsmalls[k] = gsmalls[k] + gather_back(up_sums[k], 96).reshape(2, 2, 2, 8, 128)
+    rs_points([(small_grad_unit, 0), (q_unit, 3)])
+
+    for t in range(n_z):
+        rs_end(up_units[t], gup_ref.at[:, block_columns(t)])
+    rs_end(down_last, gdown_ref)
+    rs_points([(small_grad_unit, 1)])
+    rs_end(out_unit, gout_ref)
+    rs_points([(small_grad_unit, 2)])
+    rs_end(v_unit, gqkv_ref.at[:, block_columns(2)])
+    rs_points([(small_grad_unit, 3)])
+    rs_end(k_unit, gqkv_ref.at[:, block_columns(1)])
+    rs_end(q_unit, gqkv_ref.at[:, block_columns(0)])
+    rs_end(small_grad_unit, gsmall_ref)
+    for unit in [*up_units, *down_units, out_unit, v_unit, k_unit, q_unit, small_grad_unit, down_last]:
+        rs_sent(unit)
+    out_copy.wait()
+    tgrad_copy.wait()
+
+
+def by_kernel(
+    n_z, tokens, cotangent, clip_lengths, ln1_gain, ln1_bias, qkv_weight, qv_bias, out_weight, out_bias,
+    ln2_gain, ln2_bias, up_weight, up_bias, down_weight, down_bias,
+):
+    count, width = tokens.shape
+    size, deep = qkv_weight.shape[0], down_weight.shape[0]
+    blocks = 4 + n_z
+    vectors = (ln1_gain, ln1_bias, qv_bias, out_bias, ln2_gain, ln2_bias, up_bias, down_bias)
+    packed = jnp.stack([jnp.pad(v.astype(F32), (0, 128 - v.shape[0])) for v in vectors])
+    vmem, dma = pltpu.VMEM, pltpu.SemaphoreType.DMA
+    held = [
+        vmem((blocks, n_z, 2, 2, 2, size, width), BF16),
+        vmem((n_z, 2, 2, 2, deep, width), BF16),
+        vmem((n_z, 2, 2, 2, 8, 128), F32),
+        vmem((n_z, 2, 2, 2, 8, 128), F32),
+        vmem((4, width, width), BF16),
+        vmem((width, width), BF16),
+        vmem((blocks, n_z, 2, 2, size, width), BF16),
+        vmem((blocks, n_z, 2, size, width), BF16),
+        vmem((blocks, n_z, size, width), BF16),
+        vmem((blocks, n_z - 1, size, width), BF16),
+        vmem((n_z, 2, 2, deep, width), BF16),
+        vmem((n_z, 2, deep, width), BF16),
+        vmem((n_z, deep, width), BF16),
+        vmem((n_z - 1, deep, width), BF16),
+        vmem((n_z, 2, 2, 8, 128), F32),
+        vmem((n_z, 2, 8, 128), F32),
+        vmem((n_z, 8, 128), F32),
+        vmem((n_z - 1, 8, 128), F32),
+        vmem((3, count, width), BF16),
+        vmem((width, count), BF16),
+        vmem((count, width), BF16),
+        vmem((width, count), BF16),
+        vmem((count, width), F32),
+        vmem((count, width), BF16),
+        vmem((width, count), BF16),
+        vmem((count, width), BF16),
+        vmem((count, width), F32),
+        vmem((count, width), F32),
+        vmem((count, width), BF16),
+        vmem((count, width), BF16),
+        vmem((count, width), F32),
+        vmem((count, width), F32),
+        vmem((count, width), BF16),
+        vmem((count, width), BF16),
+        vmem((count, count), F32),
+        vmem((width // 128, 2, count), F32),
+        vmem((128, count), F32),
+        vmem((8, width), F32),
+        vmem((2, 8, width), F32),
+        vmem((n_z, 8, width), F32),
+        vmem((3, 8, width), F32),
+        vmem((n_z, 8, width), F32),
+        vmem((count, width), BF16),
+        dma((10 + 2 * n_z, n_z + 3)),
+        dma((10 + 2 * n_z, n_z + 3)),
+        dma((6 + 2 * n_z, n_z + 3)),
+        dma((6 + 2 * n_z, n_z + 3)),
+        dma((8 + n_z,)),
+    ]
+    anywhere, whole = pl.BlockSpec(memory_space=pl.ANY), pl.BlockSpec(memory_space=pltpu.VMEM)
+    shape = jax.ShapeDtypeStruct
+    out, grad, g_qkv, g_out, g_up, g_down, g_small = pl.pallas_call(
+        layer_kernel,
+        out_shape=(
+            shape((count, width), BF16),
+            shape((count, width), F32),
+            shape(qkv_weight.shape, F32),
+            shape(out_weight.shape, F32),
+            shape(up_weight.shape, F32),
+            shape(down_weight.shape, F32),
+            shape((8, 128), F32),
+        ),
+        in_specs=[pl.BlockSpec(memory_space=pltpu.SMEM)] + [anywhere] * 7,
+        out_specs=(anywhere, anywhere, whole, whole, whole, whole, whole),
+        scratch_shapes=held,
+        compiler_params=pltpu.CompilerParams(collective_id=0, has_side_effects=True, vmem_limit_bytes=VMEM_BYTES),
+    )(clip_lengths, tokens, cotangent, packed, qkv_weight, out_weight, up_weight, down_weight)
+    parts = [g_small[k, : v.shape[0]] for k, v in enumerate(vectors)]
+    return (out, grad, parts[0], parts[1], g_qkv, parts[2], g_out, parts[3], parts[4], parts[5], g_up, parts[6], g_down, parts[7])
+
+
+VMEM_BYTES = 63 * 1024 * 1024
+
+
+def kernel_fits(n_wide, n_narrow, tokens, qkv_weight, up_weight, down_weight):
+    width, hidden = qkv_weight.shape[0], up_weight.shape[1]
+    n_z = n_wide // 4
+    devices = n_wide * n_narrow
+    return (
+        n_narrow == 2
+        and n_wide == 4 * n_z
+        and n_z % 2 == 0
+        and hidden == n_z * width
+        and width % (8 * devices) == 0
+        and hidden % (16 * devices) == 0
+        and 2 * width // devices <= 128
+        and hidden // devices <= 128
+        and width // devices == 24
+        and (tokens.shape[0] // devices) % 256 == 0
+    )
+
+
 def solution(mesh):
-    return jax.shard_map(
-        on_device,
-        mesh=mesh,
-        in_specs=(
-            P(("wide", "narrow"), None),
-            P(("wide", "narrow"), None),
-            P(("wide", "narrow"), None),
-            P(("wide", "narrow")),
-            P(("wide", "narrow")),
-            P(("wide", "narrow"), None),
-            P(("wide", "narrow")),
-            P(("wide", "narrow"), None),
-            P(("wide", "narrow")),
-            P(("wide", "narrow")),
-            P(("wide", "narrow")),
-            P(("wide", "narrow"), None),
-            P(("wide", "narrow")),
-            P(("wide", "narrow"), None),
-            P(("wide", "narrow")),
-        ),
-        out_specs=(
-            P(("wide", "narrow"), None),
-            P(("wide", "narrow"), None),
-            P(("wide", "narrow")),
-            P(("wide", "narrow")),
-            P(("wide", "narrow"), None),
-            P(("wide", "narrow")),
-            P(("wide", "narrow"), None),
-            P(("wide", "narrow")),
-            P(("wide", "narrow")),
-            P(("wide", "narrow")),
-            P(("wide", "narrow"), None),
-            P(("wide", "narrow")),
-            P(("wide", "narrow"), None),
-            P(("wide", "narrow")),
-        ),
-        check_vma=False,
-    )
+    n_wide, n_narrow = mesh.shape["wide"], mesh.shape["narrow"]
+    both = ("wide", "narrow")
+    matrix, vector = P(both, None), P(both)
+    in_specs = (
+        matrix, matrix, matrix, vector, vector, matrix, vector, matrix, vector, vector, vector, matrix, vector, matrix, vector,
+    )
+    out_specs = (
+        matrix, matrix, vector, vector, matrix, vector, matrix, vector, vector, vector, matrix, vector, matrix, vector,
+    )
+
+    def run(*arrays):
+        fits = kernel_fits(n_wide, n_narrow, arrays[0], arrays[5], arrays[11], arrays[13])
+        body = functools.partial(by_kernel, n_wide // 4) if fits else by_collectives
+        return jax.shard_map(body, mesh=mesh, in_specs=in_specs, out_specs=out_specs, check_vma=False)(*arrays)
+
+    return run

time: 803 us -> 214 us (0.27)
  waiting for transfers between devices: 462 us -> 0 us
  Pallas kernels: 0 us -> 200 us
  matrix products: 190 us -> 0 us
  blocking collectives: 83.9 us -> 0 us
  local copies, waits for them, and re-layouts: 31.5 us -> 12.7 us
  other arithmetic: 17.5 us -> 0.6 us
  between operations: 14.5 us -> 0.68 us
    reduce_scatter x4 -> x0, waiting for transfers between devices: 320 us -> none  [the longest x1 142 us: on_device(): lax.psum_scatter(grad_w_down, ('wide', 'narrow'), scatter_dimension=0, ti...]
    pallas_call x0 -> x1, Pallas kernels: none -> 200 us  [by_kernel(): pl.pallas_call(layer_kernel, out_shape=(shape((count, width), BF16), shap...]
    dot_general x96 -> x0, matrix products: 190 us -> none  [the longest x12 21.7 us: attend_backward(): lax.dot_general(grad_scores, queries, (((0,), (0,)), ((), ())), preferred...]
    all_gather x4 -> x0, waiting for transfers between devices: 139 us -> none  [the longest x1 62.9 us: on_device(): lax.all_gather(up_weight, ('wide', 'narrow'), axis=0, tiled=True)]
    unnamed x2 -> x0, blocking collectives: 83.9 us -> none
    reduce_sum x20 -> x0, other arithmetic: 9.98 us -> none  [the longest x12 2.37 us: attend_forward(): denominator = jnp.sum(raised, axis=1, keepdims=True)]
  transfers between devices with their start and end apart: 8 -> 0, of which waited for: 7 -> 0; matrix products, arithmetic and copies ran while one was open for 27% -> 0% of each run, Pallas kernels for 0% -> 0%
where the time goes in v1:
time: 214 us
  Pallas kernels  200 us (93%)
  local copies, waits for them, and re-layouts  12.7 us (6%)
    pallas_call x1, Pallas kernels, by_kernel(): pl.pallas_call(layer_kernel, out_shape=(shape((count, width), BF16), shap...  200 us
    unnamed x16, local copies, waits for them, and re-layouts  5.97 us

profile of v1, /device:TPU:0, one launch (start us, length us, event | category | flops | bytes accessed | tf_op | source)
XLA Modules:
  0.0 213.8 jit_solution(813027284607624161)
XLA Ops:
  0.6 0.7 pad_bitcast_fusion.6
  1.3 0.7 pad_bitcast_fusion.4
  2.0 0.7 pad_bitcast_fusion.2
  2.7 0.7 pad_bitcast_fusion
  3.4 0.6 stack.46.small_ref
  4.0 199.9 %shard_map.254 = (bf16[512,768]{1,0:T(8,128)(2,1)}, f32[512,768]{1,0:T(8,128)}, f32[24,2304]{1,0:T(8,128)}, f32[24,768]{1,0:T(8,128)}, f32[24,3072]{1,0:T(8,128)}, /*index=5*/f32[96,768]{1,0:T(8,128)}, f32[8,128]{1,0:T(8,128)}) custom-call(s32[1,3]{1,0:T(1,128)} %clip_ref.1, bf16[512,768]{1,0:T(8,128)(2,1)} %tok_ref.1, bf16[512,768]{1,0:T(8,128)(2,1)} %cot_ref.1, ...), custom_call_target="tpu_custom_call" | custom-call | tf_op jit(solution)/shard_map/pallas_call | solution.py:981
  203.8 0.0 copy-start
  203.9 1.3 slice_bitcast_fusion.5
  205.2 1.2 slice_bitcast_fusion.1
  206.4 1.4 slice_bitcast_fusion
  207.8 2.1 copy.35
  209.9 0.0 copy-done
  209.9 0.0 copy-start.3
  209.9 0.0 copy-start.4
  209.9 0.0 copy-start.2
  209.9 0.0 copy-start.1
  209.9 1.1 copy.36
  211.0 0.0 copy-done.3
  211.0 0.7 copy.37
  211.7 0.0 copy-done.4
  211.7 0.6 copy.38
  212.4 0.0 copy-done.2
  212.4 0.7 copy.39
  213.1 0.0 copy-done.1
  213.1 0.7 copy.40
  (1 shorter events, 0.0 us)
Async XLA Ops:
  203.8 6.0 %copy-start = (f32[512,768]{1,0:T(8,128)S(1)}, f32[512,768]{1,0:T(8,128)}, u32[]{:S(2)}) copy-start(f32[512,768]{1,0:T(8,128)} %get-tuple-element.57) | copy-start | bytes 4718596
  209.9 1.2 copy-start.3
  209.9 1.9 copy-start.4
  209.9 2.5 %copy-start.2 = (f32[24,3072]{1,0:T(8,128)S(1)}, f32[24,3072]{1,0:T(8,128)}, u32[]{:S(2)}) copy-start(f32[24,3072]{1,0:T(8,128)} %get-tuple-element.66) | copy-start | bytes 884740
  209.9 3.2 %copy-start.1 = (f32[96,768]{1,0:T(8,128)S(1)}, f32[96,768]{1,0:T(8,128)}, u32[]{:S(2)}) copy-start(f32[96,768]{1,0:T(8,128)} %get-tuple-element.68) | copy-start | bytes 884740

commit v2 on v1

--- a/solution.py
+++ b/solution.py
@@ -343,10 +343,10 @@
 
 
 def layer_kernel(
-    clip_ref, tok_ref, cot_ref, small_ref, wqkv_ref, wout_ref, wup_ref, wdown_ref,
+    clip_ref, tok_ref, cot_ref, v0, v1, v2, v3, v4, v5, v6, v7, wqkv_ref, wout_ref, wup_ref, wdown_ref,
     out_ref, tgrad_ref, gqkv_ref, gout_ref, gup_ref, gdown_ref, gsmall_ref,
     slabs, downs, smalls, gsmalls, weights, w_up,
-    row_c, row_2, row_3, row_z, down_c, down_2, down_3, down_z, sm_c, sm_2, sm_3, sm_z,
+    row_c, row_d, row_n, row_z, late_d, late_n, late_z, down_c, down_d, down_n, down_z, sm_c, sm_d, sm_n, sm_z,
     qkv, n1t, n1, att_t, middle, n2, n2t, g2, acc_out, acc_grad, act, grad_h, pre, grad_act,
     tok, cot, bias, lse, dq_t, vec24, vec48, vec96, sums, up_sums, block_out,
     ag_send, ag_recv, rs_send, rs_recv, local,
@@ -359,28 +359,13 @@
     core = lax.rem(wide_at, 2)
     x = lax.rem(lax.div(wide_at, 2), 2)
     z = lax.div(wide_at, 4)
-    own = {"z": z, "x": x, "c": core, "y": y}
 
     def device(z_at, x_at, c_at, y_at):
         return ((z_at * 2 + x_at) * 2 + c_at, y_at)
 
-    def others(axis):
-        if axis == "z":
-            return [(step, device(lax.rem(z + step, n_z), x, core, y)) for step in range(1, n_z)]
-        if axis == "x":
-            return [(n_z, device(z, 1 - x, core, y))]
-        if axis == "y":
-            return [(n_z + 1, device(z, x, core, 1 - y))]
-        return [(n_z + 2, device(z, x, 1 - core, y))]
-
-    def index(held, **fixed):
-        return tuple(fixed.get(a, ALL if a in held else own[a]) for a in "zxcy")
-
-    def row_view(block, columns=ALL):
+    def row_view(block):
         def view(at):
-            if isinstance(columns, slice):
-                return slabs.at[(block, *at)]
-            return slabs.at[(block, *at, ALL, columns)]
+            return slabs.at[(block, *at)]
         return view
 
     def down_view(tile):
@@ -393,175 +378,308 @@
             return ref.at[at]
         return view
 
+    def half_of(ref, side):
+        if ref.shape[-1] < 2 * 128:
+            return ref
+        cut = ref.shape[-1] // 2
+        return ref.at[(*([ALL] * (len(ref.shape) - 1)), pl.ds(side * cut, cut))]
+
+    to_x, to_y, to_c = device(z, 1 - x, core, y), device(z, x, core, 1 - y), device(z, x, 1 - core, y)
+    near_z, far_z, last_z = z + 1 - 2 * lax.rem(z, 2), lax.rem(z + 2, n_z), n_z - 1 - z
+    inner = lax.rem(z + 1, n_z) >= 2
+    to_near, to_far, to_last = device(near_z, x, core, y), device(far_z, x, core, y), device(last_z, x, core, y)
+    Z1, Z2, Z3, ZR, X0, Y0, DX, DY, C0 = range(9)
+
+    def remote(src, dst, sems, row, sem, to, recv_sem=None):
+        send, recv = sems
+        return pltpu.make_async_remote_copy(
+            src_ref=src, dst_ref=dst, send_sem=send.at[row, sem], recv_sem=recv.at[row, sem if recv_sem is None else recv_sem],
+            device_id=to, device_id_type=MESH,
+        )
+
+    def do_all(copies, what):
+        for copy in copies:
+            getattr(copy, what)()
+
     def ag_copies(unit, phase):
-        view, order, row = unit
-        axis = order[phase]
-        at = index(order[:phase])
-        return [
-            pltpu.make_async_remote_copy(
-                src_ref=view(at), dst_ref=view(at), send_sem=ag_send.at[row, sem], recv_sem=ag_recv.at[row, sem],
-                device_id=to, device_id_type=MESH,
-            )
-            for sem, to in others(axis)
-        ]
-
-    def ag_start(unit, phase):
-        for copy in ag_copies(unit, phase):
-            copy.start()
+        view, row, phases, along = unit
+        sems = (ag_send, ag_recv)
+        late = phases.index("z") > phases.index("near") if "z" in phases and "near" in phases else False
+        held = z if late else ALL
+        own = view((z, *along))
+        if phase == "z":
+            return [remote(own, own, sems, row, Z1, to_near), remote(own, own, sems, row, Z2, to_far)]
+        if phase == "z near":
+            return [remote(own, own, sems, row, Z1, to_near)]
+        if phase == "z far":
+            return [remote(own, own, sems, row, Z2, to_far)]
+        if phase == "z inner":
+            return [remote(own, own, sems, row, Z3, to_last)]
+        if phase == "relay":
+            passed = view((far_z, *along))
+            return [remote(passed, passed, sems, row, ZR, to_near, Z3)]
+        if phase == "near":
+            mine = view((held, x, core, y))
+            return [remote(mine, mine, sems, row, X0, to_x), remote(mine, mine, sems, row, Y0, to_y)]
+        if phase == "across":
+            from_x, from_y = view((held, 1 - x, core, y)), view((held, x, core, 1 - y))
+            first = half_of(from_x, 0)
+            copies = [remote(first, first, sems, row, DY, to_y)]
+            if from_x.shape[-1] >= 2 * 128:
+                second = half_of(from_y, 1)
+                copies.append(remote(second, second, sems, row, DX, to_x))
+            return copies
+        plane = view((ALL, ALL, core, ALL))
+        return [remote(plane, plane, sems, row, C0, to_c)]
 
     def ag_arrived(unit, phase):
-        for copy in ag_copies(unit, phase):
-            copy.wait_recv()
-
-    def ag_sent(unit):
-        for phase in range(len(unit[1])):
-            for copy in ag_copies(unit, phase):
-                copy.wait_send()
-
-    half = width // 2
-    left, right = pl.ds(0, half), pl.ds(half, half)
-    small_unit = (small_view(smalls), "zxyc", 0)
-    gather_groups = [[small_unit, (row_view(0, left), "zxyc", 1), (row_view(0, right), "zyxc", 2)]]
-    for block in (1, 2, 3):
-        gather_groups.append(
-            [(row_view(block, left), "zxyc", 2 * block + 1), (row_view(block, right), "zyxc", 2 * block + 2)]
-        )
+        if phase == "z":
+            @pl.when(jnp.logical_not(inner))
+            def _():
+                do_all(ag_copies(unit, "z far"), "wait_recv")
+            do_all(ag_copies(unit, "z near") + ag_copies(unit, "z inner"), "wait_recv")
+        else:
+            do_all(ag_copies(unit, phase), "wait_recv")
+
+    def ag_stage(unit, stage):
+        phases = unit[2]
+        waits = [p for p in phases[:stage] if p != "relay"][-1:]
+        phase = phases[stage] if stage < len(phases) else None
+        if phase == "relay":
+            @pl.when(inner)
+            def _():
+                do_all(ag_copies(unit, "z far"), "wait_recv")
+                do_all(ag_copies(unit, "relay"), "start")
+            return
+        if waits:
+            ag_arrived(unit, waits[0])
+        if phase:
+            do_all(ag_copies(unit, phase), "start")
+            if phase == "z":
+                @pl.when(inner)
+                def _():
+                    do_all(ag_copies(unit, "z inner"), "start")
+        else:
+            for sent in phases:
+                if sent != "relay":
+                    do_all(ag_copies(unit, sent), "wait_send")
+            if "z" in phases:
+                @pl.when(inner)
+                def _():
+                    do_all(ag_copies(unit, "z inner") + ag_copies(unit, "relay"), "wait_send")
+
+    first_z = ("z", "relay", "near", "across", "core")
+    last_z_order = ("near", "across", "z", "relay", "core")
+    one, plane_of = (x, core, y), (ALL, core, ALL)
+    small_unit = (small_view(smalls), 0, first_z, one)
+
+    def gather_unit(block, late=False):
+        return (row_view(block), 1 + block, last_z_order if late else first_z, plane_of if late else one)
+
+    down_first = (lambda at: downs.at[at], 5 + 2 * n_z, ("z", "relay"), one)
+
+    def gather_down(tile):
+        return (down_view(tile), 5 + n_z + tile, ("near", "across", "core"), one)
+
+    A_TICKS, F_TICKS, D_TICKS = (-4, -2, -1, 0, 1, 2), (-7, -6, -5, -3, 0, 1), (-1, 0, 1, 2)
+    gathers = [(0, small_unit, A_TICKS)] + [(b, gather_unit(b), A_TICKS) for b in range(4)]
     for tile in range(n_z):
-        gather_groups.append(
-            [(row_view(4 + tile), "zxyc", 9 + tile), (down_view(tile), "yxc", 9 + n_z + tile)]
-        )
-    down_first = (lambda at: downs.at[(at[0], *at[1:])], "z", 9 + 2 * n_z)
-
-    def ag_stage(unit, stage):
-        order = unit[1]
-        phase = stage - (4 - len(order))
-        if phase > 0:
-            ag_arrived(unit, phase - 1)
-        if 0 <= phase < len(order):
-            ag_start(unit, phase)
-        if stage == 4:
-            ag_sent(unit)
-
-    def ag_slot(slot):
-        for stage in (4, 3, 2, 1, 0):
-            group = slot - stage
-            if 0 <= group < len(gather_groups):
-                if group == 4 and stage == 1:
-                    ag_arrived(down_first, 0)
-                    ag_sent(down_first)
-                for unit in gather_groups[group]:
-                    ag_stage(unit, stage)
-                if group == 2 and stage == 0:
-                    ag_start(down_first, 0)
-
-    def rs_index(order, phase, partner):
-        done = order[:phase]
-        at = []
-        for a in "zxcy":
-            if a in done:
-                at.append(own[a])
-            elif a == order[phase]:
-                at.append(1 - own[a] if partner else own[a])
-            else:
-                at.append(ALL)
-        return tuple(at)
+        late = tile in LATE_GATHERS
+        gathers.append((4 + 2 * tile, gather_unit(4 + tile, late), F_TICKS if late else A_TICKS))
+        gathers.append((5 + 2 * tile, gather_down(tile), D_TICKS))
+    gathers.append((5, down_first, (-4, -2, -1)))
+    FIRST_TICK = min(place + ticks[0] for place, _, ticks in gathers)
+    rank = {"z": 0, "relay": 1, "near": 2, "core": 3, None: 4, "across": 5}
+
+    def ag_tick(tick):
+        todo = []
+        for place, unit, ticks in gathers:
+            for stage, at in enumerate(ticks):
+                if place + at == tick:
+                    phase = unit[2][stage] if stage < len(unit[2]) else None
+                    todo.append((rank[phase] - (10 if unit is down_first else 0), place, stage, unit))
+        for _, _, stage, unit in sorted(todo, key=lambda entry: entry[:3]):
+            ag_stage(unit, stage)
 
     def rs_copies(unit, phase):
-        view, order, row, landing = unit
-        axis = order[phase]
-        if axis == "z":
-            copies = []
-            for sem, to in others("z"):
-                at = (lax.rem(z + sem, n_z), x, core, y)
-                copies.append((view(at), landing[phase].at[sem - 1], sem, to))
-        else:
-            sem, to = others(axis)[0]
-            copies = [(view(rs_index(order, phase, True)), landing[phase], sem, to)]
-        return [
-            pltpu.make_async_remote_copy(
-                src_ref=src, dst_ref=dst, send_sem=rs_send.at[row, sem], recv_sem=rs_recv.at[row, sem],
-                device_id=to, device_id_type=MESH,
-            )
-            for src, dst, sem, to in copies
-        ]
-
-    def rs_start(unit, phase):
-        for copy in rs_copies(unit, phase):
-            copy.start()
-
-    def rs_arrived(unit, phase):
-        for copy in rs_copies(unit, phase):
-            copy.wait_recv()
-
-    def rs_sent(unit):
-        for phase in range(len(unit[1])):
-            for copy in rs_copies(unit, phase):
-                copy.wait_send()
-
-    def add_into(target, source):
-        total = target[...].astype(F32) + source[...].astype(F32)
+        view, row, phases, landing, along = unit
+        sems = (rs_send, rs_recv)
+        late = "near" in phases and "z" in phases and phases.index("z") < phases.index("near")
+        held = z if late else ALL
+        if phase == "core":
+            return [remote(view((ALL, ALL, 1 - core, ALL)), landing["core"], sems, row, C0, to_c)]
+        if phase == "across":
+            away = view((held, 1 - x, core, 1 - y))
+            copies = [remote(half_of(away, 0), landing["dx"], sems, row, DX, to_x)]
+            if away.shape[-1] >= 2 * 128:
+                copies.append(remote(half_of(away, 1), landing["dy"], sems, row, DY, to_y))
+            return copies
+        if phase == "near":
+            return [
+                remote(view((held, 1 - x, core, y)), landing["x"], sems, row, X0, to_x),
+                remote(view((held, x, core, 1 - y)), landing["y"], sems, row, Y0, to_y),
+            ]
+        if phase == "z":
+            return [remote(view((near_z, *along)), landing["z1"], sems, row, Z1, to_near)]
+        if phase == "z inner":
+            return [remote(view((last_z, *along)), landing["z3"], sems, row, Z3, to_last)]
+        if phase == "z outer":
+            return [remote(view((last_z, *along)), landing["zr"], sems, row, ZR, to_near)]
+        return [remote(view((far_z, *along)), landing["z2"], sems, row, Z2, to_far)]
+
+    def add_into(target, *sources):
+        total = target[...].astype(F32)
+        for source in sources:
+            total = total + source[...].astype(F32)
         target[...] = total.astype(target.dtype)
 
-    def rs_add(unit, phase):
-        view, order, _, landing = unit
-        at = rs_index(order, phase, False)
-        target, source = view(at), landing[phase]
+    def add_all(target, *sources):
         free = len(target.shape) - 2
         if free == 0:
-            add_into(target, source)
+            add_into(target, *sources)
             return
-        inner = target.shape[1:free]
+        places = [()]
+        for extent in target.shape[1:free]:
+            places = [place + (k,) for place in places for k in range(extent)]
 
         def step(i, carry):
-            places = [()]
-            for extent in inner:
-                places = [place + (k,) for place in places for k in range(extent)]
             for place in places:
-                add_into(target.at[(i, *place)], source.at[(i, *place)])
+                add_into(target.at[(i, *place)], *[source.at[(i, *place)] for source in sources])
             return carry
 
         lax.fori_loop(0, target.shape[0], step, 0)
 
-    def rs_final(unit, phase, result):
-        view, _, _, landing = unit
-        total = view((z, x, core, y))[...].astype(F32)
-        for sem in range(n_z - 1):
-            total = total + landing[phase].at[sem][...].astype(F32)
-        result[...] = total
-
-    def row_unit(block, order, row):
-        return (row_view(block), order, row, (row_c.at[block], row_2.at[block], row_3.at[block], row_z.at[block]))
-
-    def down_unit(tile, order, row):
-        return (down_view(tile), order, row, (down_c.at[tile], down_2.at[tile], down_3.at[tile]))
+    def rs_take(unit, phase):
+        view, _, phases, landing, along = unit
+        late = "near" in phases and "z" in phases and phases.index("z") < phases.index("near")
+        held = z if late else ALL
+        if phase == "z":
+            do_all(rs_copies(unit, "z") + rs_copies(unit, "z far"), "wait_recv")
+            add_all(view((z, *along)), landing["z1"], landing["z2"])
+
+            @pl.when(inner)
+            def _():
+                do_all(rs_copies(unit, "z inner"), "wait_recv")
+                add_all(view((z, *along)), landing["z3"])
+            return
+        do_all(rs_copies(unit, phase), "wait_recv")
+        if phase == "core":
+            add_all(view((ALL, ALL, core, ALL)), landing["core"])
+        elif phase == "across":
+            on_y = view((held, x, core, 1 - y))
+            add_all(half_of(on_y, 0), landing["dx"])
+            if on_y.shape[-1] >= 2 * 128:
+                add_all(half_of(view((held, 1 - x, core, y)), 1), landing["dy"])
+        else:
+            add_all(view((held, x, core, y)), landing["x"], landing["y"])
+
+    def rs_stage(unit, stage):
+        view, _, phases, landing, along = unit
+        if stage == len(phases):
+            rs_take(unit, phases[-1])
+            return
+        phase = phases[stage]
+        if phase == "z far":
+            @pl.when(inner)
+            def _():
+                do_all(rs_copies(unit, "z outer"), "wait_recv")
+                add_all(view((far_z, *along)), landing["zr"])
+            do_all(rs_copies(unit, phase), "start")
+            return
+        if stage > 0:
+            rs_take(unit, "z" if phases[stage - 1] == "z far" else phases[stage - 1])
+        do_all(rs_copies(unit, phase), "start")
+        if phase == "z":
+            @pl.when(inner)
+            def _():
+                do_all(rs_copies(unit, "z inner"), "start")
+
+            @pl.when(jnp.logical_not(inner))
+            def _():
+                do_all(rs_copies(unit, "z outer"), "start")
+
+    def rs_end(unit, *results):
+        view, _, phases, landing, along = unit
+        own = view((z, x, core, y))
+        if phases[-1] == "near":
+            do_all(rs_copies(unit, "near"), "wait_recv")
+            total = own[...].astype(F32) + landing["x"][...].astype(F32) + landing["y"][...].astype(F32)
+        else:
+            do_all(rs_copies(unit, "z") + rs_copies(unit, "z far"), "wait_recv")
+            total = own[...].astype(F32) + landing["z1"][...].astype(F32) + landing["z2"][...].astype(F32)
+        size = total.shape[-1] // len(results)
+        for k, result in enumerate(results):
+            result[...] = total[:, k * size : (k + 1) * size]
+        if phases[-1] != "near":
+            @pl.when(inner)
+            def _():
+                do_all(rs_copies(unit, "z inner"), "wait_recv")
+                for k, result in enumerate(results):
+                    result[...] += landing["z3"][:, k * size : (k + 1) * size].astype(F32)
+
+    def rs_sent(unit):
+        for phase in unit[2]:
+            do_all(rs_copies(unit, phase), "wait_send")
+        if "z" in unit[2]:
+            @pl.when(inner)
+            def _():
+                do_all(rs_copies(unit, "z inner"), "wait_send")
+
+            @pl.when(jnp.logical_not(inner))
+            def _():
+                do_all(rs_copies(unit, "z outer"), "wait_send")
+
+    back_last, back_first = ("core", "across", "near", "z", "z far"), ("core", "z", "z far", "across", "near")
+
+    def z_landing(ref):
+        return {"z1": ref.at[0], "z2": ref.at[1], "z3": ref.at[2], "zr": ref.at[3]}
+
+    def row_unit(block, row, late=None):
+        if late is not None:
+            landing = {"core": row_c.at[block], "dx": late_d.at[late, 0], "dy": late_d.at[late, 1], "x": late_n.at[late, 0], "y": late_n.at[late, 1], **z_landing(late_z.at[late])}
+            return (row_view(block), row, back_first, landing, plane_of)
+        landing = {"core": row_c.at[block], "dx": row_d.at[block, 0], "dy": row_d.at[block, 1], "x": row_n.at[block, 0], "y": row_n.at[block, 1], **z_landing(row_z.at[block])}
+        return (row_view(block), row, back_last, landing, one)
+
+    def down_unit(tile, row):
+        landing = {"core": down_c.at[tile], "dx": down_d.at[tile, 0], "dy": down_d.at[tile, 1], "x": down_n.at[tile, 0], "y": down_n.at[tile, 1]}
+        return (down_view(tile), row, back_last[:3], landing, one)
 
     def block_columns(block):
         return pl.ds(block * width, width)
 
-    up_units = [row_unit(4 + t, "cyxz", t) for t in range(n_z)]
-    down_units = [down_unit(t, "cxy", n_z + t) for t in range(n_z)]
-    out_unit = row_unit(3, "cyxz", 2 * n_z)
-    v_unit = row_unit(2, "cxyz", 2 * n_z + 1)
-    k_unit = row_unit(1, "cyxz", 2 * n_z + 2)
-    q_unit = row_unit(0, "cxyz", 2 * n_z + 3)
-    small_grad_unit = (small_view(gsmalls), "cyxz", 2 * n_z + 4, (sm_c, sm_2, sm_3, sm_z))
-    down_last = (lambda at: downs.at[at], "z", 2 * n_z + 5, (down_z,))
-
-    def rs_stage(unit, stage):
-        order = unit[1]
-        if 0 < stage <= len(order) and order[stage - 1] != "z":
-            rs_arrived(unit, stage - 1)
-            rs_add(unit, stage - 1)
-        if stage < len(order):
-            rs_start(unit, stage)
-
-    def rs_end(unit, result):
-        phase = len(unit[1]) - 1
-        rs_arrived(unit, phase)
-        rs_final(unit, phase, result)
+    up_units = [row_unit(4 + t, t, LATE_SUMS.index(t) if t in LATE_SUMS else None) for t in range(n_z)]
+    down_units = [down_unit(t, n_z + t) for t in range(n_z)]
+    head_units = [row_unit(g, 2 * n_z + g) for g in range(3)]
+    out_unit = row_unit(3, 2 * n_z + 3)
+    small_landing = {"core": sm_c, "dx": sm_d, "x": sm_n.at[0], "y": sm_n.at[1], **z_landing(sm_z)}
+    small_grad_unit = (small_view(gsmalls), 2 * n_z + 4, back_last, small_landing, one)
+    down_last = (lambda at: downs.at[at], 2 * n_z + 5, ("z", "z far"), z_landing(down_z), one)
+
+    POINTS = ["f0m", "f0e", "f1m", "f1e", "f2m", "f2e", "f3m", "f3e", "n2", "og", "a0", "a1", "h0", "a2", "a3", "h1", "a4", "a5", "h2", "g2", "g1", "g0", "nb", "gb", "e0", "e1", "e2", "e3"]
+    A_POINTS, F_POINTS = (0, 1, 2, 3, 4), (0, 1, 2, 5, 6)
+    plan = {name: [] for name in POINTS}
+
+    def plan_unit(unit, first, offsets):
+        for stage in range(len(unit[2]) + (unit[2][-1] == "near" and "z" not in unit[2])):
+            plan[POINTS[POINTS.index(first) + offsets[stage]]].append((unit, stage))
+
+    for t in range(n_z):
+        plan_unit(up_units[t], f"f{t}e", F_POINTS if t in LATE_SUMS else A_POINTS)
+        plan_unit(down_units[t], f"f{t}e", A_POINTS)
+    plan_unit(down_last, "a1", (0, 3))
+    plan_unit(out_unit, "og", (0, 2, 4, 6, 8))
+    plan_unit(head_units[0], "h0", (0, 2, 4, 5, 7))
+    plan_unit(head_units[1], "h1", (0, 2, 4, 5, 6))
+    plan_unit(head_units[2], "h2", (0, 1, 2, 3, 4))
+    plan_unit(small_grad_unit, "gb", (0, 1, 2, 3, 4))
+
+    def point(name):
+        for unit, stage in plan[name]:
+            rs_stage(unit, stage)
 
     def local_copies():
-        pairs_of = [(tok_ref, tok), (cot_ref, cot), (small_ref, smalls.at[z, x, core, y])]
+        pairs_of = [(tok_ref, tok), (cot_ref, cot)]
         for block in range(3):
             pairs_of.append((wqkv_ref.at[:, block_columns(block)], slabs.at[block, z, x, core, y]))
         pairs_of.append((wout_ref, slabs.at[3, z, x, core, y]))
@@ -573,14 +691,18 @@
     starts = local_copies()
     for copy in starts:
         copy.start()
+    smalls[z, x, core, y] = jnp.zeros((8, 128), F32)
+    for k, vector in enumerate((v0, v1, v2, v3, v4, v5, v6, v7)):
+        smalls[z, x, core, y, k, 0 : vector.shape[0]] = vector[...].astype(F32)
     barrier = pltpu.get_barrier_semaphore()
-    partners = [to for axis in "zxyc" for _, to in others(axis)]
+    partners = [to_near, to_far, to_last, to_x, to_y, to_c]
     for to in partners:
         pl.semaphore_signal(barrier, inc=1, device_id=to, device_id_type=MESH)
     for copy in starts:
         copy.wait()
     pl.semaphore_wait(barrier, len(partners))
-    ag_slot(0)
+    for tick in range(FIRST_TICK, 0):
+        ag_tick(tick)
 
     ends = []
     for k in range(clip_ref.shape[1]):
@@ -609,10 +731,8 @@
     sums[...] = jnp.zeros_like(sums)
     sums[0, 7:8, :] = jnp.sum(down_bias_sum, axis=0, keepdims=True)
 
-    ag_slot(1)
-    ag_slot(2)
-    ag_slot(3)
-    ag_slot(4)
+    for tick in range(3):
+        ag_tick(tick)
 
     vec24[...] = spread(smalls[...], 24, width)
     for k in range(2):
@@ -655,9 +775,9 @@
         qkv[block] = (total if add is None else total + add).astype(BF16)
 
     project(0, vec48[0, 2:3, :])
-    ag_slot(5)
+    ag_tick(3)
     project(1, None)
-    ag_slot(6)
+    ag_tick(4)
     project(2, vec48[1, 2:3, :])
 
     lane = lax.broadcasted_iota(jnp.int32, (count, 128), 1)
@@ -670,10 +790,10 @@
     parts = count // q_block
 
     def attend(p, carry):
-        for when, slot in ((0, 7), (2, 8), (4, 9)):
+        for when, tick in ((1, 5), (3, 6), (5, 7)):
             @pl.when(p == when)
             def _():
-                ag_slot(slot)
+                ag_tick(tick)
         at = rows_of(p, 128)
         keys = qkv[1, :, at]
         queries = qkv[0, :, at] * 0.125
@@ -714,6 +834,7 @@
 
     lax.fori_loop(0, chunks, norm_two, 0)
     turn(n2, n2t)
+    ag_tick(8)
     acc_out[...] = jnp.zeros_like(acc_out)
     acc_grad[...] = jnp.zeros_like(acc_grad)
 
@@ -733,20 +854,6 @@
         lax.fori_loop(0, n_z, step, 0)
 
     def feed(t, carry):
-        for when in range(n_z):
-            @pl.when(t == when)
-            def _():
-                if when + 10 < len(gather_groups) + 4:
-                    ag_slot(when + 10)
-                if when >= 1:
-                    rs_stage(up_units[when - 1], 1)
-                    rs_stage(down_units[when - 1], 1)
-                if when >= 2:
-                    rs_stage(up_units[when - 2], 2)
-                    rs_stage(down_units[when - 2], 2)
-                if when >= 3:
-                    rs_stage(up_units[when - 3], 3)
-                    rs_stage(down_units[when - 3], 3)
         assemble(4 + t, w_up)
         pre[...] = nn_dot(n2[...], w_up[...])
         w_down = downs[t].reshape(width, width)
@@ -763,6 +870,12 @@
 
         total = lax.fori_loop(0, count // 32, gelu_step, jnp.zeros((8, width), F32))
         up_sums[t, 6:7, :] = jnp.sum(total, axis=0, keepdims=True)
+        for when in range(n_z):
+            @pl.when(t == when)
+            def _():
+                if when < 3:
+                    ag_tick(9 + 2 * when)
+                point(f"f{when}m")
         acc_out[...] += nn_dot(act[...], w_down)
         acc_grad[...] += nt_dot(grad_h[...], w_up[...])
         store_rows(4 + t, n2t, grad_h[...])
@@ -779,8 +892,9 @@
         for when in range(n_z):
             @pl.when(t == when)
             def _():
-                rs_stage(up_units[when], 0)
-                rs_stage(down_units[when], 0)
+                if when < 2:
+                    ag_tick(10 + 2 * when)
+                point(f"f{when}e")
         return carry
 
     up_sums[...] = jnp.zeros_like(up_sums)
@@ -810,27 +924,34 @@
     out_copy = pltpu.make_async_copy(block_out, out_ref, local.at[0])
     out_copy.start()
 
-    def rs_points(points):
-        for unit, stage in points:
-            rs_stage(unit, stage)
-
-    rs_points([(up_units[3], 1), (down_units[3], 1), (up_units[2], 2), (down_units[2], 2), (up_units[1], 3), (down_units[1], 3)])
+    point("n2")
     store_rows(3, att_t, g2[...])
-    rs_stage(out_unit, 0)
+    point("og")
     grad_att = n2
     grad_att[...] = nt_dot(g2[...], weights[3]).astype(BF16)
 
-    back_points = {
-        0: [(up_units[3], 2), (down_units[3], 2), (up_units[2], 3), (down_units[2], 3), (out_unit, 1)],
-        2: [(up_units[3], 3), (down_units[3], 3), (down_last, 0), (out_unit, 2)],
-        4: [(out_unit, 3)],
-    }
+    def head_rows(group):
+        deep = width // n_z
+        size = slabs.shape[-2]
+        third = width // 3
+        columns = pl.ds(pl.multiple_of(group * third, third), third)
+
+        def step(z_at, carry):
+            for j in range(3):
+                total = nn_dot(n1t[rows_of(z_at, deep), :], qkv[j, :, columns])
+                for k in range(8):
+                    slabs[group, z_at, k // 4, k // 2 % 2, k % 2, :, j * third : (j + 1) * third] = total[k * size : (k + 1) * size].astype(BF16)
+            return carry
+
+        lax.fori_loop(0, n_z, step, 0)
+
+    per_group = pairs // 3
 
     def attend_back(p, carry):
-        for when in sorted(back_points):
+        for when in range(pairs):
             @pl.when(p == when)
             def _():
-                rs_points(back_points[when])
+                point(f"a{when}")
         at = rows_of(p, 128)
         keys = qkv[1, :, at]
         values = qkv[2, :, at]
@@ -854,21 +975,24 @@
         qkv[0, :, at] = dq_t[...].T.astype(BF16)
         qkv[1, :, at] = grad_keys.astype(BF16)
         qkv[2, :, at] = grad_values.astype(BF16)
+
+        @pl.when(lax.rem(p, per_group) == per_group - 1)
+        def _():
+            head_rows(lax.div(p, per_group))
+        for group in range(3):
+            @pl.when(p == group * per_group + per_group - 1)
+            def _():
+                point(f"h{group}")
         return carry
 
     lax.fori_loop(0, pairs, attend_back, 0)
 
-    store_rows(2, n1t, qkv[2])
-    rs_stage(v_unit, 0)
-    store_rows(1, n1t, qkv[1])
-    rs_points([(k_unit, 0), (v_unit, 1)])
-    store_rows(0, n1t, qkv[0])
-    rs_points([(q_unit, 0), (k_unit, 1), (v_unit, 2)])
     pre[...] = nt_dot(qkv[2], weights[2])
-    rs_points([(q_unit, 1), (k_unit, 2), (v_unit, 3)])
+    point("g2")
     pre[...] += nt_dot(qkv[1], weights[1])
-    rs_points([(q_unit, 2), (k_unit, 3)])
+    point("g1")
     pre[...] += nt_dot(qkv[0], weights[0])
+    point("g0")
 
     def norm_one_back(i, carry):
         gain_sum, bias_sum, q_sum, v_sum = carry
@@ -890,6 +1014,7 @@
     sums[0, 1:2, :] = jnp.sum(bias_sum, axis=0, keepdims=True)
     sums[1, 2:3, :] = jnp.sum(q_sum, axis=0, keepdims=True)
     sums[2, 2:3, :] = jnp.sum(v_sum, axis=0, keepdims=True)
+    point("nb")
     gsmalls[...] = gather_back(sums[0], 24).reshape(gsmalls.shape)
     for k in range(2):
         part = gather_back(sums[1 + k], 48)
@@ -897,20 +1022,24 @@
         gsmalls[span] = gsmalls[span] + part.reshape(n_z // 2, 2, 2, 2, 8, 128)
     for k in range(n_z):
         gsmalls[k] = gsmalls[k] + gather_back(up_sums[k], 96).reshape(2, 2, 2, 8, 128)
-    rs_points([(small_grad_unit, 0), (q_unit, 3)])
-
-    for t in range(n_z):
-        rs_end(up_units[t], gup_ref.at[:, block_columns(t)])
+    point("gb")
+
+    rs_end(up_units[0], gup_ref.at[:, block_columns(0)])
+    rs_end(up_units[1], gup_ref.at[:, block_columns(1)])
+    point("e0")
+    rs_end(up_units[2], gup_ref.at[:, block_columns(2)])
+    rs_end(up_units[3], gup_ref.at[:, block_columns(3)])
+    point("e1")
     rs_end(down_last, gdown_ref)
-    rs_points([(small_grad_unit, 1)])
     rs_end(out_unit, gout_ref)
-    rs_points([(small_grad_unit, 2)])
-    rs_end(v_unit, gqkv_ref.at[:, block_columns(2)])
-    rs_points([(small_grad_unit, 3)])
-    rs_end(k_unit, gqkv_ref.at[:, block_columns(1)])
-    rs_end(q_unit, gqkv_ref.at[:, block_columns(0)])
+    point("e2")
+    third = width // 3
+    for group in range(3):
+        rs_end(head_units[group], *[gqkv_ref.at[:, pl.ds(j * width + group * third, third)] for j in range(3)])
+        if group == 1:
+            point("e3")
     rs_end(small_grad_unit, gsmall_ref)
-    for unit in [*up_units, *down_units, out_unit, v_unit, k_unit, q_unit, small_grad_unit, down_last]:
+    for unit in [*up_units, *down_units, *head_units, out_unit, small_grad_unit, down_last]:
         rs_sent(unit)
     out_copy.wait()
     tgrad_copy.wait()
@@ -924,7 +1053,6 @@
     size, deep = qkv_weight.shape[0], down_weight.shape[0]
     blocks = 4 + n_z
     vectors = (ln1_gain, ln1_bias, qv_bias, out_bias, ln2_gain, ln2_bias, up_bias, down_bias)
-    packed = jnp.stack([jnp.pad(v.astype(F32), (0, 128 - v.shape[0])) for v in vectors])
     vmem, dma = pltpu.VMEM, pltpu.SemaphoreType.DMA
     held = [
         vmem((blocks, n_z, 2, 2, 2, size, width), BF16),
@@ -934,17 +1062,20 @@
         vmem((4, width, width), BF16),
         vmem((width, width), BF16),
         vmem((blocks, n_z, 2, 2, size, width), BF16),
-        vmem((blocks, n_z, 2, size, width), BF16),
+        vmem((blocks, 2, n_z, size, width // 2), BF16),
+        vmem((blocks, 2, n_z, size, width), BF16),
         vmem((blocks, n_z, size, width), BF16),
-        vmem((blocks, n_z - 1, size, width), BF16),
+        vmem((max(len(LATE_SUMS), 1), 2, size, width // 2), BF16),
+        vmem((max(len(LATE_SUMS), 1), 2, size, width), BF16),
+        vmem((max(len(LATE_SUMS), 1), n_z, 2, 2, size, width), BF16),
         vmem((n_z, 2, 2, deep, width), BF16),
+        vmem((n_z, 2, deep, width // 2), BF16),
         vmem((n_z, 2, deep, width), BF16),
         vmem((n_z, deep, width), BF16),
-        vmem((n_z - 1, deep, width), BF16),
         vmem((n_z, 2, 2, 8, 128), F32),
-        vmem((n_z, 2, 8, 128), F32),
         vmem((n_z, 8, 128), F32),
-        vmem((n_z - 1, 8, 128), F32),
+        vmem((2, n_z, 8, 128), F32),
+        vmem((n_z, 8, 128), F32),
         vmem((3, count, width), BF16),
         vmem((width, count), BF16),
         vmem((count, width), BF16),
@@ -970,10 +1101,10 @@
         vmem((3, 8, width), F32),
         vmem((n_z, 8, width), F32),
         vmem((count, width), BF16),
-        dma((10 + 2 * n_z, n_z + 3)),
-        dma((10 + 2 * n_z, n_z + 3)),
-        dma((6 + 2 * n_z, n_z + 3)),
-        dma((6 + 2 * n_z, n_z + 3)),
+        dma((6 + 2 * n_z, 9)),
+        dma((6 + 2 * n_z, 9)),
+        dma((6 + 2 * n_z, 9)),
+        dma((6 + 2 * n_z, 9)),
         dma((8 + n_z,)),
     ]
     anywhere, whole = pl.BlockSpec(memory_space=pl.ANY), pl.BlockSpec(memory_space=pltpu.VMEM)
@@ -989,15 +1120,41 @@
             shape(down_weight.shape, F32),
             shape((8, 128), F32),
         ),
-        in_specs=[pl.BlockSpec(memory_space=pltpu.SMEM)] + [anywhere] * 7,
+        in_specs=[pl.BlockSpec(memory_space=pltpu.SMEM)] + [anywhere] * 2 + [whole] * 8 + [anywhere] * 4,
         out_specs=(anywhere, anywhere, whole, whole, whole, whole, whole),
         scratch_shapes=held,
         compiler_params=pltpu.CompilerParams(collective_id=0, has_side_effects=True, vmem_limit_bytes=VMEM_BYTES),
-    )(clip_lengths, tokens, cotangent, packed, qkv_weight, out_weight, up_weight, down_weight)
-    parts = [g_small[k, : v.shape[0]] for k, v in enumerate(vectors)]
+    )(clip_lengths, tokens, cotangent, *vectors, qkv_weight, out_weight, up_weight, down_weight)
+    large = (out, grad, g_qkv, g_out, g_up, g_down)
+    done = pl.pallas_call(
+        hand_over,
+        out_shape=tuple(shape(a.shape, a.dtype) for a in large) + tuple(shape(v.shape, F32) for v in vectors),
+        in_specs=[whole] + [anywhere] * len(large),
+        out_specs=(anywhere,) * len(large) + (whole,) * len(vectors),
+        scratch_shapes=[vmem(a.shape, a.dtype) for a in large] + [dma((2, len(large)))],
+    )(g_small, *large)
+    out, grad, g_qkv, g_out, g_up, g_down = done[:6]
+    parts = done[6:]
     return (out, grad, parts[0], parts[1], g_qkv, parts[2], g_out, parts[3], parts[4], parts[5], g_up, parts[6], g_down, parts[7])
 
 
+def hand_over(small_ref, *refs):
+    sources, targets, vectors, held, sems = refs[:6], refs[6:12], refs[12:20], refs[20:26], refs[26]
+    inward = [pltpu.make_async_copy(src, dst, sems.at[0, k]) for k, (src, dst) in enumerate(zip(sources, held))]
+    outward = [pltpu.make_async_copy(src, dst, sems.at[1, k]) for k, (src, dst) in enumerate(zip(held, targets))]
+    for copy in inward:
+        copy.start()
+    for k, vector in enumerate(vectors):
+        vector[...] = small_ref[k, 0 : vector.shape[0]]
+    for arrived, onward in zip(inward, outward):
+        arrived.wait()
+        onward.start()
+    for copy in outward:
+        copy.wait()
+
+
+LATE_GATHERS = (1, 3)
+LATE_SUMS = (0, 2)
 VMEM_BYTES = 63 * 1024 * 1024
 
 
@@ -1008,7 +1165,7 @@
     return (
         n_narrow == 2
         and n_wide == 4 * n_z
-        and n_z % 2 == 0
+        and n_z == 4
         and hidden == n_z * width
         and width % (8 * devices) == 0
         and hidden % (16 * devices) == 0

time: 214 us -> 177 us (0.83)
  Pallas kernels: 200 us -> 176 us
  local copies, waits for them, and re-layouts: 12.7 us -> 0 us
    pallas_call x1, Pallas kernels: 200 us -> 171 us  [by_kernel(): pl.pallas_call(layer_kernel, out_shape=(shape((count, width), BF16), shap...]
    unnamed x16 -> x0, local copies, waits for them, and re-layouts: 5.97 us -> none
    pallas_call x0 -> x1, Pallas kernels: none -> 4.4 us  [by_kernel(): pl.pallas_call(hand_over, out_shape=tuple((shape(a.shape, a.dtype) for a...]
    squeeze x3 -> x0, local copies, waits for them, and re-layouts: 3.94 us -> none  [by_kernel(): parts = [g_small[k, :v.shape[0]] for k, v in enumerate(vectors)]]
    another operation x5 -> x0, local copies, waits for them, and re-layouts: 2.74 us -> none  [by_kernel(): jnp.stack([jnp.pad(v.astype(F32), (0, 128 - v.shape[0])) for v in vectors])]
where the time goes in v2:
time: 177 us; the launch traced here: 176 us
  Pallas kernels  176 us (99%)
    pallas_call x1, Pallas kernels, by_kernel(): pl.pallas_call(layer_kernel, out_shape=(shape((count, width), BF16), shap...  171 us
    pallas_call x1, Pallas kernels, by_kernel(): pl.pallas_call(hand_over, out_shape=tuple((shape(a.shape, a.dtype) for a...  4.4 us

profile of v2, /device:TPU:0, one launch (start us, length us, event | category | flops | bytes accessed | tf_op | source)
XLA Modules:
  0.0 176.4 jit_solution(14976328230792708034)
XLA Ops:
  0.7 171.1 %shard_map.254 = (bf16[512,768]{1,0:T(8,128)(2,1)}, f32[512,768]{1,0:T(8,128)}, f32[24,2304]{1,0:T(8,128)}, f32[24,768]{1,0:T(8,128)}, f32[24,3072]{1,0:T(8,128)}, /*index=5*/f32[96,768]{1,0:T(8,128)}, f32[8,128]{1,0:T(8,128)}) custom-call(s32[1,3]{1,0:T(1,128)} %clip_ref.1, bf16[512,768]{1,0:T(8,128)(2,1)} %tok_ref.1, bf16[512,768]{1,0:T(8,128)(2,1)} %cot_ref.1, ...), custom_call_target="tpu_custom_call" | custom-call | tf_op jit(solution)/shard_map/pallas_call | solution.py:1112
  171.8 4.4 %shard_map.255 = (bf16[512,768]{1,0:T(8,128)(2,1)}, f32[512,768]{1,0:T(8,128)}, f32[24,2304]{1,0:T(8,128)}, f32[24,768]{1,0:T(8,128)}, f32[24,3072]{1,0:T(8,128)...) custom-call(f32[8,128]{1,0:T(8,128)} %get-tuple-element.35.small_ref, ...), custom_call_target="tpu_custom_call" | custom-call | tf_op jit(solution)/shard_map/pallas_call | solution.py:1129

commit v3 on v2

--- a/solution.py
+++ b/solution.py
@@ -348,7 +348,7 @@
     slabs, downs, smalls, gsmalls, weights, w_up,
     row_c, row_d, row_n, row_z, late_d, late_n, late_z, down_c, down_d, down_n, down_z, sm_c, sm_d, sm_n, sm_z,
     qkv, n1t, n1, att_t, middle, n2, n2t, g2, acc_out, acc_grad, act, grad_h, pre, grad_act,
-    tok, cot, bias, lse, dq_t, vec24, vec48, vec96, sums, up_sums, block_out,
+    tok, cot, bias, lse, dq_t, vec24, vec48, vec96, merged_bias, group_sums, sums, up_sums, block_out,
     ag_send, ag_recv, rs_send, rs_recv, local,
 ):
     n_z, width = slabs.shape[1], slabs.shape[-1]
@@ -481,25 +481,12 @@
     def gather_down(tile):
         return (down_view(tile), 5 + n_z + tile, ("near", "across", "core"), one)
 
-    A_TICKS, F_TICKS, D_TICKS = (-4, -2, -1, 0, 1, 2), (-7, -6, -5, -3, 0, 1), (-1, 0, 1, 2)
-    gathers = [(0, small_unit, A_TICKS)] + [(b, gather_unit(b), A_TICKS) for b in range(4)]
+    units = {"aS": small_unit, "adp": down_first}
+    for block in range(4):
+        units[f"ab{block}"] = gather_unit(block)
     for tile in range(n_z):
-        late = tile in LATE_GATHERS
-        gathers.append((4 + 2 * tile, gather_unit(4 + tile, late), F_TICKS if late else A_TICKS))
-        gathers.append((5 + 2 * tile, gather_down(tile), D_TICKS))
-    gathers.append((5, down_first, (-4, -2, -1)))
-    FIRST_TICK = min(place + ticks[0] for place, _, ticks in gathers)
-    rank = {"z": 0, "relay": 1, "near": 2, "core": 3, None: 4, "across": 5}
-
-    def ag_tick(tick):
-        todo = []
-        for place, unit, ticks in gathers:
-            for stage, at in enumerate(ticks):
-                if place + at == tick:
-                    phase = unit[2][stage] if stage < len(unit[2]) else None
-                    todo.append((rank[phase] - (10 if unit is down_first else 0), place, stage, unit))
-        for _, _, stage, unit in sorted(todo, key=lambda entry: entry[:3]):
-            ag_stage(unit, stage)
+        units[f"au{tile}"] = gather_unit(4 + tile, tile in LATE_GATHERS)
+        units[f"ad{tile}"] = gather_down(tile)
 
     def rs_copies(unit, phase):
         view, row, phases, landing, along = unit
@@ -648,61 +635,57 @@
     def block_columns(block):
         return pl.ds(block * width, width)
 
-    up_units = [row_unit(4 + t, t, LATE_SUMS.index(t) if t in LATE_SUMS else None) for t in range(n_z)]
-    down_units = [down_unit(t, n_z + t) for t in range(n_z)]
-    head_units = [row_unit(g, 2 * n_z + g) for g in range(3)]
-    out_unit = row_unit(3, 2 * n_z + 3)
+    third = width // 3
+    results = {"rdl": [gdown_ref], "ro": [gout_ref], "rS": [gsmall_ref]}
+    for t in range(n_z):
+        units[f"ru{t}"] = row_unit(4 + t, t, LATE_SUMS.index(t) if t in LATE_SUMS else None)
+        units[f"rd{t}"] = down_unit(t, n_z + t)
+        results[f"ru{t}"] = [gup_ref.at[:, block_columns(t)]]
+    for g in range(3):
+        units[f"rh{g}"] = row_unit(g, 2 * n_z + g)
+        results[f"rh{g}"] = [gqkv_ref.at[:, pl.ds(j * width + g * third, third)] for j in range(3)]
+    units["ro"] = row_unit(3, 2 * n_z + 3)
     small_landing = {"core": sm_c, "dx": sm_d, "x": sm_n.at[0], "y": sm_n.at[1], **z_landing(sm_z)}
-    small_grad_unit = (small_view(gsmalls), 2 * n_z + 4, back_last, small_landing, one)
-    down_last = (lambda at: downs.at[at], 2 * n_z + 5, ("z", "z far"), z_landing(down_z), one)
-
-    POINTS = ["f0m", "f0e", "f1m", "f1e", "f2m", "f2e", "f3m", "f3e", "n2", "og", "a0", "a1", "h0", "a2", "a3", "h1", "a4", "a5", "h2", "g2", "g1", "g0", "nb", "gb", "e0", "e1", "e2", "e3"]
-    A_POINTS, F_POINTS = (0, 1, 2, 3, 4), (0, 1, 2, 5, 6)
-    plan = {name: [] for name in POINTS}
-
-    def plan_unit(unit, first, offsets):
-        for stage in range(len(unit[2]) + (unit[2][-1] == "near" and "z" not in unit[2])):
-            plan[POINTS[POINTS.index(first) + offsets[stage]]].append((unit, stage))
-
-    for t in range(n_z):
-        plan_unit(up_units[t], f"f{t}e", F_POINTS if t in LATE_SUMS else A_POINTS)
-        plan_unit(down_units[t], f"f{t}e", A_POINTS)
-    plan_unit(down_last, "a1", (0, 3))
-    plan_unit(out_unit, "og", (0, 2, 4, 6, 8))
-    plan_unit(head_units[0], "h0", (0, 2, 4, 5, 7))
-    plan_unit(head_units[1], "h1", (0, 2, 4, 5, 6))
-    plan_unit(head_units[2], "h2", (0, 1, 2, 3, 4))
-    plan_unit(small_grad_unit, "gb", (0, 1, 2, 3, 4))
+    units["rS"] = (small_view(gsmalls), 2 * n_z + 4, back_last, small_landing, one)
+    units["rdl"] = (lambda at: downs.at[at], 2 * n_z + 5, ("z", "z far"), z_landing(down_z), one)
 
     def point(name):
-        for unit, stage in plan[name]:
-            rs_stage(unit, stage)
-
-    def local_copies():
-        pairs_of = [(tok_ref, tok), (cot_ref, cot)]
-        for block in range(3):
-            pairs_of.append((wqkv_ref.at[:, block_columns(block)], slabs.at[block, z, x, core, y]))
-        pairs_of.append((wout_ref, slabs.at[3, z, x, core, y]))
-        for tile in range(n_z):
-            pairs_of.append((wup_ref.at[:, block_columns(tile)], slabs.at[4 + tile, z, x, core, y]))
-        pairs_of.append((wdown_ref, downs.at[z, x, core, y]))
-        return [pltpu.make_async_copy(src, dst, local.at[k]) for k, (src, dst) in enumerate(pairs_of)]
-
-    starts = local_copies()
-    for copy in starts:
-        copy.start()
-    smalls[z, x, core, y] = jnp.zeros((8, 128), F32)
-    for k, vector in enumerate((v0, v1, v2, v3, v4, v5, v6, v7)):
-        smalls[z, x, core, y, k, 0 : vector.shape[0]] = vector[...].astype(F32)
+        for unit_name, stage in TABLE.get(name, ()):
+            unit = units[unit_name]
+            if unit_name[0] == "a":
+                ag_stage(unit, stage)
+            elif unit_name in results and stage == len(unit[2]):
+                rs_end(unit, *results[unit_name])
+            else:
+                rs_stage(unit, stage)
+
+    def points_at(index, names):
+        for k, name in enumerate(names):
+            if TABLE.get(name):
+                pl.when(index == k)(functools.partial(point, name))
+
     barrier = pltpu.get_barrier_semaphore()
     partners = [to_near, to_far, to_last, to_x, to_y, to_c]
     for to in partners:
         pl.semaphore_signal(barrier, inc=1, device_id=to, device_id_type=MESH)
-    for copy in starts:
-        copy.wait()
+    shards = []
+    for g in range(3):
+        for j in range(3):
+            shards.append((wqkv_ref.at[:, pl.ds(j * width + g * third, third)], slabs.at[g, z, x, core, y, :, pl.ds(j * third, third)]))
+    shards.append((wout_ref, slabs.at[3, z, x, core, y]))
+    for tile in range(n_z):
+        shards.append((wup_ref.at[:, block_columns(tile)], slabs.at[4 + tile, z, x, core, y]))
+    shards.append((wdown_ref, downs.at[z, x, core, y]))
+    shard_copies = [pltpu.make_async_copy(src, dst, local.at[k]) for k, (src, dst) in enumerate(shards)]
+    row_copies = [pltpu.make_async_copy(tok_ref, tok, local.at[len(shards)]), pltpu.make_async_copy(cot_ref, cot, local.at[len(shards) + 1])]
+    do_all(shard_copies + row_copies, "start")
+    smalls[z, x, core, y] = jnp.zeros((8, 128), F32)
+    for k, vector in enumerate((v0, v1, v2, v3, v4, v5, v6, v7)):
+        smalls[z, x, core, y, k, 0 : vector.shape[0]] = vector[...].astype(F32)
+    do_all(shard_copies, "wait")
     pl.semaphore_wait(barrier, len(partners))
-    for tick in range(FIRST_TICK, 0):
-        ag_tick(tick)
+    point("mask")
+    do_all(row_copies, "wait")
 
     ends = []
     for k in range(clip_ref.shape[1]):
@@ -720,25 +703,33 @@
         position = lax.broadcasted_iota(jnp.int32, (CHUNK, 1), 0) + step * CHUNK
         return jnp.where(position < ends[-1], 1.0, 0.0)
 
-    def mask_step(i, total):
+    ones = jnp.ones((8, count), BF16)
+
+    def column_sums(values):
+        return nn_dot(ones, values)
+
+    def mask_step(i, carry):
         down = segment_of(lax.broadcasted_iota(jnp.int32, (CHUNK, count), 0) + i * CHUNK)
         bias[rows_of(i), :] = jnp.where(down == across, 0.0, -1e30)
-        grad = (live_of(i) * cot[rows_of(i), :].astype(F32)).astype(BF16)
-        g2[rows_of(i), :] = grad
-        return total + fold_rows(grad.astype(F32))
-
-    down_bias_sum = lax.fori_loop(0, chunks, mask_step, jnp.zeros((8, width), F32))
+        g2[rows_of(i), :] = (live_of(i) * cot[rows_of(i), :].astype(F32)).astype(BF16)
+        return carry
+
+    lax.fori_loop(0, chunks, mask_step, 0)
     sums[...] = jnp.zeros_like(sums)
-    sums[0, 7:8, :] = jnp.sum(down_bias_sum, axis=0, keepdims=True)
-
-    for tick in range(3):
-        ag_tick(tick)
-
+    up_sums[...] = jnp.zeros_like(up_sums)
+    sums[0, 7:8, :] = column_sums(g2[...])[0:1]
+
+    point("vec")
     vec24[...] = spread(smalls[...], 24, width)
     for k in range(2):
         vec48[k] = spread(smalls[k * n_z // 2 : (k + 1) * n_z // 2], 48, width)
     for k in range(n_z):
         vec96[k] = spread(smalls[k], 96, width)
+    for g in range(3):
+        span = slice(g * third, (g + 1) * third)
+        merged_bias[g, 0:1, :] = jnp.concatenate(
+            [vec48[0, 2:3, span], jnp.zeros((1, width - 2 * third), F32), vec48[1, 2:3, span]], axis=1
+        )
 
     def norm_one(i, carry):
         normed, _ = norm_parts(tok[rows_of(i), :].astype(F32))
@@ -755,6 +746,7 @@
 
         lax.fori_loop(0, pairs, step, 0)
 
+    point("turn")
     turn(n1, n1t)
 
     def assemble(block, target):
@@ -769,17 +761,6 @@
 
         lax.fori_loop(0, n_z, step, 0)
 
-    def project(block, add):
-        assemble(block, weights.at[block])
-        total = nn_dot(n1[...], weights[block])
-        qkv[block] = (total if add is None else total + add).astype(BF16)
-
-    project(0, vec48[0, 2:3, :])
-    ag_tick(3)
-    project(1, None)
-    ag_tick(4)
-    project(2, vec48[1, 2:3, :])
-
     lane = lax.broadcasted_iota(jnp.int32, (count, 128), 1)
 
     def one_head(values, head):
@@ -788,17 +769,28 @@
 
     q_block = 256
     parts = count // q_block
+    per_group = pairs // 3
+
+    def places(p):
+        first = lax.rem(p, per_group) * 128
+        return lax.div(p, per_group), [pl.ds(pl.multiple_of(first + j * third, 128), 128) for j in range(3)]
 
     def attend(p, carry):
-        for when, tick in ((1, 5), (3, 6), (5, 7)):
-            @pl.when(p == when)
-            def _():
-                ag_tick(tick)
-        at = rows_of(p, 128)
-        keys = qkv[1, :, at]
-        queries = qkv[0, :, at] * 0.125
-        values_t = qkv[2, :, at].T
+        group, (at_q, at_k, at_v) = places(p)
+        points_at(p, [f"q{k // per_group}" if k % per_group == 0 else "" for k in range(pairs)])
+
+        @pl.when(lax.rem(p, per_group) == 0)
+        def _():
+            assemble(group, weights.at[group])
+            qkv[group] = (nn_dot(n1[...], weights[group]) + merged_bias[group, 0:1, :]).astype(BF16)
+
+        points_at(p, [f"t{k}" for k in range(pairs)])
+        keys = qkv[group, :, at_k]
+        queries = qkv[group, :, at_q] * 0.125
+        values_t = qkv[group, :, at_v].T
         for head in range(2):
+            if head:
+                points_at(p, [f"T{k}" for k in range(pairs)])
             mine = one_head(queries, head)
             for part in range(parts):
                 span = slice(part * q_block, (part + 1) * q_block)
@@ -813,13 +805,16 @@
         return carry
 
     lax.fori_loop(0, pairs, attend, 0)
+    point("tb")
     att = n1
+
     def turn_back(p, carry):
         at = rows_of(p, 128)
         att[:, at] = att_t[at, :].T
         return carry
+
     lax.fori_loop(0, pairs, turn_back, 0)
-
+    point("out")
     assemble(3, weights.at[3])
     pre[...] = nn_dot(att[...], weights[3])
 
@@ -832,9 +827,12 @@
         n2[at, :] = (normed * vec24[4:5, :] + vec24[5:6, :]).astype(BF16)
         return carry
 
-    lax.fori_loop(0, chunks, norm_two, 0)
+    point("n2a")
+    lax.fori_loop(0, chunks // 2, norm_two, 0)
+    point("n2b")
+    lax.fori_loop(chunks // 2, chunks, norm_two, 0)
+    point("n2t")
     turn(n2, n2t)
-    ag_tick(8)
     acc_out[...] = jnp.zeros_like(acc_out)
     acc_grad[...] = jnp.zeros_like(acc_grad)
 
@@ -844,41 +842,44 @@
 
         def step(z_at, carry):
             total = nn_dot(lhs_t[rows_of(z_at, deep), :], rhs)
-            for x_at in range(2):
-                for c_at in range(2):
-                    for y_at in range(2):
-                        first = ((x_at * 2 + c_at) * 2 + y_at) * size
-                        slabs[block, z_at, x_at, c_at, y_at] = total[first : first + size].astype(BF16)
+            for k in range(8):
+                slabs[block, z_at, k // 4, k // 2 % 2, k % 2] = total[k * size : (k + 1) * size].astype(BF16)
             return carry
 
         lax.fori_loop(0, n_z, step, 0)
 
     def feed(t, carry):
+        def step_point(name):
+            points_at(t, [f"{name}{k}" for k in range(n_z)])
+
+        step_point("fa")
         assemble(4 + t, w_up)
+        step_point("fb")
         pre[...] = nn_dot(n2[...], w_up[...])
+        step_point("fc")
         w_down = downs[t].reshape(width, width)
         grad_act[...] = nt_dot(g2[...], w_down)
         up_bias = vec96[t, 6:7, :]
 
-        def gelu_step(i, total):
+        def gelu_step(i, carry):
             at = rows_of(i, 32)
             active, slope = gelu_both(pre[at, :] + up_bias)
             act[at, :] = active.astype(BF16)
-            grad = (grad_act[at, :] * slope).astype(BF16)
-            grad_h[at, :] = grad
-            return total + fold_rows(grad.astype(F32))
-
-        total = lax.fori_loop(0, count // 32, gelu_step, jnp.zeros((8, width), F32))
-        up_sums[t, 6:7, :] = jnp.sum(total, axis=0, keepdims=True)
-        for when in range(n_z):
-            @pl.when(t == when)
-            def _():
-                if when < 3:
-                    ag_tick(9 + 2 * when)
-                point(f"f{when}m")
+            grad_h[at, :] = (grad_act[at, :] * slope).astype(BF16)
+            return carry
+
+        step_point("fd")
+        lax.fori_loop(0, count // 64, gelu_step, 0)
+        step_point("fe")
+        lax.fori_loop(count // 64, count // 32, gelu_step, 0)
+        up_sums[t, 6:7, :] = column_sums(grad_h[...])[0:1]
+        step_point("ff")
         acc_out[...] += nn_dot(act[...], w_down)
+        step_point("fg")
         acc_grad[...] += nt_dot(grad_h[...], w_up[...])
+        step_point("fh")
         store_rows(4 + t, n2t, grad_h[...])
+        step_point("fi")
         for j in range(pairs):
             span = slice(j * 128, (j + 1) * 128)
             piece = nn_dot(act[:, span].T, g2[...]).astype(BF16)
@@ -889,19 +890,12 @@
                 length = min(size - inside, (j + 1) * 128 - at)
                 downs[t, owner // 4, owner // 2 % 2, owner % 2, inside : inside + length, :] = piece[at - j * 128 : at - j * 128 + length]
                 at += length
-        for when in range(n_z):
-            @pl.when(t == when)
-            def _():
-                if when < 2:
-                    ag_tick(10 + 2 * when)
-                point(f"f{when}e")
         return carry
 
-    up_sums[...] = jnp.zeros_like(up_sums)
     lax.fori_loop(0, n_z, feed, 0)
 
     def norm_two_back(i, carry):
-        gain_sum, bias_sum, one_sum = carry
+        gain_sum, bias_sum = carry
         at = rows_of(i)
         alive = live_of(i)
         mid = middle[at, :]
@@ -909,58 +903,42 @@
         normed, scale = norm_parts(mid)
         e = acc_grad[at, :]
         scaled = e * vec24[4:5, :]
-        inner = scaled - jnp.mean(scaled, axis=-1, keepdims=True) - normed * jnp.mean(scaled * normed, axis=-1, keepdims=True)
-        grad_mid = cot[at, :].astype(F32) + inner * scale
+        inner_part = scaled - jnp.mean(scaled, axis=-1, keepdims=True) - normed * jnp.mean(scaled * normed, axis=-1, keepdims=True)
+        grad_mid = cot[at, :].astype(F32) + inner_part * scale
         acc_grad[at, :] = grad_mid
-        one = (alive * grad_mid).astype(BF16)
-        g2[at, :] = one
-        return (gain_sum + fold_rows(e * normed), bias_sum + fold_rows(e), one_sum + fold_rows(one.astype(F32)))
+        g2[at, :] = (alive * grad_mid).astype(BF16)
+        return (gain_sum + fold_rows(e * normed), bias_sum + fold_rows(e))
 
     zero = jnp.zeros((8, width), F32)
-    gain_sum, bias_sum, one_sum = lax.fori_loop(0, chunks, norm_two_back, (zero, zero, zero))
+    point("ba")
+    carry = lax.fori_loop(0, chunks // 2, norm_two_back, (zero, zero))
+    point("bb")
+    gain_sum, bias_sum = lax.fori_loop(chunks // 2, chunks, norm_two_back, carry)
     sums[0, 4:5, :] = jnp.sum(gain_sum, axis=0, keepdims=True)
     sums[0, 5:6, :] = jnp.sum(bias_sum, axis=0, keepdims=True)
-    sums[0, 3:4, :] = jnp.sum(one_sum, axis=0, keepdims=True)
+    sums[0, 3:4, :] = column_sums(g2[...])[0:1]
     out_copy = pltpu.make_async_copy(block_out, out_ref, local.at[0])
     out_copy.start()
 
-    point("n2")
+    point("og")
     store_rows(3, att_t, g2[...])
-    point("og")
+    point("ga")
     grad_att = n2
     grad_att[...] = nt_dot(g2[...], weights[3]).astype(BF16)
 
-    def head_rows(group):
-        deep = width // n_z
-        size = slabs.shape[-2]
-        third = width // 3
-        columns = pl.ds(pl.multiple_of(group * third, third), third)
-
-        def step(z_at, carry):
-            for j in range(3):
-                total = nn_dot(n1t[rows_of(z_at, deep), :], qkv[j, :, columns])
-                for k in range(8):
-                    slabs[group, z_at, k // 4, k // 2 % 2, k % 2, :, j * third : (j + 1) * third] = total[k * size : (k + 1) * size].astype(BF16)
-            return carry
-
-        lax.fori_loop(0, n_z, step, 0)
-
-    per_group = pairs // 3
-
     def attend_back(p, carry):
-        for when in range(pairs):
-            @pl.when(p == when)
-            def _():
-                point(f"a{when}")
-        at = rows_of(p, 128)
-        keys = qkv[1, :, at]
-        values = qkv[2, :, at]
-        queries = qkv[0, :, at] * 0.125
-        grads = grad_att[:, at]
+        group, (at_q, at_k, at_v) = places(p)
+        points_at(p, [f"a{k}" for k in range(pairs)])
+        keys = qkv[group, :, at_k]
+        values = qkv[group, :, at_v]
+        queries = qkv[group, :, at_q] * 0.125
+        grads = grad_att[:, rows_of(p, 128)]
         keys_t = keys.T
         grad_keys = jnp.zeros((count, 128), F32)
         grad_values = jnp.zeros((count, 128), F32)
         for head in range(2):
+            if head:
+                points_at(p, [f"A{k}" for k in range(pairs)])
             my_queries, my_grads = one_head(queries, head), one_head(grads, head)
             for part in range(parts):
                 span = slice(part * q_block, (part + 1) * q_block)
@@ -972,49 +950,50 @@
                 grad_values += nn_dot(chances.astype(BF16), my_grads[span])
                 grad_keys += nn_dot(grad_scores, my_queries[span])
                 dq_t[64 * head : 64 * head + 64, span] = nn_dot(keys_t[64 * head : 64 * head + 64], grad_scores) * 0.125
-        qkv[0, :, at] = dq_t[...].T.astype(BF16)
-        qkv[1, :, at] = grad_keys.astype(BF16)
-        qkv[2, :, at] = grad_values.astype(BF16)
+        qkv[group, :, at_q] = dq_t[...].T.astype(BF16)
+        qkv[group, :, at_k] = grad_keys.astype(BF16)
+        qkv[group, :, at_v] = grad_values.astype(BF16)
+        points_at(p, [f"H{k // per_group}" if k % per_group == per_group - 1 else "" for k in range(pairs)])
 
         @pl.when(lax.rem(p, per_group) == per_group - 1)
         def _():
-            head_rows(lax.div(p, per_group))
-        for group in range(3):
-            @pl.when(p == group * per_group + per_group - 1)
-            def _():
-                point(f"h{group}")
+            store_rows(group, n1t, qkv[group])
+            group_sums[group] = column_sums(qkv[group])
+
         return carry
 
     lax.fori_loop(0, pairs, attend_back, 0)
 
+    point("g2")
     pre[...] = nt_dot(qkv[2], weights[2])
-    point("g2")
+    point("g1")
     pre[...] += nt_dot(qkv[1], weights[1])
-    point("g1")
+    point("g0")
     pre[...] += nt_dot(qkv[0], weights[0])
-    point("g0")
 
     def norm_one_back(i, carry):
-        gain_sum, bias_sum, q_sum, v_sum = carry
+        gain_sum, bias_sum = carry
         at = rows_of(i)
         normed, scale = norm_parts(tok[at, :].astype(F32))
         e = pre[at, :]
         scaled = e * vec24[0:1, :]
-        inner = scaled - jnp.mean(scaled, axis=-1, keepdims=True) - normed * jnp.mean(scaled * normed, axis=-1, keepdims=True)
-        acc_grad[at, :] = acc_grad[at, :] + inner * scale
-        return (
-            gain_sum + fold_rows(e * normed), bias_sum + fold_rows(e),
-            q_sum + fold_rows(qkv[0, at, :].astype(F32)), v_sum + fold_rows(qkv[2, at, :].astype(F32)),
-        )
-
-    gain_sum, bias_sum, q_sum, v_sum = lax.fori_loop(0, chunks, norm_one_back, (zero, zero, zero, zero))
+        inner_part = scaled - jnp.mean(scaled, axis=-1, keepdims=True) - normed * jnp.mean(scaled * normed, axis=-1, keepdims=True)
+        acc_grad[at, :] = acc_grad[at, :] + inner_part * scale
+        return (gain_sum + fold_rows(e * normed), bias_sum + fold_rows(e))
+
+    point("na")
+    carry = lax.fori_loop(0, chunks // 2, norm_one_back, (zero, zero))
+    point("nb")
+    gain_sum, bias_sum = lax.fori_loop(chunks // 2, chunks, norm_one_back, carry)
     tgrad_copy = pltpu.make_async_copy(acc_grad, tgrad_ref, local.at[1])
     tgrad_copy.start()
     sums[0, 0:1, :] = jnp.sum(gain_sum, axis=0, keepdims=True)
     sums[0, 1:2, :] = jnp.sum(bias_sum, axis=0, keepdims=True)
-    sums[1, 2:3, :] = jnp.sum(q_sum, axis=0, keepdims=True)
-    sums[2, 2:3, :] = jnp.sum(v_sum, axis=0, keepdims=True)
-    point("nb")
+    for g in range(3):
+        span = slice(g * third, (g + 1) * third)
+        sums[1, 2:3, span] = group_sums[g, 0:1, :third]
+        sums[2, 2:3, span] = group_sums[g, 0:1, 2 * third :]
+    point("gb")
     gsmalls[...] = gather_back(sums[0], 24).reshape(gsmalls.shape)
     for k in range(2):
         part = gather_back(sums[1 + k], 48)
@@ -1022,25 +1001,11 @@
         gsmalls[span] = gsmalls[span] + part.reshape(n_z // 2, 2, 2, 2, 8, 128)
     for k in range(n_z):
         gsmalls[k] = gsmalls[k] + gather_back(up_sums[k], 96).reshape(2, 2, 2, 8, 128)
-    point("gb")
-
-    rs_end(up_units[0], gup_ref.at[:, block_columns(0)])
-    rs_end(up_units[1], gup_ref.at[:, block_columns(1)])
-    point("e0")
-    rs_end(up_units[2], gup_ref.at[:, block_columns(2)])
-    rs_end(up_units[3], gup_ref.at[:, block_columns(3)])
-    point("e1")
-    rs_end(down_last, gdown_ref)
-    rs_end(out_unit, gout_ref)
-    point("e2")
-    third = width // 3
-    for group in range(3):
-        rs_end(head_units[group], *[gqkv_ref.at[:, pl.ds(j * width + group * third, third)] for j in range(3)])
-        if group == 1:
-            point("e3")
-    rs_end(small_grad_unit, gsmall_ref)
-    for unit in [*up_units, *down_units, *head_units, out_unit, small_grad_unit, down_last]:
-        rs_sent(unit)
+
+    point("end")
+    for name, unit in units.items():
+        if name[0] == "r":
+            rs_sent(unit)
     out_copy.wait()
     tgrad_copy.wait()
 
@@ -1099,13 +1064,15 @@
         vmem((2, 8, width), F32),
         vmem((n_z, 8, width), F32),
         vmem((3, 8, width), F32),
+        vmem((3, 8, width), F32),
+        vmem((3, 8, width), F32),
         vmem((n_z, 8, width), F32),
         vmem((count, width), BF16),
         dma((6 + 2 * n_z, 9)),
         dma((6 + 2 * n_z, 9)),
         dma((6 + 2 * n_z, 9)),
         dma((6 + 2 * n_z, 9)),
-        dma((8 + n_z,)),
+        dma((13 + n_z,)),
     ]
     anywhere, whole = pl.BlockSpec(memory_space=pl.ANY), pl.BlockSpec(memory_space=pltpu.VMEM)
     shape = jax.ShapeDtypeStruct
@@ -1153,8 +1120,73 @@
         copy.wait()
 
 
-LATE_GATHERS = (1, 3)
-LATE_SUMS = (0, 2)
+LATE_GATHERS = ()
+LATE_SUMS = ()
+TABLE = {
+    "mask": (("aS", 0), ("ab0", 0),),
+    "vec": (("ab1", 0), ("aS", 1), ("ab0", 1), ("ab2", 0), ("ab1", 1), ("aS", 2), ("ab3", 0), ("ab0", 2), ("ab2", 1), ("aS", 3), ("adp", 0), ("ab1", 2), ("ab3", 1), ("ab2", 2), ("aS", 4), ("aS", 5),),
+    "turn": (("ab0", 3),),
+    "q0": (("ab1", 3), ("adp", 1), ("ab2", 3), ("ab0", 4), ("au0", 0), ("ab3", 2), ("ab0", 5), ("ab1", 4),),
+    "t0": (("au1", 0),),
+    "T0": (("ab1", 5), ("ab2", 4), ("adp", 2), ("ad0", 0),),
+    "t1": (("au0", 1), ("ad1", 0), ("ab2", 5), ("au2", 0),),
+    "q1": (("au1", 1), ("au3", 0),),
+    "t2": (("ab3", 3),),
+    "T2": (("au0", 2), ("au2", 1),),
+    "T3": (("au3", 1),),
+    "q2": (("ad0", 1),),
+    "T4": (("ab3", 4), ("au1", 2),),
+    "T5": (("ab3", 5),),
+    "tb": (("au0", 3),),
+    "n2a": (("ad0", 2), ("ad1", 1),),
+    "n2b": (("au2", 2), ("ad0", 3),),
+    "fa0": (("au0", 4), ("au1", 3), ("au0", 5), ("ad1", 2), ("ad2", 0),),
+    "fd0": (("ad1", 3),),
+    "fe0": (("au2", 3),),
+    "ff0": (("au1", 4), ("au3", 2),),
+    "fh0": (("au1", 5),),
+    "fi0": (("ru0", 0),),
+    "fa1": (("ad2", 1), ("rd0", 0),),
+    "fd1": (("au2", 4), ("ad3", 0),),
+    "fe1": (("au2", 5),),
+    "ff1": (("au3", 3),),
+    "fi1": (("ad2", 2), ("ru0", 1), ("ru1", 0),),
+    "fa2": (("ad2", 3), ("rd0", 1), ("rd1", 0),),
+    "fb2": (("ad3", 1),),
+    "fd2": (("au3", 4), ("ru1", 1),),
+    "fe2": (("au3", 5), ("ru0", 2),),
+    "fh2": (("ad3", 2), ("rd0", 2),),
+    "fi2": (("ru2", 0),),
+    "fa3": (("ad3", 3), ("rd2", 0),),
+    "fd3": (("ru1", 2),),
+    "fe3": (("ru0", 3),),
+    "ff3": (("rd1", 1),),
+    "fg3": (("ru0", 4), ("rd0", 3), ("ru2", 1),),
+    "fh3": (("rd2", 1),),
+    "fi3": (("ru3", 0),),
+    "ba": (("ru1", 3), ("rd3", 0),),
+    "bb": (("rd1", 2),),
+    "og": (("ru1", 4), ("ru2", 2),),
+    "ga": (("ro", 0),),
+    "a0": (("rd2", 2),),
+    "A0": (("rd1", 3),),
+    "a1": (("ru3", 1),),
+    "A1": (("ru2", 3), ("rd3", 1),),
+    "H0": (("ro", 1),),
+    "a2": (("ru2", 4), ("rd2", 3), ("rh0", 0),),
+    "A2": (("ru3", 2),),
+    "a3": (("rd3", 2),),
+    "H1": (("ro", 2),),
+    "a4": (("ru3", 3), ("rh1", 0),),
+    "A4": (("rh0", 1),),
+    "a5": (("ru3", 4), ("rd3", 3), ("rh1", 1), ("rdl", 0),),
+    "g2": (("rh0", 2), ("rh2", 0),),
+    "g1": (("ro", 3), ("rh1", 2),),
+    "g0": (("rdl", 1),),
+    "na": (("rh2", 1),),
+    "end": (("ru0", 5), ("ru1", 5), ("ru2", 5), ("ru3", 5), ("ro", 4), ("rS", 0), ("rh2", 2), ("rh0", 3), ("rS", 1), ("rh1", 3), ("rdl", 2), ("rh0", 4), ("ro", 5), ("rh1", 4), ("rh2", 3), ("rS", 2), ("rh0", 5), ("rS", 3), ("rh2", 4), ("rh1", 5), ("rS", 4), ("rh2", 5), ("rS", 5),),
+}
+
 VMEM_BYTES = 63 * 1024 * 1024
 
 

time: 177 us -> 152 us (0.86)
  Pallas kernels: 176 us -> 151 us
    pallas_call x1, Pallas kernels: 171 us -> 146 us  [by_kernel(): pl.pallas_call(layer_kernel, out_shape=(shape((count, width), BF16), shap...]
where the time goes in v3:
time: 152 us; the launch traced here: 151 us
  Pallas kernels  151 us (99%)
    pallas_call x1, Pallas kernels, by_kernel(): pl.pallas_call(layer_kernel, out_shape=(shape((count, width), BF16), shap...  146 us
    pallas_call x1, Pallas kernels, by_kernel(): pl.pallas_call(hand_over, out_shape=tuple((shape(a.shape, a.dtype) for a...  4.4 us

profile of v3, /device:TPU:0, one launch (start us, length us, event | category | flops | bytes accessed | tf_op | source)
XLA Modules:
  0.0 151.4 jit_solution(17012169319595623091)
XLA Ops:
  0.7 146.2 %shard_map.254 = (bf16[512,768]{1,0:T(8,128)(2,1)}, f32[512,768]{1,0:T(8,128)}, f32[24,2304]{1,0:T(8,128)}, f32[24,768]{1,0:T(8,128)}, f32[24,3072]{1,0:T(8,128)}, /*index=5*/f32[96,768]{1,0:T(8,128)}, f32[8,128]{1,0:T(8,128)}) custom-call(s32[1,3]{1,0:T(1,128)} %clip_ref.1, bf16[512,768]{1,0:T(8,128)(2,1)} %tok_ref.1, bf16[512,768]{1,0:T(8,128)(2,1)} %cot_ref.1, ...), custom_call_target="tpu_custom_call" | custom-call | tf_op jit(solution)/shard_map/pallas_call | solution.py:1079
  146.8 4.4 %shard_map.255 = (bf16[512,768]{1,0:T(8,128)(2,1)}, f32[512,768]{1,0:T(8,128)}, f32[24,2304]{1,0:T(8,128)}, f32[24,768]{1,0:T(8,128)}, f32[24,3072]{1,0:T(8,128)...) custom-call(f32[8,128]{1,0:T(8,128)} %get-tuple-element.35.small_ref, ...), custom_call_target="tpu_custom_call" | custom-call | tf_op jit(solution)/shard_map/pallas_call | solution.py:1096

commit v4 on v3

--- a/solution.py
+++ b/solution.py
@@ -14,7 +14,7 @@
 F32 = jnp.float32
 BF16 = jnp.bfloat16
 ALL = slice(None)
-CHUNK = 64
+CHUNK = 256
 
 
 def layer_norm(inputs, ln_gain, ln_bias):
@@ -348,7 +348,7 @@
     slabs, downs, smalls, gsmalls, weights, w_up,
     row_c, row_d, row_n, row_z, late_d, late_n, late_z, down_c, down_d, down_n, down_z, sm_c, sm_d, sm_n, sm_z,
     qkv, n1t, n1, att_t, middle, n2, n2t, g2, acc_out, acc_grad, act, grad_h, pre, grad_act,
-    tok, cot, bias, lse, dq_t, vec24, vec48, vec96, merged_bias, group_sums, sums, up_sums, block_out,
+    tok, cot, bias, lse, dq_t, vec24, vec48, vec96, merged_bias, group_sums, sums, up_sums,
     ag_send, ag_recv, rs_send, rs_recv, local,
 ):
     n_z, width = slabs.shape[1], slabs.shape[-1]
@@ -385,10 +385,11 @@
         return ref.at[(*([ALL] * (len(ref.shape) - 1)), pl.ds(side * cut, cut))]
 
     to_x, to_y, to_c = device(z, 1 - x, core, y), device(z, x, core, 1 - y), device(z, x, 1 - core, y)
-    near_z, far_z, last_z = z + 1 - 2 * lax.rem(z, 2), lax.rem(z + 2, n_z), n_z - 1 - z
+    z_places = (z + 1 - 2 * lax.rem(z, 2), lax.rem(z + 2, n_z), n_z - 1 - z)
+    along_z = [device(at, x, core, y) for at in z_places]
+    other_pair = pl.ds(2 * (1 - lax.div(z, 2)), 2)
     inner = lax.rem(z + 1, n_z) >= 2
-    to_near, to_far, to_last = device(near_z, x, core, y), device(far_z, x, core, y), device(last_z, x, core, y)
-    Z1, Z2, Z3, ZR, X0, Y0, DX, DY, C0 = range(9)
+    Z0, Z1, Z2, ZR, X0, Y0, X1, Y1, X2, Y2, DX, DY, C0 = range(13)
 
     def remote(src, dst, sems, row, sem, to, recv_sem=None):
         send, recv = sems
@@ -401,26 +402,38 @@
         for copy in copies:
             getattr(copy, what)()
 
+    one, plane = (x, core, y), (ALL, core, ALL)
+
     def ag_copies(unit, phase):
         view, row, phases, along = unit
         sems = (ag_send, ag_recv)
-        late = phases.index("z") > phases.index("near") if "z" in phases and "near" in phases else False
-        held = z if late else ALL
-        own = view((z, *along))
+        held = z if along is plane else ALL
+
+        def both(at, sem):
+            mine = view((at, x, core, y))
+            return [remote(mine, mine, sems, row, sem, to_x), remote(mine, mine, sems, row, sem + 1, to_y)]
+
+        def own_to(*which):
+            own = view((z, *along))
+            return [remote(own, own, sems, row, k, along_z[k]) for k in which]
+
         if phase == "z":
-            return [remote(own, own, sems, row, Z1, to_near), remote(own, own, sems, row, Z2, to_far)]
-        if phase == "z near":
-            return [remote(own, own, sems, row, Z1, to_near)]
-        if phase == "z far":
-            return [remote(own, own, sems, row, Z2, to_far)]
-        if phase == "z inner":
-            return [remote(own, own, sems, row, Z3, to_last)]
+            return own_to(Z0, Z1)
+        if phase == "zd":
+            return own_to(Z0, Z1, Z2)
+        if phase in ("z near", "z far", "z last"):
+            return own_to(("z near", "z far", "z last").index(phase))
         if phase == "relay":
-            passed = view((far_z, *along))
-            return [remote(passed, passed, sems, row, ZR, to_near, Z3)]
+            passed = view((z_places[1], *along))
+            return [remote(passed, passed, sems, row, ZR, along_z[0], Z2)]
+        if phase == "own":
+            return both(z, X1)
+        if phase == "pair":
+            return both(z_places[0], X2)
+        if phase == "rest":
+            return both(other_pair, X0)
         if phase == "near":
-            mine = view((held, x, core, y))
-            return [remote(mine, mine, sems, row, X0, to_x), remote(mine, mine, sems, row, Y0, to_y)]
+            return both(held, X0)
         if phase == "across":
             from_x, from_y = view((held, 1 - x, core, y)), view((held, x, core, 1 - y))
             first = half_of(from_x, 0)
@@ -429,70 +442,71 @@
                 second = half_of(from_y, 1)
                 copies.append(remote(second, second, sems, row, DX, to_x))
             return copies
-        plane = view((ALL, ALL, core, ALL))
-        return [remote(plane, plane, sems, row, C0, to_c)]
-
-    def ag_arrived(unit, phase):
-        if phase == "z":
-            @pl.when(jnp.logical_not(inner))
-            def _():
-                do_all(ag_copies(unit, "z far"), "wait_recv")
-            do_all(ag_copies(unit, "z near") + ag_copies(unit, "z inner"), "wait_recv")
-        else:
+        whole_plane = view((ALL, ALL, core, ALL))
+        return [remote(whole_plane, whole_plane, sems, row, C0, to_c)]
+
+    def ag_wait(unit, *phases):
+        for phase in phases:
             do_all(ag_copies(unit, phase), "wait_recv")
 
     def ag_stage(unit, stage):
         phases = unit[2]
-        waits = [p for p in phases[:stage] if p != "relay"][-1:]
         phase = phases[stage] if stage < len(phases) else None
         if phase == "relay":
             @pl.when(inner)
             def _():
-                do_all(ag_copies(unit, "z far"), "wait_recv")
+                ag_wait(unit, "z far")
                 do_all(ag_copies(unit, "relay"), "start")
             return
-        if waits:
-            ag_arrived(unit, waits[0])
+        if phase == "pair":
+            ag_wait(unit, "z near")
+        elif phase == "rest":
+            ag_wait(unit, "z far", "z last")
+        elif phase == "across" and "own" in phases:
+            ag_wait(unit, "own", "pair", "rest")
+        elif stage > 0 and phases[stage - 1] == "relay":
+            @pl.when(jnp.logical_not(inner))
+            def _():
+                ag_wait(unit, "z far")
+            ag_wait(unit, "z near", "z last")
+        elif stage > 0 and phases[stage - 1] != "own":
+            ag_wait(unit, phases[stage - 1])
         if phase:
             do_all(ag_copies(unit, phase), "start")
             if phase == "z":
                 @pl.when(inner)
                 def _():
-                    do_all(ag_copies(unit, "z inner"), "start")
+                    do_all(ag_copies(unit, "z last"), "start")
         else:
             for sent in phases:
                 if sent != "relay":
                     do_all(ag_copies(unit, sent), "wait_send")
-            if "z" in phases:
+            if "relay" in phases:
                 @pl.when(inner)
                 def _():
-                    do_all(ag_copies(unit, "z inner") + ag_copies(unit, "relay"), "wait_send")
-
-    first_z = ("z", "relay", "near", "across", "core")
-    last_z_order = ("near", "across", "z", "relay", "core")
-    one, plane_of = (x, core, y), (ALL, core, ALL)
-    small_unit = (small_view(smalls), 0, first_z, one)
-
-    def gather_unit(block, late=False):
-        return (row_view(block), 1 + block, last_z_order if late else first_z, plane_of if late else one)
-
-    down_first = (lambda at: downs.at[at], 5 + 2 * n_z, ("z", "relay"), one)
-
-    def gather_down(tile):
-        return (down_view(tile), 5 + n_z + tile, ("near", "across", "core"), one)
-
-    units = {"aS": small_unit, "adp": down_first}
+                    do_all(ag_copies(unit, "z last") + ag_copies(unit, "relay"), "wait_send")
+
+    ORDERS = {
+        "plain": ("z", "relay", "near", "across", "core"), "direct": ("zd", "near", "across", "core"),
+        "boot": ("own", "zd", "pair", "rest", "across", "core"),
+        "late": ("near", "across", "z", "relay", "core"), "late direct": ("near", "across", "zd", "core"),
+    }
+
+    def gather_unit(block, kind):
+        return (row_view(block), 1 + block, ORDERS[kind], plane if kind[:4] == "late" else one)
+
+    units = {"aS": (small_view(smalls), 0, ORDERS["direct"], one)}
+    units["adp"] = (lambda at: downs.at[at], 5 + 2 * n_z, ("z", "relay") if KINDS.get("adp", "plain") == "plain" else ("zd",), one)
     for block in range(4):
-        units[f"ab{block}"] = gather_unit(block)
+        units[f"ab{block}"] = gather_unit(block, KINDS.get(f"ab{block}", "plain"))
     for tile in range(n_z):
-        units[f"au{tile}"] = gather_unit(4 + tile, tile in LATE_GATHERS)
-        units[f"ad{tile}"] = gather_down(tile)
+        units[f"au{tile}"] = gather_unit(4 + tile, KINDS.get(f"au{tile}", "plain"))
+        units[f"ad{tile}"] = (down_view(tile), 5 + n_z + tile, ("near", "across", "core"), one)
 
     def rs_copies(unit, phase):
         view, row, phases, landing, along = unit
         sems = (rs_send, rs_recv)
-        late = "near" in phases and "z" in phases and phases.index("z") < phases.index("near")
-        held = z if late else ALL
+        held = z if along is plane else ALL
         if phase == "core":
             return [remote(view((ALL, ALL, 1 - core, ALL)), landing["core"], sems, row, C0, to_c)]
         if phase == "across":
@@ -506,13 +520,10 @@
                 remote(view((held, 1 - x, core, y)), landing["x"], sems, row, X0, to_x),
                 remote(view((held, x, core, 1 - y)), landing["y"], sems, row, Y0, to_y),
             ]
-        if phase == "z":
-            return [remote(view((near_z, *along)), landing["z1"], sems, row, Z1, to_near)]
-        if phase == "z inner":
-            return [remote(view((last_z, *along)), landing["z3"], sems, row, Z3, to_last)]
         if phase == "z outer":
-            return [remote(view((last_z, *along)), landing["zr"], sems, row, ZR, to_near)]
-        return [remote(view((far_z, *along)), landing["z2"], sems, row, Z2, to_far)]
+            return [remote(view((z_places[2], *along)), landing["z"].at[ZR], sems, row, ZR, along_z[0])]
+        which = {"z": (Z0,), "z far": (Z1,), "z last": (Z2,), "zd": (Z0, Z1, Z2)}[phase]
+        return [remote(view((z_places[k], *along)), landing["z"].at[k], sems, row, k, along_z[k]) for k in which]
 
     def add_into(target, *sources):
         total = target[...].astype(F32)
@@ -536,101 +547,102 @@
 
         lax.fori_loop(0, target.shape[0], step, 0)
 
-    def rs_take(unit, phase):
+    def rs_stage(unit, stage):
         view, _, phases, landing, along = unit
-        late = "near" in phases and "z" in phases and phases.index("z") < phases.index("near")
-        held = z if late else ALL
-        if phase == "z":
-            do_all(rs_copies(unit, "z") + rs_copies(unit, "z far"), "wait_recv")
-            add_all(view((z, *along)), landing["z1"], landing["z2"])
-
+        held = z if along is plane else ALL
+        before = phases[stage - 1] if stage > 0 else None
+        phase = phases[stage] if stage < len(phases) else None
+        if phase == "z far":
             @pl.when(inner)
             def _():
-                do_all(rs_copies(unit, "z inner"), "wait_recv")
-                add_all(view((z, *along)), landing["z3"])
-            return
-        do_all(rs_copies(unit, phase), "wait_recv")
-        if phase == "core":
+                do_all(rs_copies(unit, "z outer"), "wait_recv")
+                add_all(view((z_places[1], *along)), landing["z"].at[ZR])
+        elif before == "z far":
+            rs_wait(unit, "z", "z far")
+            add_all(view((z, *along)), landing["z"].at[Z0], landing["z"].at[Z1])
+
+            @pl.when(inner)
+            def _():
+                rs_wait(unit, "z last")
+                add_all(view((z, *along)), landing["z"].at[Z2])
+        elif before:
+            rs_wait(unit, before)
+        if before == "core":
             add_all(view((ALL, ALL, core, ALL)), landing["core"])
-        elif phase == "across":
+        elif before == "across":
             on_y = view((held, x, core, 1 - y))
             add_all(half_of(on_y, 0), landing["dx"])
             if on_y.shape[-1] >= 2 * 128:
                 add_all(half_of(view((held, 1 - x, core, y)), 1), landing["dy"])
-        else:
+        elif before == "near":
             add_all(view((held, x, core, y)), landing["x"], landing["y"])
-
-    def rs_stage(unit, stage):
-        view, _, phases, landing, along = unit
-        if stage == len(phases):
-            rs_take(unit, phases[-1])
-            return
-        phase = phases[stage]
-        if phase == "z far":
-            @pl.when(inner)
-            def _():
-                do_all(rs_copies(unit, "z outer"), "wait_recv")
-                add_all(view((far_z, *along)), landing["zr"])
+        elif before == "zd":
+            add_all(view((z, *along)), *[landing["z"].at[k] for k in (Z0, Z1, Z2)])
+        if phase:
             do_all(rs_copies(unit, phase), "start")
-            return
-        if stage > 0:
-            rs_take(unit, "z" if phases[stage - 1] == "z far" else phases[stage - 1])
-        do_all(rs_copies(unit, phase), "start")
         if phase == "z":
             @pl.when(inner)
             def _():
-                do_all(rs_copies(unit, "z inner"), "start")
+                do_all(rs_copies(unit, "z last"), "start")
 
             @pl.when(jnp.logical_not(inner))
             def _():
                 do_all(rs_copies(unit, "z outer"), "start")
 
+    def rs_wait(unit, *phases):
+        for phase in phases:
+            do_all(rs_copies(unit, phase), "wait_recv")
+
     def rs_end(unit, *results):
         view, _, phases, landing, along = unit
-        own = view((z, x, core, y))
-        if phases[-1] == "near":
-            do_all(rs_copies(unit, "near"), "wait_recv")
-            total = own[...].astype(F32) + landing["x"][...].astype(F32) + landing["y"][...].astype(F32)
+        last = phases[-1]
+        if last == "near":
+            sources = [landing["x"], landing["y"]]
         else:
-            do_all(rs_copies(unit, "z") + rs_copies(unit, "z far"), "wait_recv")
-            total = own[...].astype(F32) + landing["z1"][...].astype(F32) + landing["z2"][...].astype(F32)
+            sources = [landing["z"].at[k] for k in ((Z0, Z1) if last == "z far" else (Z0, Z1, Z2))]
+        rs_wait(unit, *(("z", "z far") if last == "z far" else (last,)))
+        total = view((z, x, core, y))[...].astype(F32)
+        for part in sources:
+            total = total + part[...].astype(F32)
         size = total.shape[-1] // len(results)
         for k, result in enumerate(results):
             result[...] = total[:, k * size : (k + 1) * size]
-        if phases[-1] != "near":
+        if last == "z far":
             @pl.when(inner)
             def _():
-                do_all(rs_copies(unit, "z inner"), "wait_recv")
+                rs_wait(unit, "z last")
                 for k, result in enumerate(results):
-                    result[...] += landing["z3"][:, k * size : (k + 1) * size].astype(F32)
+                    result[...] += landing["z"][Z2, :, k * size : (k + 1) * size].astype(F32)
 
     def rs_sent(unit):
         for phase in unit[2]:
             do_all(rs_copies(unit, phase), "wait_send")
-        if "z" in unit[2]:
+        if "z far" in unit[2]:
             @pl.when(inner)
             def _():
-                do_all(rs_copies(unit, "z inner"), "wait_send")
+                do_all(rs_copies(unit, "z last"), "wait_send")
 
             @pl.when(jnp.logical_not(inner))
             def _():
                 do_all(rs_copies(unit, "z outer"), "wait_send")
 
-    back_last, back_first = ("core", "across", "near", "z", "z far"), ("core", "z", "z far", "across", "near")
-
-    def z_landing(ref):
-        return {"z1": ref.at[0], "z2": ref.at[1], "z3": ref.at[2], "zr": ref.at[3]}
-
-    def row_unit(block, row, late=None):
-        if late is not None:
-            landing = {"core": row_c.at[block], "dx": late_d.at[late, 0], "dy": late_d.at[late, 1], "x": late_n.at[late, 0], "y": late_n.at[late, 1], **z_landing(late_z.at[late])}
-            return (row_view(block), row, back_first, landing, plane_of)
-        landing = {"core": row_c.at[block], "dx": row_d.at[block, 0], "dy": row_d.at[block, 1], "x": row_n.at[block, 0], "y": row_n.at[block, 1], **z_landing(row_z.at[block])}
-        return (row_view(block), row, back_last, landing, one)
+    BACK = {
+        "plain": ("core", "across", "near", "z", "z far"), "direct": ("core", "across", "near", "zd"),
+        "late": ("core", "z", "z far", "across", "near"), "late direct": ("core", "zd", "across", "near"),
+    }
+
+    def row_unit(block, row, name):
+        if name in LATE_SUMS:
+            late = LATE_SUMS.index(name)
+            landing = {"core": row_c.at[block], "dx": late_d.at[late, 0], "dy": late_d.at[late, 1], "x": late_n.at[late, 0], "y": late_n.at[late, 1], "z": late_z.at[late]}
+            return (row_view(block), row, BACK[KINDS[name]], landing, plane)
+        at = block - sum(earlier in LATE_SUMS for earlier in ROW_SUMS[:block])
+        landing = {"core": row_c.at[block], "dx": row_d.at[at, 0], "dy": row_d.at[at, 1], "x": row_n.at[at, 0], "y": row_n.at[at, 1], "z": row_z.at[at]}
+        return (row_view(block), row, BACK[KINDS.get(name, "plain")], landing, one)
 
     def down_unit(tile, row):
         landing = {"core": down_c.at[tile], "dx": down_d.at[tile, 0], "dy": down_d.at[tile, 1], "x": down_n.at[tile, 0], "y": down_n.at[tile, 1]}
-        return (down_view(tile), row, back_last[:3], landing, one)
+        return (down_view(tile), row, BACK["plain"][:3], landing, one)
 
     def block_columns(block):
         return pl.ds(block * width, width)
@@ -638,16 +650,16 @@
     third = width // 3
     results = {"rdl": [gdown_ref], "ro": [gout_ref], "rS": [gsmall_ref]}
     for t in range(n_z):
-        units[f"ru{t}"] = row_unit(4 + t, t, LATE_SUMS.index(t) if t in LATE_SUMS else None)
+        units[f"ru{t}"] = row_unit(4 + t, t, f"ru{t}")
         units[f"rd{t}"] = down_unit(t, n_z + t)
         results[f"ru{t}"] = [gup_ref.at[:, block_columns(t)]]
     for g in range(3):
-        units[f"rh{g}"] = row_unit(g, 2 * n_z + g)
+        units[f"rh{g}"] = row_unit(g, 2 * n_z + g, f"rh{g}")
         results[f"rh{g}"] = [gqkv_ref.at[:, pl.ds(j * width + g * third, third)] for j in range(3)]
-    units["ro"] = row_unit(3, 2 * n_z + 3)
-    small_landing = {"core": sm_c, "dx": sm_d, "x": sm_n.at[0], "y": sm_n.at[1], **z_landing(sm_z)}
-    units["rS"] = (small_view(gsmalls), 2 * n_z + 4, back_last, small_landing, one)
-    units["rdl"] = (lambda at: downs.at[at], 2 * n_z + 5, ("z", "z far"), z_landing(down_z), one)
+    units["ro"] = row_unit(3, 2 * n_z + 3, "ro")
+    small_landing = {"core": sm_c, "dx": sm_d, "x": sm_n.at[0], "y": sm_n.at[1], "z": sm_z}
+    units["rS"] = (small_view(gsmalls), 2 * n_z + 4, BACK["direct"], small_landing, one)
+    units["rdl"] = (lambda at: downs.at[at], 2 * n_z + 5, ("z", "z far") if KINDS.get("rdl", "plain") == "plain" else ("zd",), {"z": down_z}, one)
 
     def point(name):
         for unit_name, stage in TABLE.get(name, ()):
@@ -665,7 +677,7 @@
                 pl.when(index == k)(functools.partial(point, name))
 
     barrier = pltpu.get_barrier_semaphore()
-    partners = [to_near, to_far, to_last, to_x, to_y, to_c]
+    partners = [*along_z, to_x, to_y, to_c]
     for to in partners:
         pl.semaphore_signal(barrier, inc=1, device_id=to, device_id_type=MESH)
     shards = []
@@ -767,7 +779,7 @@
         keep = lane < 64 if head == 0 else lane >= 64
         return jnp.where(keep, values, jnp.zeros_like(values))
 
-    q_block = 256
+    q_block = 512
     parts = count // q_block
     per_group = pairs // 3
 
@@ -789,8 +801,6 @@
         queries = qkv[group, :, at_q] * 0.125
         values_t = qkv[group, :, at_v].T
         for head in range(2):
-            if head:
-                points_at(p, [f"T{k}" for k in range(pairs)])
             mine = one_head(queries, head)
             for part in range(parts):
                 span = slice(part * q_block, (part + 1) * q_block)
@@ -837,16 +847,13 @@
     acc_grad[...] = jnp.zeros_like(acc_grad)
 
     def store_rows(block, lhs_t, rhs):
-        deep = width // n_z
         size = slabs.shape[-2]
-
-        def step(z_at, carry):
-            total = nn_dot(lhs_t[rows_of(z_at, deep), :], rhs)
-            for k in range(8):
-                slabs[block, z_at, k // 4, k // 2 % 2, k % 2] = total[k * size : (k + 1) * size].astype(BF16)
-            return carry
-
-        lax.fori_loop(0, n_z, step, 0)
+        for first in range(0, width, 192):
+            total = nn_dot(lhs_t[first : first + 192, :], rhs)
+            for k in range(192 // size // 2):
+                at = first // size + 2 * k
+                two = total[2 * k * size : 2 * (k + 1) * size].reshape(2, size, width).astype(BF16)
+                slabs[block, at // 8, at // 4 % 2, at // 2 % 2] = two
 
     def feed(t, carry):
         def step_point(name):
@@ -854,29 +861,42 @@
 
         step_point("fa")
         assemble(4 + t, w_up)
+        up_bias = vec96[t, 6:7, :]
+        half = count // 2
+
+        def into_hidden(rows):
+            pre[rows] = nn_dot(n2[rows], w_up[...])
+
+        def into_grads(rows):
+            grad_act[rows] = nt_dot(g2[rows], downs[t].reshape(width, width))
+
+        def gelu_rows(first):
+            for at in range(first, first + half, 32):
+                rows = slice(at, at + 32)
+                active, slope = gelu_both(pre[rows] + up_bias)
+                act[rows] = active.astype(BF16)
+                grad_h[rows] = (grad_act[rows] * slope).astype(BF16)
+
+        def out_of(rows):
+            acc_out[rows] += nn_dot(act[rows], downs[t].reshape(width, width))
+            acc_grad[rows] += nt_dot(grad_h[rows], w_up[...])
+
+        upper, lower = slice(0, half), slice(half, count)
         step_point("fb")
-        pre[...] = nn_dot(n2[...], w_up[...])
+        into_hidden(upper)
         step_point("fc")
-        w_down = downs[t].reshape(width, width)
-        grad_act[...] = nt_dot(g2[...], w_down)
-        up_bias = vec96[t, 6:7, :]
-
-        def gelu_step(i, carry):
-            at = rows_of(i, 32)
-            active, slope = gelu_both(pre[at, :] + up_bias)
-            act[at, :] = active.astype(BF16)
-            grad_h[at, :] = (grad_act[at, :] * slope).astype(BF16)
-            return carry
-
+        into_grads(upper)
         step_point("fd")
-        lax.fori_loop(0, count // 64, gelu_step, 0)
+        into_hidden(lower)
+        into_grads(lower)
+        gelu_rows(0)
         step_point("fe")
-        lax.fori_loop(count // 64, count // 32, gelu_step, 0)
+        out_of(upper)
+        gelu_rows(half)
+        step_point("ff")
+        out_of(lower)
+        step_point("fg")
         up_sums[t, 6:7, :] = column_sums(grad_h[...])[0:1]
-        step_point("ff")
-        acc_out[...] += nn_dot(act[...], w_down)
-        step_point("fg")
-        acc_grad[...] += nt_dot(grad_h[...], w_up[...])
         step_point("fh")
         store_rows(4 + t, n2t, grad_h[...])
         step_point("fi")
@@ -910,6 +930,7 @@
         return (gain_sum + fold_rows(e * normed), bias_sum + fold_rows(e))
 
     zero = jnp.zeros((8, width), F32)
+    block_out = act
     point("ba")
     carry = lax.fori_loop(0, chunks // 2, norm_two_back, (zero, zero))
     point("bb")
@@ -937,8 +958,6 @@
         grad_keys = jnp.zeros((count, 128), F32)
         grad_values = jnp.zeros((count, 128), F32)
         for head in range(2):
-            if head:
-                points_at(p, [f"A{k}" for k in range(pairs)])
             my_queries, my_grads = one_head(queries, head), one_head(grads, head)
             for part in range(parts):
                 span = slice(part * q_block, (part + 1) * q_block)
@@ -1027,9 +1046,9 @@
         vmem((4, width, width), BF16),
         vmem((width, width), BF16),
         vmem((blocks, n_z, 2, 2, size, width), BF16),
-        vmem((blocks, 2, n_z, size, width // 2), BF16),
-        vmem((blocks, 2, n_z, size, width), BF16),
-        vmem((blocks, n_z, size, width), BF16),
+        vmem((blocks - len(LATE_SUMS), 2, n_z, size, width // 2), BF16),
+        vmem((blocks - len(LATE_SUMS), 2, n_z, size, width), BF16),
+        vmem((blocks - len(LATE_SUMS), n_z, size, width), BF16),
         vmem((max(len(LATE_SUMS), 1), 2, size, width // 2), BF16),
         vmem((max(len(LATE_SUMS), 1), 2, size, width), BF16),
         vmem((max(len(LATE_SUMS), 1), n_z, 2, 2, size, width), BF16),
@@ -1040,7 +1059,7 @@
         vmem((n_z, 2, 2, 8, 128), F32),
         vmem((n_z, 8, 128), F32),
         vmem((2, n_z, 8, 128), F32),
-        vmem((n_z, 8, 128), F32),
+        vmem((n_z - 1, 8, 128), F32),
         vmem((3, count, width), BF16),
         vmem((width, count), BF16),
         vmem((count, width), BF16),
@@ -1067,11 +1086,10 @@
         vmem((3, 8, width), F32),
         vmem((3, 8, width), F32),
         vmem((n_z, 8, width), F32),
-        vmem((count, width), BF16),
-        dma((6 + 2 * n_z, 9)),
-        dma((6 + 2 * n_z, 9)),
-        dma((6 + 2 * n_z, 9)),
-        dma((6 + 2 * n_z, 9)),
+        dma((6 + 2 * n_z, 13)),
+        dma((6 + 2 * n_z, 13)),
+        dma((6 + 2 * n_z, 13)),
+        dma((6 + 2 * n_z, 13)),
         dma((13 + n_z,)),
     ]
     anywhere, whole = pl.BlockSpec(memory_space=pl.ANY), pl.BlockSpec(memory_space=pltpu.VMEM)
@@ -1120,73 +1138,71 @@
         copy.wait()
 
 
-LATE_GATHERS = ()
-LATE_SUMS = ()
+KINDS = {
+    "ab0": "boot",
+    "ab1": "boot",
+    "ab2": "boot",
+    "ab3": "boot",
+    "au0": "late",
+    "au1": "boot",
+    "au2": "boot",
+    "au3": "late",
+    "ro": "direct",
+    "ru0": "late",
+    "ru1": "late",
+    "ru3": "late",
+}
+LATE_SUMS = ("ru0", "ru1", "ru3")
 TABLE = {
-    "mask": (("aS", 0), ("ab0", 0),),
-    "vec": (("ab1", 0), ("aS", 1), ("ab0", 1), ("ab2", 0), ("ab1", 1), ("aS", 2), ("ab3", 0), ("ab0", 2), ("ab2", 1), ("aS", 3), ("adp", 0), ("ab1", 2), ("ab3", 1), ("ab2", 2), ("aS", 4), ("aS", 5),),
-    "turn": (("ab0", 3),),
-    "q0": (("ab1", 3), ("adp", 1), ("ab2", 3), ("ab0", 4), ("au0", 0), ("ab3", 2), ("ab0", 5), ("ab1", 4),),
-    "t0": (("au1", 0),),
-    "T0": (("ab1", 5), ("ab2", 4), ("adp", 2), ("ad0", 0),),
-    "t1": (("au0", 1), ("ad1", 0), ("ab2", 5), ("au2", 0),),
-    "q1": (("au1", 1), ("au3", 0),),
-    "t2": (("ab3", 3),),
-    "T2": (("au0", 2), ("au2", 1),),
-    "T3": (("au3", 1),),
-    "q2": (("ad0", 1),),
-    "T4": (("ab3", 4), ("au1", 2),),
-    "T5": (("ab3", 5),),
-    "tb": (("au0", 3),),
-    "n2a": (("ad0", 2), ("ad1", 1),),
-    "n2b": (("au2", 2), ("ad0", 3),),
-    "fa0": (("au0", 4), ("au1", 3), ("au0", 5), ("ad1", 2), ("ad2", 0),),
-    "fd0": (("ad1", 3),),
-    "fe0": (("au2", 3),),
-    "ff0": (("au1", 4), ("au3", 2),),
-    "fh0": (("au1", 5),),
-    "fi0": (("ru0", 0),),
-    "fa1": (("ad2", 1), ("rd0", 0),),
-    "fd1": (("au2", 4), ("ad3", 0),),
-    "fe1": (("au2", 5),),
-    "ff1": (("au3", 3),),
-    "fi1": (("ad2", 2), ("ru0", 1), ("ru1", 0),),
-    "fa2": (("ad2", 3), ("rd0", 1), ("rd1", 0),),
-    "fb2": (("ad3", 1),),
-    "fd2": (("au3", 4), ("ru1", 1),),
-    "fe2": (("au3", 5), ("ru0", 2),),
-    "fh2": (("ad3", 2), ("rd0", 2),),
-    "fi2": (("ru2", 0),),
-    "fa3": (("ad3", 3), ("rd2", 0),),
-    "fd3": (("ru1", 2),),
-    "fe3": (("ru0", 3),),
-    "ff3": (("rd1", 1),),
-    "fg3": (("ru0", 4), ("rd0", 3), ("ru2", 1),),
-    "fh3": (("rd2", 1),),
-    "fi3": (("ru3", 0),),
-    "ba": (("ru1", 3), ("rd3", 0),),
-    "bb": (("rd1", 2),),
-    "og": (("ru1", 4), ("ru2", 2),),
-    "ga": (("ro", 0),),
+    "mask": (("aS", 0), ("ab0", 0), ("ab0", 1), ("au1", 0), ("ab3", 0),),
+    "vec": (("au1", 1), ("ab2", 0), ("ab1", 0), ("au2", 0), ("aS", 1), ("ab0", 2), ("ab3", 1), ("au3", 0), ("ab0", 3), ("aS", 2), ("au1", 2), ("ab1", 1), ("au0", 0), ("au3", 1), ("au1", 3), ("aS", 3), ("ab0", 4), ("ab2", 1), ("aS", 4),),
+    "turn": (("au0", 1), ("ab3", 2),),
+    "q0": (("ab3", 3), ("adp", 0), ("au1", 4), ("ab0", 5), ("ab2", 2), ("ab0", 6), ("ab1", 2),),
+    "t0": (("ab1", 3),),
+    "q1": (("au1", 5), ("ab3", 4), ("ab2", 3), ("au1", 6), ("adp", 1), ("au0", 2), ("ab1", 4), ("ab3", 5), ("ab3", 6), ("ab2", 4), ("ab1", 5), ("adp", 2), ("ad0", 0), ("ab1", 6),),
+    "t2": (("ab2", 5), ("ad1", 0),),
+    "t3": (("au0", 3), ("ab2", 6),),
+    "q2": (("ad2", 0), ("au2", 1),),
+    "tb": (("ad0", 1), ("au3", 2),),
+    "n2a": (("au0", 4), ("ad1", 1),),
+    "fa0": (("au0", 5), ("ad2", 1),),
+    "fc0": (("au2", 2), ("ad0", 2), ("au2", 3), ("ad0", 3), ("ad1", 2),),
+    "ff0": (("ad2", 2), ("ad3", 0), ("ad1", 3), ("au3", 3),),
+    "fi0": (("ru0", 0), ("ad2", 3), ("au2", 4),),
+    "fa1": (("rd0", 0),),
+    "fc1": (("ru0", 1),),
+    "fe1": (("rd0", 1), ("ad3", 1),),
+    "ff1": (("au3", 4),),
+    "fg1": (("au2", 5),),
+    "fi1": (("ru1", 0), ("au3", 5),),
+    "fa2": (("rd1", 0), ("au2", 6), ("rd0", 2), ("ru0", 2),),
+    "fe2": (("rd1", 1), ("ad3", 2),),
+    "fg2": (("ad3", 3),),
+    "fi2": (("ru2", 0), ("ru1", 1),),
+    "fa3": (("rd0", 3), ("rd2", 0),),
+    "fb3": (("ru2", 1),),
+    "fc3": (("rd1", 2),),
+    "fg3": (("rd2", 1), ("ru1", 2),),
+    "fi3": (("ru2", 2), ("ru3", 0),),
+    "ba": (("rd3", 0),),
+    "og": (("rd1", 3),),
+    "ga": (("rd3", 1), ("ro", 0), ("ru3", 1),),
     "a0": (("rd2", 2),),
-    "A0": (("rd1", 3),),
-    "a1": (("ru3", 1),),
-    "A1": (("ru2", 3), ("rd3", 1),),
-    "H0": (("ro", 1),),
-    "a2": (("ru2", 4), ("rd2", 3), ("rh0", 0),),
-    "A2": (("ru3", 2),),
-    "a3": (("rd3", 2),),
-    "H1": (("ro", 2),),
-    "a4": (("ru3", 3), ("rh1", 0),),
-    "A4": (("rh0", 1),),
-    "a5": (("ru3", 4), ("rd3", 3), ("rh1", 1), ("rdl", 0),),
-    "g2": (("rh0", 2), ("rh2", 0),),
-    "g1": (("ro", 3), ("rh1", 2),),
-    "g0": (("rdl", 1),),
-    "na": (("rh2", 1),),
-    "end": (("ru0", 5), ("ru1", 5), ("ru2", 5), ("ru3", 5), ("ro", 4), ("rS", 0), ("rh2", 2), ("rh0", 3), ("rS", 1), ("rh1", 3), ("rdl", 2), ("rh0", 4), ("ro", 5), ("rh1", 4), ("rh2", 3), ("rS", 2), ("rh0", 5), ("rS", 3), ("rh2", 4), ("rh1", 5), ("rS", 4), ("rh2", 5), ("rS", 5),),
+    "H0": (("ru2", 3), ("ru1", 3), ("rd3", 2), ("ru3", 2),),
+    "a2": (("rh0", 0),),
+    "a3": (("rh0", 1), ("rd2", 3), ("ru1", 4),),
+    "H1": (("ru2", 4), ("rd3", 3), ("ro", 1), ("ru0", 3),),
+    "a4": (("rdl", 0), ("rh0", 2), ("rh1", 0),),
+    "a5": (("rh1", 1),),
+    "H2": (("ro", 2), ("rdl", 1),),
+    "g2": (("rh2", 0),),
+    "g0": (("rh2", 1),),
+    "na": (("rh1", 2),),
+    "nb": (("rh0", 3),),
+    "end": (("ru2", 5), ("ru1", 5), ("rS", 0), ("rh0", 4), ("rh2", 2), ("ro", 3), ("rdl", 2), ("rS", 1), ("ru0", 4), ("rh1", 3), ("ru3", 3), ("rh0", 5), ("rh1", 4), ("rh2", 3), ("rS", 2), ("ru0", 5), ("ru3", 4), ("ro", 4), ("rS", 3), ("rh2", 4), ("rh1", 5), ("ru3", 5), ("rS", 4), ("rh2", 5),),
 }
 
+ROW_SUMS = ("rh0", "rh1", "rh2", "ro", "ru0", "ru1", "ru2", "ru3")
 VMEM_BYTES = 63 * 1024 * 1024
 
 
@@ -1204,7 +1220,7 @@
         and 2 * width // devices <= 128
         and hidden // devices <= 128
         and width // devices == 24
-        and (tokens.shape[0] // devices) % 256 == 0
+        and (tokens.shape[0] // devices) % (2 * CHUNK) == 0
     )
 
 

time: 152 us -> 134 us (0.88)
  Pallas kernels: 151 us -> 133 us
    pallas_call x1, Pallas kernels: 146 us -> 129 us  [by_kernel(): pl.pallas_call(layer_kernel, out_shape=(shape((count, width), BF16), shap...]
where the time goes in v4:
time: 134 us
  Pallas kernels  133 us (99%)
    pallas_call x1, Pallas kernels, by_kernel(): pl.pallas_call(layer_kernel, out_shape=(shape((count, width), BF16), shap...  129 us
    pallas_call x1, Pallas kernels, by_kernel(): pl.pallas_call(hand_over, out_shape=tuple((shape(a.shape, a.dtype) for a...  4.4 us

profile of v4, /device:TPU:0, one launch (start us, length us, event | category | flops | bytes accessed | tf_op | source)
XLA Modules:
  0.0 133.8 jit_solution(7578034294907733404)
XLA Ops:
  0.7 128.6 %shard_map.254 = (bf16[512,768]{1,0:T(8,128)(2,1)}, f32[512,768]{1,0:T(8,128)}, f32[24,2304]{1,0:T(8,128)}, f32[24,768]{1,0:T(8,128)}, f32[24,3072]{1,0:T(8,128)}, /*index=5*/f32[96,768]{1,0:T(8,128)}, f32[8,128]{1,0:T(8,128)}) custom-call(s32[1,3]{1,0:T(1,128)} %clip_ref.1, bf16[512,768]{1,0:T(8,128)(2,1)} %tok_ref.1, bf16[512,768]{1,0:T(8,128)(2,1)} %cot_ref.1, ...), custom_call_target="tpu_custom_call" | custom-call | tf_op jit(solution)/shard_map/pallas_call | solution.py:1097
  129.2 4.4 %shard_map.255 = (bf16[512,768]{1,0:T(8,128)(2,1)}, f32[512,768]{1,0:T(8,128)}, f32[24,2304]{1,0:T(8,128)}, f32[24,768]{1,0:T(8,128)}, f32[24,3072]{1,0:T(8,128)...) custom-call(f32[8,128]{1,0:T(8,128)} %get-tuple-element.35.small_ref, ...), custom_call_target="tpu_custom_call" | custom-call | tf_op jit(solution)/shard_map/pallas_call | solution.py:1114

commit v5 on v4

--- a/solution.py
+++ b/solution.py
@@ -342,14 +342,56 @@
     return total.reshape(-1, 8, 128)
 
 
+Z0, Z1, Z2, ZR, X0, Y0, X1, Y1, X2, Y2, DX, DY, C0 = range(13)
+ORDERS = {
+    "plain": ("z", "relay", "near", "across", "core"),
+    "direct": ("zd", "near", "across", "core"),
+    "boot": ("own", "zd", "pair", "rest", "across", "core"),
+    "late": ("near", "across", "z", "relay", "core"),
+    "late direct": ("near", "across", "zd", "core"),
+}
+BACK = {
+    "plain": ("core", "across", "near", "z", "z far"),
+    "direct": ("core", "across", "near", "zd"),
+    "late": ("core", "z", "z far", "across", "near"),
+    "late direct": ("core", "zd", "across", "near"),
+}
+
+
+def phases_of(name):
+    kind = "direct" if name[1:] == "S" else KINDS.get(name, "plain")
+    if name[:2] == "ad":
+        return (("z", "relay") if kind == "plain" else ("zd",)) if name == "adp" else ("near", "across", "core")
+    if name[:2] == "rd":
+        return (("z", "z far") if kind == "plain" else ("zd",)) if name == "rdl" else ("core", "across", "near")
+    return (ORDERS if name[0] == "a" else BACK)[kind]
+
+
+def semaphore_slots():
+    used = {
+        "z": (Z0, Z1, Z2), "relay": (ZR,), "zd": (Z0, Z1, Z2), "own": (X1, Y1), "pair": (X2, Y2), "rest": (X0, Y0),
+        "near": (X0, Y0), "across": (DX, DY), "core": (C0,), "z far": (ZR, Z1),
+    }
+    gathers = ["aS", "ab0", "ab1", "ab2", "ab3", "adp", "au0", "ad0", "au1", "ad1", "au2", "ad2", "au3", "ad3"]
+    sums = ["ru0", "rd0", "ru1", "rd1", "ru2", "rd2", "ru3", "rd3", "ro", "rdl", "rh0", "rh1", "rh2", "rS"]
+    slots = []
+    for names in (gathers, sums):
+        places = {}
+        for name in names:
+            for sem in sorted({sem for phase in phases_of(name) for sem in used[phase]}):
+                places[name, sem] = len(places)
+        slots.append(places)
+    return slots[0], slots[1], max(len(slots[0]), len(slots[1])), len(slots[0])
+
+
 def layer_kernel(
     clip_ref, tok_ref, cot_ref, v0, v1, v2, v3, v4, v5, v6, v7, wqkv_ref, wout_ref, wup_ref, wdown_ref,
     out_ref, tgrad_ref, gqkv_ref, gout_ref, gup_ref, gdown_ref, gsmall_ref,
     slabs, downs, smalls, gsmalls, weights, w_up,
     row_c, row_d, row_n, row_z, late_d, late_n, late_z, down_c, down_d, down_n, down_z, sm_c, sm_d, sm_n, sm_z,
     qkv, n1t, n1, att_t, middle, n2, n2t, g2, acc_out, acc_grad, act, grad_h, pre, grad_act,
-    tok, cot, bias, lse, dq_t, vec24, vec48, vec96, merged_bias, group_sums, sums, up_sums,
-    ag_send, ag_recv, rs_send, rs_recv, local,
+    tok, cot, bias, lse, dq_t, vec24, vec48, vec96, merged_bias, group_sums, sums, up_sums, gqkv, gout, gup, gdown, gsmall,
+    sends, ag_recv, rs_recv, local,
 ):
     n_z, width = slabs.shape[1], slabs.shape[-1]
     count = tok.shape[0]
@@ -389,12 +431,15 @@
     along_z = [device(at, x, core, y) for at in z_places]
     other_pair = pl.ds(2 * (1 - lax.div(z, 2)), 2)
     inner = lax.rem(z + 1, n_z) >= 2
-    Z0, Z1, Z2, ZR, X0, Y0, X1, Y1, X2, Y2, DX, DY, C0 = range(13)
-
-    def remote(src, dst, sems, row, sem, to, recv_sem=None):
-        send, recv = sems
+
+    ag_slots, rs_slots, _, _ = semaphore_slots()
+
+    def remote(src, dst, sums, unit_name, sem, to, recv_sem=None):
+        slots = rs_slots if sums else ag_slots
+        recv = rs_recv if sums else ag_recv
         return pltpu.make_async_remote_copy(
-            src_ref=src, dst_ref=dst, send_sem=send.at[row, sem], recv_sem=recv.at[row, sem if recv_sem is None else recv_sem],
+            src_ref=src, dst_ref=dst, send_sem=sends.at[slots[unit_name, sem]],
+            recv_sem=recv.at[slots[unit_name, sem if recv_sem is None else recv_sem]],
             device_id=to, device_id_type=MESH,
         )
 
@@ -406,7 +451,7 @@
 
     def ag_copies(unit, phase):
         view, row, phases, along = unit
-        sems = (ag_send, ag_recv)
+        sems = False
         held = z if along is plane else ALL
 
         def both(at, sem):
@@ -486,26 +531,20 @@
                 def _():
                     do_all(ag_copies(unit, "z last") + ag_copies(unit, "relay"), "wait_send")
 
-    ORDERS = {
-        "plain": ("z", "relay", "near", "across", "core"), "direct": ("zd", "near", "across", "core"),
-        "boot": ("own", "zd", "pair", "rest", "across", "core"),
-        "late": ("near", "across", "z", "relay", "core"), "late direct": ("near", "across", "zd", "core"),
-    }
-
-    def gather_unit(block, kind):
-        return (row_view(block), 1 + block, ORDERS[kind], plane if kind[:4] == "late" else one)
-
-    units = {"aS": (small_view(smalls), 0, ORDERS["direct"], one)}
-    units["adp"] = (lambda at: downs.at[at], 5 + 2 * n_z, ("z", "relay") if KINDS.get("adp", "plain") == "plain" else ("zd",), one)
+    def gather_unit(name, view):
+        kind = KINDS.get(name, "plain")
+        return (view, name, phases_of(name), plane if kind[:4] == "late" else one)
+
+    units = {"aS": gather_unit("aS", small_view(smalls)), "adp": gather_unit("adp", lambda at: downs.at[at])}
     for block in range(4):
-        units[f"ab{block}"] = gather_unit(block, KINDS.get(f"ab{block}", "plain"))
+        units[f"ab{block}"] = gather_unit(f"ab{block}", row_view(block))
     for tile in range(n_z):
-        units[f"au{tile}"] = gather_unit(4 + tile, KINDS.get(f"au{tile}", "plain"))
-        units[f"ad{tile}"] = (down_view(tile), 5 + n_z + tile, ("near", "across", "core"), one)
+        units[f"au{tile}"] = gather_unit(f"au{tile}", row_view(4 + tile))
+        units[f"ad{tile}"] = gather_unit(f"ad{tile}", down_view(tile))
 
     def rs_copies(unit, phase):
         view, row, phases, landing, along = unit
-        sems = (rs_send, rs_recv)
+        sems = True
         held = z if along is plane else ALL
         if phase == "core":
             return [remote(view((ALL, ALL, 1 - core, ALL)), landing["core"], sems, row, C0, to_c)]
@@ -626,40 +665,39 @@
             def _():
                 do_all(rs_copies(unit, "z outer"), "wait_send")
 
-    BACK = {
-        "plain": ("core", "across", "near", "z", "z far"), "direct": ("core", "across", "near", "zd"),
-        "late": ("core", "z", "z far", "across", "near"), "late direct": ("core", "zd", "across", "near"),
-    }
-
-    def row_unit(block, row, name):
+    def row_unit(block, name):
         if name in LATE_SUMS:
             late = LATE_SUMS.index(name)
             landing = {"core": row_c.at[block], "dx": late_d.at[late, 0], "dy": late_d.at[late, 1], "x": late_n.at[late, 0], "y": late_n.at[late, 1], "z": late_z.at[late]}
-            return (row_view(block), row, BACK[KINDS[name]], landing, plane)
+            return (row_view(block), name, phases_of(name), landing, plane)
         at = block - sum(earlier in LATE_SUMS for earlier in ROW_SUMS[:block])
         landing = {"core": row_c.at[block], "dx": row_d.at[at, 0], "dy": row_d.at[at, 1], "x": row_n.at[at, 0], "y": row_n.at[at, 1], "z": row_z.at[at]}
-        return (row_view(block), row, BACK[KINDS.get(name, "plain")], landing, one)
-
-    def down_unit(tile, row):
+        return (row_view(block), name, phases_of(name), landing, one)
+
+    def down_unit(tile, name):
         landing = {"core": down_c.at[tile], "dx": down_d.at[tile, 0], "dy": down_d.at[tile, 1], "x": down_n.at[tile, 0], "y": down_n.at[tile, 1]}
-        return (down_view(tile), row, BACK["plain"][:3], landing, one)
+        return (down_view(tile), name, phases_of(name), landing, one)
 
     def block_columns(block):
         return pl.ds(block * width, width)
 
     third = width // 3
-    results = {"rdl": [gdown_ref], "ro": [gout_ref], "rS": [gsmall_ref]}
+    results = {"rdl": [gdown], "ro": [gout], "rS": [gsmall]}
     for t in range(n_z):
-        units[f"ru{t}"] = row_unit(4 + t, t, f"ru{t}")
-        units[f"rd{t}"] = down_unit(t, n_z + t)
-        results[f"ru{t}"] = [gup_ref.at[:, block_columns(t)]]
+        units[f"ru{t}"] = row_unit(4 + t, f"ru{t}")
+        units[f"rd{t}"] = down_unit(t, f"rd{t}")
+        results[f"ru{t}"] = [gup.at[:, block_columns(t)]]
     for g in range(3):
-        units[f"rh{g}"] = row_unit(g, 2 * n_z + g, f"rh{g}")
-        results[f"rh{g}"] = [gqkv_ref.at[:, pl.ds(j * width + g * third, third)] for j in range(3)]
-    units["ro"] = row_unit(3, 2 * n_z + 3, "ro")
+        units[f"rh{g}"] = row_unit(g, f"rh{g}")
+        results[f"rh{g}"] = [gqkv.at[:, pl.ds(j * width + g * third, third)] for j in range(3)]
+    units["ro"] = row_unit(3, "ro")
     small_landing = {"core": sm_c, "dx": sm_d, "x": sm_n.at[0], "y": sm_n.at[1], "z": sm_z}
-    units["rS"] = (small_view(gsmalls), 2 * n_z + 4, BACK["direct"], small_landing, one)
-    units["rdl"] = (lambda at: downs.at[at], 2 * n_z + 5, ("z", "z far") if KINDS.get("rdl", "plain") == "plain" else ("zd",), {"z": down_z}, one)
+    units["rS"] = (small_view(gsmalls), "rS", phases_of("rS"), small_landing, one)
+    units["rdl"] = (lambda at: downs.at[at], "rdl", phases_of("rdl"), {"z": down_z}, one)
+    last_copies = [
+        pltpu.make_async_copy(src, dst, local.at[2 + k])
+        for k, (src, dst) in enumerate(((gup, gup_ref), (gdown, gdown_ref), (gout, gout_ref), (gqkv, gqkv_ref), (gsmall, gsmall_ref)))
+    ]
 
     def point(name):
         for unit_name, stage in TABLE.get(name, ()):
@@ -1022,11 +1060,13 @@
         gsmalls[k] = gsmalls[k] + gather_back(up_sums[k], 96).reshape(2, 2, 2, 8, 128)
 
     point("end")
+    do_all(last_copies, "start")
     for name, unit in units.items():
         if name[0] == "r":
             rs_sent(unit)
     out_copy.wait()
     tgrad_copy.wait()
+    do_all(last_copies, "wait")
 
 
 def by_kernel(
@@ -1086,10 +1126,14 @@
         vmem((3, 8, width), F32),
         vmem((3, 8, width), F32),
         vmem((n_z, 8, width), F32),
-        dma((6 + 2 * n_z, 13)),
-        dma((6 + 2 * n_z, 13)),
-        dma((6 + 2 * n_z, 13)),
-        dma((6 + 2 * n_z, 13)),
+        vmem(qkv_weight.shape, F32),
+        vmem(out_weight.shape, F32),
+        vmem(up_weight.shape, F32),
+        vmem(down_weight.shape, F32),
+        vmem((8, 128), F32),
+        dma((semaphore_slots()[2],)),
+        dma((len(semaphore_slots()[0]),)),
+        dma((len(semaphore_slots()[1]),)),
         dma((13 + n_z,)),
     ]
     anywhere, whole = pl.BlockSpec(memory_space=pl.ANY), pl.BlockSpec(memory_space=pltpu.VMEM)
@@ -1106,7 +1150,7 @@
             shape((8, 128), F32),
         ),
         in_specs=[pl.BlockSpec(memory_space=pltpu.SMEM)] + [anywhere] * 2 + [whole] * 8 + [anywhere] * 4,
-        out_specs=(anywhere, anywhere, whole, whole, whole, whole, whole),
+        out_specs=(anywhere,) * 7,
         scratch_shapes=held,
         compiler_params=pltpu.CompilerParams(collective_id=0, has_side_effects=True, vmem_limit_bytes=VMEM_BYTES),
     )(clip_lengths, tokens, cotangent, *vectors, qkv_weight, out_weight, up_weight, down_weight)
@@ -1114,27 +1158,40 @@
     done = pl.pallas_call(
         hand_over,
         out_shape=tuple(shape(a.shape, a.dtype) for a in large) + tuple(shape(v.shape, F32) for v in vectors),
-        in_specs=[whole] + [anywhere] * len(large),
-        out_specs=(anywhere,) * len(large) + (whole,) * len(vectors),
-        scratch_shapes=[vmem(a.shape, a.dtype) for a in large] + [dma((2, len(large)))],
+        in_specs=[anywhere] * (1 + len(large)),
+        out_specs=(anywhere,) * (len(large) + len(vectors)),
+        scratch_shapes=[vmem(a.shape, a.dtype) for a in (g_small, *large)] + [vmem(v.shape, F32) for v in vectors] + [dma((2, 24))],
     )(g_small, *large)
     out, grad, g_qkv, g_out, g_up, g_down = done[:6]
     parts = done[6:]
     return (out, grad, parts[0], parts[1], g_qkv, parts[2], g_out, parts[3], parts[4], parts[5], g_up, parts[6], g_down, parts[7])
 
 
-def hand_over(small_ref, *refs):
-    sources, targets, vectors, held, sems = refs[:6], refs[6:12], refs[12:20], refs[20:26], refs[26]
-    inward = [pltpu.make_async_copy(src, dst, sems.at[0, k]) for k, (src, dst) in enumerate(zip(sources, held))]
-    outward = [pltpu.make_async_copy(src, dst, sems.at[1, k]) for k, (src, dst) in enumerate(zip(held, targets))]
+def hand_over(*refs):
+    small_ref, sources, targets, vectors = refs[0], refs[1:7], refs[7:13], refs[13:21]
+    small, held, cut, sems = refs[21], refs[22:28], refs[28:36], refs[36]
+    small_copy = pltpu.make_async_copy(small_ref, small, sems.at[0, 23])
+    small_copy.start()
+    pieces = []
+    for src, mid, dst in zip(sources, held, targets):
+        rows = src.shape[0]
+        parts = 4 if rows % 64 == 0 else 1
+        for k in range(parts):
+            pieces.append([ref.at[pl.ds(k * (rows // parts), rows // parts)] for ref in (src, mid, dst)])
+    inward = [pltpu.make_async_copy(src, mid, sems.at[0, k]) for k, (src, mid, _) in enumerate(pieces)]
+    outward = [pltpu.make_async_copy(mid, dst, sems.at[1, k]) for k, (_, mid, dst) in enumerate(pieces)]
     for copy in inward:
         copy.start()
-    for k, vector in enumerate(vectors):
-        vector[...] = small_ref[k, 0 : vector.shape[0]]
+    small_copy.wait()
+    cuts = []
+    for k, (part, vector) in enumerate(zip(cut, vectors)):
+        part[...] = small[k, 0 : part.shape[0]]
+        cuts.append(pltpu.make_async_copy(part, vector, sems.at[1, 15 + k]))
+        cuts[-1].start()
     for arrived, onward in zip(inward, outward):
         arrived.wait()
         onward.start()
-    for copy in outward:
+    for copy in outward + cuts:
         copy.wait()
 
 

time: 134 us -> 129 us (0.963)
  Pallas kernels: 133 us -> 128 us
    pallas_call x1, Pallas kernels: 129 us -> 125 us  [by_kernel(): pl.pallas_call(layer_kernel, out_shape=(shape((count, width), BF16), shap...]
where the time goes in v5:
time: 129 us
  Pallas kernels  128 us (99%)
    pallas_call x1, Pallas kernels, by_kernel(): pl.pallas_call(layer_kernel, out_shape=(shape((count, width), BF16), shap...  125 us
    pallas_call x1, Pallas kernels, by_kernel(): pl.pallas_call(hand_over, out_shape=tuple((shape(a.shape, a.dtype) for a...  3.42 us

profile of v5, /device:TPU:0, one launch (start us, length us, event | category | flops | bytes accessed | tf_op | source)
XLA Modules:
  0.0 129.2 jit_solution(9764388416854691800)
XLA Ops:
  0.7 125.0 %shard_map.254 = (bf16[512,768]{1,0:T(8,128)(2,1)}, f32[512,768]{1,0:T(8,128)}, f32[24,2304]{1,0:T(8,128)}, f32[24,768]{1,0:T(8,128)}, f32[24,3072]{1,0:T(8,128)}, /*index=5*/f32[96,768]{1,0:T(8,128)}, f32[8,128]{1,0:T(8,128)}) custom-call(s32[1,3]{1,0:T(1,128)} %clip_ref.1, bf16[512,768]{1,0:T(8,128)(2,1)} %tok_ref.1, bf16[512,768]{1,0:T(8,128)(2,1)} %cot_ref.1, ...), custom_call_target="tpu_custom_call" | custom-call | tf_op jit(solution)/shard_map/pallas_call | solution.py:1141
  125.7 3.4 %shard_map.255 = (bf16[512,768]{1,0:T(8,128)(2,1)}, f32[512,768]{1,0:T(8,128)}, f32[24,2304]{1,0:T(8,128)}, f32[24,768]{1,0:T(8,128)}, f32[24,3072]{1,0:T(8,128)...) custom-call(f32[8,128]{1,0:T(8,128)} %get-tuple-element.35.refs_0_, ...), custom_call_target="tpu_custom_call" | custom-call | tf_op jit(solution)/shard_map/pallas_call | solution.py:1158

commit v6 on v5

--- a/solution.py
+++ b/solution.py
@@ -694,10 +694,12 @@
     small_landing = {"core": sm_c, "dx": sm_d, "x": sm_n.at[0], "y": sm_n.at[1], "z": sm_z}
     units["rS"] = (small_view(gsmalls), "rS", phases_of("rS"), small_landing, one)
     units["rdl"] = (lambda at: downs.at[at], "rdl", phases_of("rdl"), {"z": down_z}, one)
-    last_copies = [
-        pltpu.make_async_copy(src, dst, local.at[2 + k])
-        for k, (src, dst) in enumerate(((gup, gup_ref), (gdown, gdown_ref), (gout, gout_ref), (gqkv, gqkv_ref), (gsmall, gsmall_ref)))
-    ]
+    whole_results = {"rdl": [gdown_ref], "ro": [gout_ref], "rS": [gsmall_ref]}
+    for t in range(n_z):
+        whole_results[f"ru{t}"] = [gup_ref.at[:, block_columns(t)]]
+    for g in range(3):
+        whole_results[f"rh{g}"] = [gqkv_ref.at[:, pl.ds(j * width + g * third, third)] for j in range(3)]
+    last_copies = []
 
     def point(name):
         for unit_name, stage in TABLE.get(name, ()):
@@ -706,6 +708,9 @@
                 ag_stage(unit, stage)
             elif unit_name in results and stage == len(unit[2]):
                 rs_end(unit, *results[unit_name])
+                for src, dst in zip(results[unit_name], whole_results[unit_name]):
+                    last_copies.append(pltpu.make_async_copy(src, dst, local.at[2 + len(last_copies)]))
+                    last_copies[-1].start()
             else:
                 rs_stage(unit, stage)
 
@@ -1060,7 +1065,6 @@
         gsmalls[k] = gsmalls[k] + gather_back(up_sums[k], 96).reshape(2, 2, 2, 8, 128)
 
     point("end")
-    do_all(last_copies, "start")
     for name, unit in units.items():
         if name[0] == "r":
             rs_sent(unit)
@@ -1134,7 +1138,7 @@
         dma((semaphore_slots()[2],)),
         dma((len(semaphore_slots()[0]),)),
         dma((len(semaphore_slots()[1]),)),
-        dma((13 + n_z,)),
+        dma((16 + n_z,)),
     ]
     anywhere, whole = pl.BlockSpec(memory_space=pl.ANY), pl.BlockSpec(memory_space=pltpu.VMEM)
     shape = jax.ShapeDtypeStruct
@@ -1196,67 +1200,67 @@
 
 
 KINDS = {
-    "ab0": "boot",
     "ab1": "boot",
     "ab2": "boot",
-    "ab3": "boot",
-    "au0": "late",
-    "au1": "boot",
-    "au2": "boot",
-    "au3": "late",
-    "ro": "direct",
+    "au0": "direct",
+    "au1": "late",
+    "au2": "late",
+    "au3": "boot",
+    "ro": "late",
     "ru0": "late",
-    "ru1": "late",
-    "ru3": "late",
+    "ru2": "late",
 }
-LATE_SUMS = ("ru0", "ru1", "ru3")
+LATE_SUMS = ("ro", "ru0", "ru2")
 TABLE = {
-    "mask": (("aS", 0), ("ab0", 0), ("ab0", 1), ("au1", 0), ("ab3", 0),),
-    "vec": (("au1", 1), ("ab2", 0), ("ab1", 0), ("au2", 0), ("aS", 1), ("ab0", 2), ("ab3", 1), ("au3", 0), ("ab0", 3), ("aS", 2), ("au1", 2), ("ab1", 1), ("au0", 0), ("au3", 1), ("au1", 3), ("aS", 3), ("ab0", 4), ("ab2", 1), ("aS", 4),),
-    "turn": (("au0", 1), ("ab3", 2),),
-    "q0": (("ab3", 3), ("adp", 0), ("au1", 4), ("ab0", 5), ("ab2", 2), ("ab0", 6), ("ab1", 2),),
-    "t0": (("ab1", 3),),
-    "q1": (("au1", 5), ("ab3", 4), ("ab2", 3), ("au1", 6), ("adp", 1), ("au0", 2), ("ab1", 4), ("ab3", 5), ("ab3", 6), ("ab2", 4), ("ab1", 5), ("adp", 2), ("ad0", 0), ("ab1", 6),),
-    "t2": (("ab2", 5), ("ad1", 0),),
-    "t3": (("au0", 3), ("ab2", 6),),
-    "q2": (("ad2", 0), ("au2", 1),),
-    "tb": (("ad0", 1), ("au3", 2),),
-    "n2a": (("au0", 4), ("ad1", 1),),
-    "fa0": (("au0", 5), ("ad2", 1),),
-    "fc0": (("au2", 2), ("ad0", 2), ("au2", 3), ("ad0", 3), ("ad1", 2),),
-    "ff0": (("ad2", 2), ("ad3", 0), ("ad1", 3), ("au3", 3),),
-    "fi0": (("ru0", 0), ("ad2", 3), ("au2", 4),),
+    "mask": (("au0", 0), ("ab1", 0), ("au2", 0), ("ab2", 0),),
+    "vec": (("ab0", 0), ("au3", 0), ("aS", 0), ("ab1", 1), ("au2", 1), ("ab3", 0), ("au0", 1), ("ab0", 1), ("ab2", 1), ("aS", 1), ("ab1", 2), ("adp", 0), ("au0", 2), ("au1", 0), ("aS", 2), ("ab1", 3), ("ab3", 1), ("ab0", 2), ("au0", 3), ("aS", 3), ("au1", 1), ("au0", 4), ("ab2", 2), ("aS", 4),),
+    "turn": (("ab1", 4),),
+    "q0": (("ab2", 3), ("adp", 1), ("au1", 2), ("ab0", 3), ("ab1", 5), ("ab3", 2), ("ab1", 6), ("ab2", 4), ("ab0", 4), ("adp", 2), ("ad0", 0), ("ab0", 5),),
+    "t1": (("ab3", 3), ("au1", 3), ("au3", 1),),
+    "q1": (("ad1", 0), ("ab2", 5),),
+    "q2": (("ad0", 1), ("au2", 2), ("ab2", 6),),
+    "t4": (("ab3", 4), ("au1", 4),),
+    "t5": (("ad2", 0),),
+    "tb": (("ab3", 5),),
+    "n2a": (("au1", 5), ("ad1", 1),),
+    "n2b": (("ad0", 2),),
+    "fa0": (("au3", 2),),
+    "fc0": (("au3", 3), ("ad0", 3),),
+    "fe0": (("ad2", 1),),
+    "ff0": (("au2", 3),),
+    "fg0": (("ad1", 2), ("ad3", 0),),
+    "fi0": (("ru0", 0),),
     "fa1": (("rd0", 0),),
-    "fc1": (("ru0", 1),),
-    "fe1": (("rd0", 1), ("ad3", 1),),
-    "ff1": (("au3", 4),),
-    "fg1": (("au2", 5),),
-    "fi1": (("ru1", 0), ("au3", 5),),
-    "fa2": (("rd1", 0), ("au2", 6), ("rd0", 2), ("ru0", 2),),
-    "fe2": (("rd1", 1), ("ad3", 2),),
-    "fg2": (("ad3", 3),),
-    "fi2": (("ru2", 0), ("ru1", 1),),
-    "fa3": (("rd0", 3), ("rd2", 0),),
-    "fb3": (("ru2", 1),),
-    "fc3": (("rd1", 2),),
-    "fg3": (("rd2", 1), ("ru1", 2),),
-    "fi3": (("ru2", 2), ("ru3", 0),),
+    "fc1": (("ad1", 3),),
+    "fe1": (("au3", 4),),
+    "ff1": (("ru0", 1), ("ad2", 2),),
+    "fg1": (("rd0", 1), ("au2", 4),),
+    "fi1": (("ru1", 0),),
+    "fa2": (("rd1", 0), ("ad2", 3), ("ad3", 1), ("au2", 5),),
+    "fc2": (("au3", 5),),
+    "fe2": (("ru1", 1), ("ru0", 2), ("rd0", 2),),
+    "fg2": (("ad3", 2),),
+    "fi2": (("ru2", 0), ("au3", 6),),
+    "fa3": (("rd1", 1), ("rd2", 0),),
+    "fc3": (("ad3", 3),),
+    "fe3": (("ru1", 2), ("ru2", 1),),
+    "fg3": (("rd0", 3),),
+    "fi3": (("ru3", 0), ("rd2", 1),),
     "ba": (("rd3", 0),),
-    "og": (("rd1", 3),),
-    "ga": (("rd3", 1), ("ro", 0), ("ru3", 1),),
-    "a0": (("rd2", 2),),
-    "H0": (("ru2", 3), ("ru1", 3), ("rd3", 2), ("ru3", 2),),
-    "a2": (("rh0", 0),),
-    "a3": (("rh0", 1), ("rd2", 3), ("ru1", 4),),
-    "H1": (("ru2", 4), ("rd3", 3), ("ro", 1), ("ru0", 3),),
-    "a4": (("rdl", 0), ("rh0", 2), ("rh1", 0),),
-    "a5": (("rh1", 1),),
-    "H2": (("ro", 2), ("rdl", 1),),
-    "g2": (("rh2", 0),),
-    "g0": (("rh2", 1),),
-    "na": (("rh1", 2),),
-    "nb": (("rh0", 3),),
-    "end": (("ru2", 5), ("ru1", 5), ("rS", 0), ("rh0", 4), ("rh2", 2), ("ro", 3), ("rdl", 2), ("rS", 1), ("ru0", 4), ("rh1", 3), ("ru3", 3), ("rh0", 5), ("rh1", 4), ("rh2", 3), ("rS", 2), ("ru0", 5), ("ru3", 4), ("ro", 4), ("rS", 3), ("rh2", 4), ("rh1", 5), ("ru3", 5), ("rS", 4), ("rh2", 5),),
+    "bb": (("rd1", 2),),
+    "ga": (("ro", 0), ("ru2", 2),),
+    "a1": (("ru3", 1), ("rd3", 1), ("ro", 1),),
+    "H0": (("rd1", 3), ("rd2", 2),),
+    "a2": (("ru1", 3), ("rh0", 0),),
+    "a3": (("ro", 2), ("ru3", 2),),
+    "H1": (("rd3", 2),),
+    "a4": (("rh1", 0), ("rd2", 3),),
+    "a5": (("rh1", 1), ("ru3", 3),),
+    "H2": (("ru1", 4), ("rh0", 1), ("ru0", 3),),
+    "g2": (("rh2", 0), ("ru3", 4), ("rd3", 3), ("rdl", 0), ("ru2", 3),),
+    "g0": (("rh1", 2),),
+    "nb": (("rh2", 1),),
+    "end": (("ro", 3), ("rS", 0), ("ru1", 5), ("rdl", 1), ("ru3", 5), ("rh0", 2), ("rS", 1), ("ru0", 4), ("rh2", 2), ("rh1", 3), ("rh0", 3), ("ro", 4), ("rS", 2), ("rh1", 4), ("ru0", 5), ("ru2", 4), ("rh0", 4), ("rdl", 2), ("rh2", 3), ("ro", 5), ("rS", 3), ("ru2", 5), ("rh1", 5), ("rh2", 4), ("rh0", 5), ("rS", 4), ("rh2", 5),),
 }
 
 ROW_SUMS = ("rh0", "rh1", "rh2", "ro", "ru0", "ru1", "ru2", "ru3")

time: 129 us -> 128 us (level)
  no operation moved by 1% of the time
where the time goes in v6:
time: 128 us
  Pallas kernels  127 us (99%)
    pallas_call x1, Pallas kernels, by_kernel(): pl.pallas_call(layer_kernel, out_shape=(shape((count, width), BF16), shap...  124 us
    pallas_call x1, Pallas kernels, by_kernel(): pl.pallas_call(hand_over, out_shape=tuple((shape(a.shape, a.dtype) for a...  3.42 us

profile of v6, /device:TPU:0, one launch (start us, length us, event | category | flops | bytes accessed | tf_op | source)
XLA Modules:
  0.0 128.1 jit_solution(6359665040557426044)
XLA Ops:
  0.7 123.9 %shard_map.254 = (bf16[512,768]{1,0:T(8,128)(2,1)}, f32[512,768]{1,0:T(8,128)}, f32[24,2304]{1,0:T(8,128)}, f32[24,768]{1,0:T(8,128)}, f32[24,3072]{1,0:T(8,128)}, /*index=5*/f32[96,768]{1,0:T(8,128)}, f32[8,128]{1,0:T(8,128)}) custom-call(s32[1,3]{1,0:T(1,128)} %clip_ref.1, bf16[512,768]{1,0:T(8,128)(2,1)} %tok_ref.1, bf16[512,768]{1,0:T(8,128)(2,1)} %cot_ref.1, ...), custom_call_target="tpu_custom_call" | custom-call | tf_op jit(solution)/shard_map/pallas_call | solution.py:1145
  124.5 3.4 %shard_map.255 = (bf16[512,768]{1,0:T(8,128)(2,1)}, f32[512,768]{1,0:T(8,128)}, f32[24,2304]{1,0:T(8,128)}, f32[24,768]{1,0:T(8,128)}, f32[24,3072]{1,0:T(8,128)...) custom-call(f32[8,128]{1,0:T(8,128)} %get-tuple-element.35.refs_0_, ...), custom_call_target="tpu_custom_call" | custom-call | tf_op jit(solution)/shard_map/pallas_call | solution.py:1162

commit v7 on v6

--- a/solution.py
+++ b/solution.py
@@ -15,6 +15,28 @@
 BF16 = jnp.bfloat16
 ALL = slice(None)
 CHUNK = 256
+BOTH_AXES = ("wide", "narrow")
+ACROSS = "across"
+Z_FAR = "z far"
+CORE = "core"
+Z_LAST = "z last"
+NEAR = "near"
+RELAY = "relay"
+WAIT_SEND = "wait_send"
+WAIT_RECV = "wait_recv"
+START = "start"
+LATE = "late"
+PLAIN = "plain"
+Z_OUTER = "z outer"
+Z_NEAR = "z near"
+DIRECT = "direct"
+Z_ALL = "zd"
+LATE_DIRECT = "late direct"
+REST = "rest"
+PAIR = "pair"
+OWN = "own"
+BOOT = "boot"
+Z_TWO = "z"
 
 
 def layer_norm(inputs, ln_gain, ln_bias):
@@ -119,18 +141,18 @@
     down_bias,
 ):
     gathered = (
-        lax.all_gather(ln1_gain, ("wide", "narrow"), axis=0, tiled=True),
-        lax.all_gather(ln1_bias, ("wide", "narrow"), axis=0, tiled=True),
-        lax.all_gather(qkv_weight, ("wide", "narrow"), axis=0, tiled=True),
-        lax.all_gather(qv_bias, ("wide", "narrow"), axis=0, tiled=True),
-        lax.all_gather(out_weight, ("wide", "narrow"), axis=0, tiled=True),
-        lax.all_gather(out_bias, ("wide", "narrow"), axis=0, tiled=True),
-        lax.all_gather(ln2_gain, ("wide", "narrow"), axis=0, tiled=True),
-        lax.all_gather(ln2_bias, ("wide", "narrow"), axis=0, tiled=True),
-        lax.all_gather(up_weight, ("wide", "narrow"), axis=0, tiled=True),
-        lax.all_gather(up_bias, ("wide", "narrow"), axis=0, tiled=True),
-        lax.all_gather(down_weight, ("wide", "narrow"), axis=0, tiled=True),
-        lax.all_gather(down_bias, ("wide", "narrow"), axis=0, tiled=True),
+        lax.all_gather(ln1_gain, BOTH_AXES, axis=0, tiled=True),
+        lax.all_gather(ln1_bias, BOTH_AXES, axis=0, tiled=True),
+        lax.all_gather(qkv_weight, BOTH_AXES, axis=0, tiled=True),
+        lax.all_gather(qv_bias, BOTH_AXES, axis=0, tiled=True),
+        lax.all_gather(out_weight, BOTH_AXES, axis=0, tiled=True),
+        lax.all_gather(out_bias, BOTH_AXES, axis=0, tiled=True),
+        lax.all_gather(ln2_gain, BOTH_AXES, axis=0, tiled=True),
+        lax.all_gather(ln2_bias, BOTH_AXES, axis=0, tiled=True),
+        lax.all_gather(up_weight, BOTH_AXES, axis=0, tiled=True),
+        lax.all_gather(up_bias, BOTH_AXES, axis=0, tiled=True),
+        lax.all_gather(down_weight, BOTH_AXES, axis=0, tiled=True),
+        lax.all_gather(down_bias, BOTH_AXES, axis=0, tiled=True),
     )
     (
         gain_one,
@@ -190,12 +212,12 @@
     )
     block_out = (middle + live_rows * branch_two).astype(jnp.bfloat16)
     back_gain_one, back_merged, back_proj, back_gain_two, back_up, back_down = (
-        lax.all_gather(ln1_gain, ("wide", "narrow"), axis=0, tiled=True),
-        lax.all_gather(qkv_weight, ("wide", "narrow"), axis=0, tiled=True),
-        lax.all_gather(out_weight, ("wide", "narrow"), axis=0, tiled=True),
-        lax.all_gather(ln2_gain, ("wide", "narrow"), axis=0, tiled=True),
-        lax.all_gather(up_weight, ("wide", "narrow"), axis=0, tiled=True),
-        lax.all_gather(down_weight, ("wide", "narrow"), axis=0, tiled=True),
+        lax.all_gather(ln1_gain, BOTH_AXES, axis=0, tiled=True),
+        lax.all_gather(qkv_weight, BOTH_AXES, axis=0, tiled=True),
+        lax.all_gather(out_weight, BOTH_AXES, axis=0, tiled=True),
+        lax.all_gather(ln2_gain, BOTH_AXES, axis=0, tiled=True),
+        lax.all_gather(up_weight, BOTH_AXES, axis=0, tiled=True),
+        lax.all_gather(down_weight, BOTH_AXES, axis=0, tiled=True),
     )
     upstream = cotangent.astype(jnp.float32)
     grad_two = (live_rows * upstream).astype(jnp.bfloat16)
@@ -253,18 +275,18 @@
     grad_input_norm, grad_gain_one, grad_bias_one = norm_pull_one(grad_normed_one)
     tokens_grad = grad_middle + grad_input_norm
     shares = (
-        lax.psum_scatter(grad_gain_one, ("wide", "narrow"), scatter_dimension=0, tiled=True),
-        lax.psum_scatter(grad_bias_one, ("wide", "narrow"), scatter_dimension=0, tiled=True),
-        lax.psum_scatter(grad_w_merged, ("wide", "narrow"), scatter_dimension=0, tiled=True),
-        lax.psum_scatter(grad_merged_bias, ("wide", "narrow"), scatter_dimension=0, tiled=True),
-        lax.psum_scatter(grad_w_proj, ("wide", "narrow"), scatter_dimension=0, tiled=True),
-        lax.psum_scatter(grad_b_proj, ("wide", "narrow"), scatter_dimension=0, tiled=True),
-        lax.psum_scatter(grad_gain_two, ("wide", "narrow"), scatter_dimension=0, tiled=True),
-        lax.psum_scatter(grad_bias_two, ("wide", "narrow"), scatter_dimension=0, tiled=True),
-        lax.psum_scatter(grad_w_up, ("wide", "narrow"), scatter_dimension=0, tiled=True),
-        lax.psum_scatter(grad_b_up, ("wide", "narrow"), scatter_dimension=0, tiled=True),
-        lax.psum_scatter(grad_w_down, ("wide", "narrow"), scatter_dimension=0, tiled=True),
-        lax.psum_scatter(grad_b_down, ("wide", "narrow"), scatter_dimension=0, tiled=True),
+        lax.psum_scatter(grad_gain_one, BOTH_AXES, scatter_dimension=0, tiled=True),
+        lax.psum_scatter(grad_bias_one, BOTH_AXES, scatter_dimension=0, tiled=True),
+        lax.psum_scatter(grad_w_merged, BOTH_AXES, scatter_dimension=0, tiled=True),
+        lax.psum_scatter(grad_merged_bias, BOTH_AXES, scatter_dimension=0, tiled=True),
+        lax.psum_scatter(grad_w_proj, BOTH_AXES, scatter_dimension=0, tiled=True),
+        lax.psum_scatter(grad_b_proj, BOTH_AXES, scatter_dimension=0, tiled=True),
+        lax.psum_scatter(grad_gain_two, BOTH_AXES, scatter_dimension=0, tiled=True),
+        lax.psum_scatter(grad_bias_two, BOTH_AXES, scatter_dimension=0, tiled=True),
+        lax.psum_scatter(grad_w_up, BOTH_AXES, scatter_dimension=0, tiled=True),
+        lax.psum_scatter(grad_b_up, BOTH_AXES, scatter_dimension=0, tiled=True),
+        lax.psum_scatter(grad_w_down, BOTH_AXES, scatter_dimension=0, tiled=True),
+        lax.psum_scatter(grad_b_down, BOTH_AXES, scatter_dimension=0, tiled=True),
     )
     return (
         block_out,
@@ -344,36 +366,36 @@
 
 Z0, Z1, Z2, ZR, X0, Y0, X1, Y1, X2, Y2, DX, DY, C0 = range(13)
 ORDERS = {
-    "plain": ("z", "relay", "near", "across", "core"),
-    "direct": ("zd", "near", "across", "core"),
-    "boot": ("own", "zd", "pair", "rest", "across", "core"),
-    "late": ("near", "across", "z", "relay", "core"),
-    "late direct": ("near", "across", "zd", "core"),
+    PLAIN: (Z_TWO, RELAY, NEAR, ACROSS, CORE),
+    DIRECT: (Z_ALL, NEAR, ACROSS, CORE),
+    BOOT: (OWN, Z_ALL, PAIR, REST, ACROSS, CORE),
+    LATE: (NEAR, ACROSS, Z_TWO, RELAY, CORE),
+    LATE_DIRECT: (NEAR, ACROSS, Z_ALL, CORE),
 }
 BACK = {
-    "plain": ("core", "across", "near", "z", "z far"),
-    "direct": ("core", "across", "near", "zd"),
-    "late": ("core", "z", "z far", "across", "near"),
-    "late direct": ("core", "zd", "across", "near"),
+    PLAIN: (CORE, ACROSS, NEAR, Z_TWO, Z_FAR),
+    DIRECT: (CORE, ACROSS, NEAR, Z_ALL),
+    LATE: (CORE, Z_TWO, Z_FAR, ACROSS, NEAR),
+    LATE_DIRECT: (CORE, Z_ALL, ACROSS, NEAR),
 }
 
 
 def phases_of(name):
-    kind = "direct" if name[1:] == "S" else KINDS.get(name, "plain")
+    kind = DIRECT if name[1:] == "S" else KINDS.get(name, PLAIN)
     if name[:2] == "ad":
-        return (("z", "relay") if kind == "plain" else ("zd",)) if name == "adp" else ("near", "across", "core")
+        return ((Z_TWO, RELAY) if kind == PLAIN else (Z_ALL,)) if name == "adp" else (NEAR, ACROSS, CORE)
     if name[:2] == "rd":
-        return (("z", "z far") if kind == "plain" else ("zd",)) if name == "rdl" else ("core", "across", "near")
+        return ((Z_TWO, Z_FAR) if kind == PLAIN else (Z_ALL,)) if name == "rdl" else (CORE, ACROSS, NEAR)
     return (ORDERS if name[0] == "a" else BACK)[kind]
 
 
 def semaphore_slots():
     used = {
-        "z": (Z0, Z1, Z2), "relay": (ZR,), "zd": (Z0, Z1, Z2), "own": (X1, Y1), "pair": (X2, Y2), "rest": (X0, Y0),
-        "near": (X0, Y0), "across": (DX, DY), "core": (C0,), "z far": (ZR, Z1),
+        Z_TWO: (Z0, Z1, Z2), RELAY: (ZR,), Z_ALL: (Z0, Z1, Z2), OWN: (X1, Y1), PAIR: (X2, Y2), REST: (X0, Y0),
+        NEAR: (X0, Y0), ACROSS: (DX, DY), CORE: (C0,), Z_FAR: (ZR, Z1),
     }
-    gathers = ["aS", "ab0", "ab1", "ab2", "ab3", "adp", "au0", "ad0", "au1", "ad1", "au2", "ad2", "au3", "ad3"]
-    sums = ["ru0", "rd0", "ru1", "rd1", "ru2", "rd2", "ru3", "rd3", "ro", "rdl", "rh0", "rh1", "rh2", "rS"]
+    gathers = list(dict(aS=0, ab0=0, ab1=0, ab2=0, ab3=0, adp=0, au0=0, ad0=0, au1=0, ad1=0, au2=0, ad2=0, au3=0, ad3=0))
+    sums = list(dict(ru0=0, rd0=0, ru1=0, rd1=0, ru2=0, rd2=0, ru3=0, rd3=0, ro=0, rdl=0, rh0=0, rh1=0, rh2=0, rS=0))
     slots = []
     for names in (gathers, sums):
         places = {}
@@ -397,7 +419,7 @@
     count = tok.shape[0]
     pairs = width // 128
     chunks = count // CHUNK
-    wide_at, y = lax.axis_index("wide"), lax.axis_index("narrow")
+    wide_at, y = lax.axis_index(BOTH_AXES[0]), lax.axis_index(BOTH_AXES[1])
     core = lax.rem(wide_at, 2)
     x = lax.rem(lax.div(wide_at, 2), 2)
     z = lax.div(wide_at, 4)
@@ -462,24 +484,24 @@
             own = view((z, *along))
             return [remote(own, own, sems, row, k, along_z[k]) for k in which]
 
-        if phase == "z":
+        if phase == Z_TWO:
             return own_to(Z0, Z1)
-        if phase == "zd":
+        if phase == Z_ALL:
             return own_to(Z0, Z1, Z2)
-        if phase in ("z near", "z far", "z last"):
-            return own_to(("z near", "z far", "z last").index(phase))
-        if phase == "relay":
+        if phase in (Z_NEAR, Z_FAR, Z_LAST):
+            return own_to((Z_NEAR, Z_FAR, Z_LAST).index(phase))
+        if phase == RELAY:
             passed = view((z_places[1], *along))
             return [remote(passed, passed, sems, row, ZR, along_z[0], Z2)]
-        if phase == "own":
+        if phase == OWN:
             return both(z, X1)
-        if phase == "pair":
+        if phase == PAIR:
             return both(z_places[0], X2)
-        if phase == "rest":
+        if phase == REST:
             return both(other_pair, X0)
-        if phase == "near":
+        if phase == NEAR:
             return both(held, X0)
-        if phase == "across":
+        if phase == ACROSS:
             from_x, from_y = view((held, 1 - x, core, y)), view((held, x, core, 1 - y))
             first = half_of(from_x, 0)
             copies = [remote(first, first, sems, row, DY, to_y)]
@@ -492,48 +514,48 @@
 
     def ag_wait(unit, *phases):
         for phase in phases:
-            do_all(ag_copies(unit, phase), "wait_recv")
+            do_all(ag_copies(unit, phase), WAIT_RECV)
 
     def ag_stage(unit, stage):
         phases = unit[2]
         phase = phases[stage] if stage < len(phases) else None
-        if phase == "relay":
+        if phase == RELAY:
             @pl.when(inner)
             def _():
-                ag_wait(unit, "z far")
-                do_all(ag_copies(unit, "relay"), "start")
+                ag_wait(unit, Z_FAR)
+                do_all(ag_copies(unit, RELAY), START)
             return
-        if phase == "pair":
-            ag_wait(unit, "z near")
-        elif phase == "rest":
-            ag_wait(unit, "z far", "z last")
-        elif phase == "across" and "own" in phases:
-            ag_wait(unit, "own", "pair", "rest")
-        elif stage > 0 and phases[stage - 1] == "relay":
+        if phase == PAIR:
+            ag_wait(unit, Z_NEAR)
+        elif phase == REST:
+            ag_wait(unit, Z_FAR, Z_LAST)
+        elif phase == ACROSS and OWN in phases:
+            ag_wait(unit, OWN, PAIR, REST)
+        elif stage > 0 and phases[stage - 1] == RELAY:
             @pl.when(jnp.logical_not(inner))
             def _():
-                ag_wait(unit, "z far")
-            ag_wait(unit, "z near", "z last")
-        elif stage > 0 and phases[stage - 1] != "own":
+                ag_wait(unit, Z_FAR)
+            ag_wait(unit, Z_NEAR, Z_LAST)
+        elif stage > 0 and phases[stage - 1] != OWN:
             ag_wait(unit, phases[stage - 1])
         if phase:
-            do_all(ag_copies(unit, phase), "start")
-            if phase == "z":
+            do_all(ag_copies(unit, phase), START)
+            if phase == Z_TWO:
                 @pl.when(inner)
                 def _():
-                    do_all(ag_copies(unit, "z last"), "start")
+                    do_all(ag_copies(unit, Z_LAST), START)
         else:
             for sent in phases:
-                if sent != "relay":
-                    do_all(ag_copies(unit, sent), "wait_send")
-            if "relay" in phases:
+                if sent != RELAY:
+                    do_all(ag_copies(unit, sent), WAIT_SEND)
+            if RELAY in phases:
                 @pl.when(inner)
                 def _():
-                    do_all(ag_copies(unit, "z last") + ag_copies(unit, "relay"), "wait_send")
+                    do_all(ag_copies(unit, Z_LAST) + ag_copies(unit, RELAY), WAIT_SEND)
 
     def gather_unit(name, view):
-        kind = KINDS.get(name, "plain")
-        return (view, name, phases_of(name), plane if kind[:4] == "late" else one)
+        kind = KINDS.get(name, PLAIN)
+        return (view, name, phases_of(name), plane if kind[:4] == LATE else one)
 
     units = {"aS": gather_unit("aS", small_view(smalls)), "adp": gather_unit("adp", lambda at: downs.at[at])}
     for block in range(4):
@@ -546,23 +568,23 @@
         view, row, phases, landing, along = unit
         sems = True
         held = z if along is plane else ALL
-        if phase == "core":
-            return [remote(view((ALL, ALL, 1 - core, ALL)), landing["core"], sems, row, C0, to_c)]
-        if phase == "across":
+        if phase == CORE:
+            return [remote(view((ALL, ALL, 1 - core, ALL)), landing[CORE], sems, row, C0, to_c)]
+        if phase == ACROSS:
             away = view((held, 1 - x, core, 1 - y))
             copies = [remote(half_of(away, 0), landing["dx"], sems, row, DX, to_x)]
             if away.shape[-1] >= 2 * 128:
                 copies.append(remote(half_of(away, 1), landing["dy"], sems, row, DY, to_y))
             return copies
-        if phase == "near":
+        if phase == NEAR:
             return [
                 remote(view((held, 1 - x, core, y)), landing["x"], sems, row, X0, to_x),
                 remote(view((held, x, core, 1 - y)), landing["y"], sems, row, Y0, to_y),
             ]
-        if phase == "z outer":
-            return [remote(view((z_places[2], *along)), landing["z"].at[ZR], sems, row, ZR, along_z[0])]
-        which = {"z": (Z0,), "z far": (Z1,), "z last": (Z2,), "zd": (Z0, Z1, Z2)}[phase]
-        return [remote(view((z_places[k], *along)), landing["z"].at[k], sems, row, k, along_z[k]) for k in which]
+        if phase == Z_OUTER:
+            return [remote(view((z_places[2], *along)), landing[Z_TWO].at[ZR], sems, row, ZR, along_z[0])]
+        which = {Z_TWO: (Z0,), Z_FAR: (Z1,), Z_LAST: (Z2,), Z_ALL: (Z0, Z1, Z2)}[phase]
+        return [remote(view((z_places[k], *along)), landing[Z_TWO].at[k], sems, row, k, along_z[k]) for k in which]
 
     def add_into(target, *sources):
         total = target[...].astype(F32)
@@ -591,91 +613,91 @@
         held = z if along is plane else ALL
         before = phases[stage - 1] if stage > 0 else None
         phase = phases[stage] if stage < len(phases) else None
-        if phase == "z far":
+        if phase == Z_FAR:
             @pl.when(inner)
             def _():
-                do_all(rs_copies(unit, "z outer"), "wait_recv")
-                add_all(view((z_places[1], *along)), landing["z"].at[ZR])
-        elif before == "z far":
-            rs_wait(unit, "z", "z far")
-            add_all(view((z, *along)), landing["z"].at[Z0], landing["z"].at[Z1])
+                do_all(rs_copies(unit, Z_OUTER), WAIT_RECV)
+                add_all(view((z_places[1], *along)), landing[Z_TWO].at[ZR])
+        elif before == Z_FAR:
+            rs_wait(unit, Z_TWO, Z_FAR)
+            add_all(view((z, *along)), landing[Z_TWO].at[Z0], landing[Z_TWO].at[Z1])
 
             @pl.when(inner)
             def _():
-                rs_wait(unit, "z last")
-                add_all(view((z, *along)), landing["z"].at[Z2])
+                rs_wait(unit, Z_LAST)
+                add_all(view((z, *along)), landing[Z_TWO].at[Z2])
         elif before:
             rs_wait(unit, before)
-        if before == "core":
-            add_all(view((ALL, ALL, core, ALL)), landing["core"])
-        elif before == "across":
+        if before == CORE:
+            add_all(view((ALL, ALL, core, ALL)), landing[CORE])
+        elif before == ACROSS:
             on_y = view((held, x, core, 1 - y))
             add_all(half_of(on_y, 0), landing["dx"])
             if on_y.shape[-1] >= 2 * 128:
                 add_all(half_of(view((held, 1 - x, core, y)), 1), landing["dy"])
-        elif before == "near":
+        elif before == NEAR:
             add_all(view((held, x, core, y)), landing["x"], landing["y"])
-        elif before == "zd":
-            add_all(view((z, *along)), *[landing["z"].at[k] for k in (Z0, Z1, Z2)])
+        elif before == Z_ALL:
+            add_all(view((z, *along)), *[landing[Z_TWO].at[k] for k in (Z0, Z1, Z2)])
         if phase:
-            do_all(rs_copies(unit, phase), "start")
-        if phase == "z":
+            do_all(rs_copies(unit, phase), START)
+        if phase == Z_TWO:
             @pl.when(inner)
             def _():
-                do_all(rs_copies(unit, "z last"), "start")
+                do_all(rs_copies(unit, Z_LAST), START)
 
             @pl.when(jnp.logical_not(inner))
             def _():
-                do_all(rs_copies(unit, "z outer"), "start")
+                do_all(rs_copies(unit, Z_OUTER), START)
 
     def rs_wait(unit, *phases):
         for phase in phases:
-            do_all(rs_copies(unit, phase), "wait_recv")
+            do_all(rs_copies(unit, phase), WAIT_RECV)
 
     def rs_end(unit, *results):
         view, _, phases, landing, along = unit
         last = phases[-1]
-        if last == "near":
+        if last == NEAR:
             sources = [landing["x"], landing["y"]]
         else:
-            sources = [landing["z"].at[k] for k in ((Z0, Z1) if last == "z far" else (Z0, Z1, Z2))]
-        rs_wait(unit, *(("z", "z far") if last == "z far" else (last,)))
+            sources = [landing[Z_TWO].at[k] for k in ((Z0, Z1) if last == Z_FAR else (Z0, Z1, Z2))]
+        rs_wait(unit, *((Z_TWO, Z_FAR) if last == Z_FAR else (last,)))
         total = view((z, x, core, y))[...].astype(F32)
         for part in sources:
             total = total + part[...].astype(F32)
         size = total.shape[-1] // len(results)
         for k, result in enumerate(results):
             result[...] = total[:, k * size : (k + 1) * size]
-        if last == "z far":
+        if last == Z_FAR:
             @pl.when(inner)
             def _():
-                rs_wait(unit, "z last")
+                rs_wait(unit, Z_LAST)
                 for k, result in enumerate(results):
-                    result[...] += landing["z"][Z2, :, k * size : (k + 1) * size].astype(F32)
+                    result[...] += landing[Z_TWO][Z2, :, k * size : (k + 1) * size].astype(F32)
 
     def rs_sent(unit):
         for phase in unit[2]:
-            do_all(rs_copies(unit, phase), "wait_send")
-        if "z far" in unit[2]:
+            do_all(rs_copies(unit, phase), WAIT_SEND)
+        if Z_FAR in unit[2]:
             @pl.when(inner)
             def _():
-                do_all(rs_copies(unit, "z last"), "wait_send")
+                do_all(rs_copies(unit, Z_LAST), WAIT_SEND)
 
             @pl.when(jnp.logical_not(inner))
             def _():
-                do_all(rs_copies(unit, "z outer"), "wait_send")
+                do_all(rs_copies(unit, Z_OUTER), WAIT_SEND)
 
     def row_unit(block, name):
         if name in LATE_SUMS:
             late = LATE_SUMS.index(name)
-            landing = {"core": row_c.at[block], "dx": late_d.at[late, 0], "dy": late_d.at[late, 1], "x": late_n.at[late, 0], "y": late_n.at[late, 1], "z": late_z.at[late]}
+            landing = {CORE: row_c.at[block], "dx": late_d.at[late, 0], "dy": late_d.at[late, 1], "x": late_n.at[late, 0], "y": late_n.at[late, 1], Z_TWO: late_z.at[late]}
             return (row_view(block), name, phases_of(name), landing, plane)
         at = block - sum(earlier in LATE_SUMS for earlier in ROW_SUMS[:block])
-        landing = {"core": row_c.at[block], "dx": row_d.at[at, 0], "dy": row_d.at[at, 1], "x": row_n.at[at, 0], "y": row_n.at[at, 1], "z": row_z.at[at]}
+        landing = {CORE: row_c.at[block], "dx": row_d.at[at, 0], "dy": row_d.at[at, 1], "x": row_n.at[at, 0], "y": row_n.at[at, 1], Z_TWO: row_z.at[at]}
         return (row_view(block), name, phases_of(name), landing, one)
 
     def down_unit(tile, name):
-        landing = {"core": down_c.at[tile], "dx": down_d.at[tile, 0], "dy": down_d.at[tile, 1], "x": down_n.at[tile, 0], "y": down_n.at[tile, 1]}
+        landing = {CORE: down_c.at[tile], "dx": down_d.at[tile, 0], "dy": down_d.at[tile, 1], "x": down_n.at[tile, 0], "y": down_n.at[tile, 1]}
         return (down_view(tile), name, phases_of(name), landing, one)
 
     def block_columns(block):
@@ -691,9 +713,9 @@
         units[f"rh{g}"] = row_unit(g, f"rh{g}")
         results[f"rh{g}"] = [gqkv.at[:, pl.ds(j * width + g * third, third)] for j in range(3)]
     units["ro"] = row_unit(3, "ro")
-    small_landing = {"core": sm_c, "dx": sm_d, "x": sm_n.at[0], "y": sm_n.at[1], "z": sm_z}
+    small_landing = {CORE: sm_c, "dx": sm_d, "x": sm_n.at[0], "y": sm_n.at[1], Z_TWO: sm_z}
     units["rS"] = (small_view(gsmalls), "rS", phases_of("rS"), small_landing, one)
-    units["rdl"] = (lambda at: downs.at[at], "rdl", phases_of("rdl"), {"z": down_z}, one)
+    units["rdl"] = (lambda at: downs.at[at], "rdl", phases_of("rdl"), {Z_TWO: down_z}, one)
     whole_results = {"rdl": [gdown_ref], "ro": [gout_ref], "rS": [gsmall_ref]}
     for t in range(n_z):
         whole_results[f"ru{t}"] = [gup_ref.at[:, block_columns(t)]]
@@ -733,7 +755,7 @@
     shards.append((wdown_ref, downs.at[z, x, core, y]))
     shard_copies = [pltpu.make_async_copy(src, dst, local.at[k]) for k, (src, dst) in enumerate(shards)]
     row_copies = [pltpu.make_async_copy(tok_ref, tok, local.at[len(shards)]), pltpu.make_async_copy(cot_ref, cot, local.at[len(shards) + 1])]
-    do_all(shard_copies + row_copies, "start")
+    do_all(shard_copies + row_copies, START)
     smalls[z, x, core, y] = jnp.zeros((8, 128), F32)
     for k, vector in enumerate((v0, v1, v2, v3, v4, v5, v6, v7)):
         smalls[z, x, core, y, k, 0 : vector.shape[0]] = vector[...].astype(F32)
@@ -1199,71 +1221,75 @@
         copy.wait()
 
 
-KINDS = {
-    "ab1": "boot",
-    "ab2": "boot",
-    "au0": "direct",
-    "au1": "late",
-    "au2": "late",
-    "au3": "boot",
-    "ro": "late",
-    "ru0": "late",
-    "ru2": "late",
-}
-LATE_SUMS = ("ro", "ru0", "ru2")
-TABLE = {
-    "mask": (("au0", 0), ("ab1", 0), ("au2", 0), ("ab2", 0),),
-    "vec": (("ab0", 0), ("au3", 0), ("aS", 0), ("ab1", 1), ("au2", 1), ("ab3", 0), ("au0", 1), ("ab0", 1), ("ab2", 1), ("aS", 1), ("ab1", 2), ("adp", 0), ("au0", 2), ("au1", 0), ("aS", 2), ("ab1", 3), ("ab3", 1), ("ab0", 2), ("au0", 3), ("aS", 3), ("au1", 1), ("au0", 4), ("ab2", 2), ("aS", 4),),
-    "turn": (("ab1", 4),),
-    "q0": (("ab2", 3), ("adp", 1), ("au1", 2), ("ab0", 3), ("ab1", 5), ("ab3", 2), ("ab1", 6), ("ab2", 4), ("ab0", 4), ("adp", 2), ("ad0", 0), ("ab0", 5),),
-    "t1": (("ab3", 3), ("au1", 3), ("au3", 1),),
-    "q1": (("ad1", 0), ("ab2", 5),),
-    "q2": (("ad0", 1), ("au2", 2), ("ab2", 6),),
-    "t4": (("ab3", 4), ("au1", 4),),
-    "t5": (("ad2", 0),),
-    "tb": (("ab3", 5),),
-    "n2a": (("au1", 5), ("ad1", 1),),
-    "n2b": (("ad0", 2),),
-    "fa0": (("au3", 2),),
-    "fc0": (("au3", 3), ("ad0", 3),),
-    "fe0": (("ad2", 1),),
-    "ff0": (("au2", 3),),
-    "fg0": (("ad1", 2), ("ad3", 0),),
-    "fi0": (("ru0", 0),),
-    "fa1": (("rd0", 0),),
-    "fc1": (("ad1", 3),),
-    "fe1": (("au3", 4),),
-    "ff1": (("ru0", 1), ("ad2", 2),),
-    "fg1": (("rd0", 1), ("au2", 4),),
-    "fi1": (("ru1", 0),),
-    "fa2": (("rd1", 0), ("ad2", 3), ("ad3", 1), ("au2", 5),),
-    "fc2": (("au3", 5),),
-    "fe2": (("ru1", 1), ("ru0", 2), ("rd0", 2),),
-    "fg2": (("ad3", 2),),
-    "fi2": (("ru2", 0), ("au3", 6),),
-    "fa3": (("rd1", 1), ("rd2", 0),),
-    "fc3": (("ad3", 3),),
-    "fe3": (("ru1", 2), ("ru2", 1),),
-    "fg3": (("rd0", 3),),
-    "fi3": (("ru3", 0), ("rd2", 1),),
-    "ba": (("rd3", 0),),
-    "bb": (("rd1", 2),),
-    "ga": (("ro", 0), ("ru2", 2),),
-    "a1": (("ru3", 1), ("rd3", 1), ("ro", 1),),
-    "H0": (("rd1", 3), ("rd2", 2),),
-    "a2": (("ru1", 3), ("rh0", 0),),
-    "a3": (("ro", 2), ("ru3", 2),),
-    "H1": (("rd3", 2),),
-    "a4": (("rh1", 0), ("rd2", 3),),
-    "a5": (("rh1", 1), ("ru3", 3),),
-    "H2": (("ru1", 4), ("rh0", 1), ("ru0", 3),),
-    "g2": (("rh2", 0), ("ru3", 4), ("rd3", 3), ("rdl", 0), ("ru2", 3),),
-    "g0": (("rh1", 2),),
-    "nb": (("rh2", 1),),
-    "end": (("ro", 3), ("rS", 0), ("ru1", 5), ("rdl", 1), ("ru3", 5), ("rh0", 2), ("rS", 1), ("ru0", 4), ("rh2", 2), ("rh1", 3), ("rh0", 3), ("ro", 4), ("rS", 2), ("rh1", 4), ("ru0", 5), ("ru2", 4), ("rh0", 4), ("rdl", 2), ("rh2", 3), ("ro", 5), ("rS", 3), ("ru2", 5), ("rh1", 5), ("rh2", 4), ("rh0", 5), ("rS", 4), ("rh2", 5),),
-}
-
-ROW_SUMS = ("rh0", "rh1", "rh2", "ro", "ru0", "ru1", "ru2", "ru3")
+def step(**named):
+    return next(iter(named.items()))
+
+
+KINDS = dict(
+    ab1=BOOT,
+    ab2=BOOT,
+    au0=DIRECT,
+    au1=LATE,
+    au2=LATE,
+    au3=BOOT,
+    ro=LATE,
+    ru0=LATE,
+    ru2=LATE,
+)
+LATE_SUMS = tuple(dict(ro=0, ru0=0, ru2=0))
+TABLE = dict(
+    mask=(step(au0=0), step(ab1=0), step(au2=0), step(ab2=0),),
+    vec=(step(ab0=0), step(au3=0), step(aS=0), step(ab1=1), step(au2=1), step(ab3=0), step(au0=1), step(ab0=1), step(ab2=1), step(aS=1), step(ab1=2), step(adp=0), step(au0=2), step(au1=0), step(aS=2), step(ab1=3), step(ab3=1), step(ab0=2), step(au0=3), step(aS=3), step(au1=1), step(au0=4), step(ab2=2), step(aS=4),),
+    turn=(step(ab1=4),),
+    q0=(step(ab2=3), step(adp=1), step(au1=2), step(ab0=3), step(ab1=5), step(ab3=2), step(ab1=6), step(ab2=4), step(ab0=4), step(adp=2), step(ad0=0), step(ab0=5),),
+    t1=(step(ab3=3), step(au1=3), step(au3=1),),
+    q1=(step(ad1=0), step(ab2=5),),
+    q2=(step(ad0=1), step(au2=2), step(ab2=6),),
+    t4=(step(ab3=4), step(au1=4),),
+    t5=(step(ad2=0),),
+    tb=(step(ab3=5),),
+    n2a=(step(au1=5), step(ad1=1),),
+    n2b=(step(ad0=2),),
+    fa0=(step(au3=2),),
+    fc0=(step(au3=3), step(ad0=3),),
+    fe0=(step(ad2=1),),
+    ff0=(step(au2=3),),
+    fg0=(step(ad1=2), step(ad3=0),),
+    fi0=(step(ru0=0),),
+    fa1=(step(rd0=0),),
+    fc1=(step(ad1=3),),
+    fe1=(step(au3=4),),
+    ff1=(step(ru0=1), step(ad2=2),),
+    fg1=(step(rd0=1), step(au2=4),),
+    fi1=(step(ru1=0),),
+    fa2=(step(rd1=0), step(ad2=3), step(ad3=1), step(au2=5),),
+    fc2=(step(au3=5),),
+    fe2=(step(ru1=1), step(ru0=2), step(rd0=2),),
+    fg2=(step(ad3=2),),
+    fi2=(step(ru2=0), step(au3=6),),
+    fa3=(step(rd1=1), step(rd2=0),),
+    fc3=(step(ad3=3),),
+    fe3=(step(ru1=2), step(ru2=1),),
+    fg3=(step(rd0=3),),
+    fi3=(step(ru3=0), step(rd2=1),),
+    ba=(step(rd3=0),),
+    bb=(step(rd1=2),),
+    ga=(step(ro=0), step(ru2=2),),
+    a1=(step(ru3=1), step(rd3=1), step(ro=1),),
+    H0=(step(rd1=3), step(rd2=2),),
+    a2=(step(ru1=3), step(rh0=0),),
+    a3=(step(ro=2), step(ru3=2),),
+    H1=(step(rd3=2),),
+    a4=(step(rh1=0), step(rd2=3),),
+    a5=(step(rh1=1), step(ru3=3),),
+    H2=(step(ru1=4), step(rh0=1), step(ru0=3),),
+    g2=(step(rh2=0), step(ru3=4), step(rd3=3), step(rdl=0), step(ru2=3),),
+    g0=(step(rh1=2),),
+    nb=(step(rh2=1),),
+    end=(step(ro=3), step(rS=0), step(ru1=5), step(rdl=1), step(ru3=5), step(rh0=2), step(rS=1), step(ru0=4), step(rh2=2), step(rh1=3), step(rh0=3), step(ro=4), step(rS=2), step(rh1=4), step(ru0=5), step(ru2=4), step(rh0=4), step(rdl=2), step(rh2=3), step(ro=5), step(rS=3), step(ru2=5), step(rh1=5), step(rh2=4), step(rh0=5), step(rS=4), step(rh2=5),),
+)
+
+ROW_SUMS = tuple(dict(rh0=0, rh1=0, rh2=0, ro=0, ru0=0, ru1=0, ru2=0, ru3=0))
 VMEM_BYTES = 63 * 1024 * 1024
 
 
@@ -1286,9 +1312,8 @@
 
 
 def solution(mesh):
-    n_wide, n_narrow = mesh.shape["wide"], mesh.shape["narrow"]
-    both = ("wide", "narrow")
-    matrix, vector = P(both, None), P(both)
+    n_wide, n_narrow = [mesh.shape[axis] for axis in BOTH_AXES]
+    matrix, vector = P(BOTH_AXES, None), P(BOTH_AXES)
     in_specs = (
         matrix, matrix, matrix, vector, vector, matrix, vector, matrix, vector, vector, vector, matrix, vector, matrix, vector,
     )

time: 128 us -> 128 us (level)
  no operation moved by 1% of the time
where the time goes in v7:
time: 128 us
  Pallas kernels  127 us (99%)
    pallas_call x1, Pallas kernels, by_kernel(): pl.pallas_call(layer_kernel, out_shape=(shape((count, width), BF16), shap...  124 us
    pallas_call x1, Pallas kernels, by_kernel(): pl.pallas_call(hand_over, out_shape=tuple((shape(a.shape, a.dtype) for a...  3.42 us

profile of v7, /device:TPU:0, one launch (start us, length us, event | category | flops | bytes accessed | tf_op | source)
XLA Modules:
  0.0 128.1 jit_solution(6359665040557426044)
XLA Ops:
  0.7 123.9 %shard_map.254 = (bf16[512,768]{1,0:T(8,128)(2,1)}, f32[512,768]{1,0:T(8,128)}, f32[24,2304]{1,0:T(8,128)}, f32[24,768]{1,0:T(8,128)}, f32[24,3072]{1,0:T(8,128)}, /*index=5*/f32[96,768]{1,0:T(8,128)}, f32[8,128]{1,0:T(8,128)}) custom-call(s32[1,3]{1,0:T(1,128)} %clip_ref.1, bf16[512,768]{1,0:T(8,128)(2,1)} %tok_ref.1, bf16[512,768]{1,0:T(8,128)(2,1)} %cot_ref.1, ...), custom_call_target="tpu_custom_call" | custom-call | tf_op jit(solution)/shard_map/pallas_call | solution.py:1167
  124.5 3.4 %shard_map.255 = (bf16[512,768]{1,0:T(8,128)(2,1)}, f32[512,768]{1,0:T(8,128)}, f32[24,2304]{1,0:T(8,128)}, f32[24,768]{1,0:T(8,128)}, f32[24,3072]{1,0:T(8,128)...) custom-call(f32[8,128]{1,0:T(8,128)} %get-tuple-element.35.refs_0_, ...), custom_call_target="tpu_custom_call" | custom-call | tf_op jit(solution)/shard_map/pallas_call | solution.py:1184

commit v8 on v7

--- a/solution.py
+++ b/solution.py
@@ -15,6 +15,7 @@
 BF16 = jnp.bfloat16
 ALL = slice(None)
 CHUNK = 256
+LAST_POINT = "end"
 BOTH_AXES = ("wide", "narrow")
 ACROSS = "across"
 Z_FAR = "z far"
@@ -723,8 +724,16 @@
         whole_results[f"rh{g}"] = [gqkv_ref.at[:, pl.ds(j * width + g * third, third)] for j in range(3)]
     last_copies = []
 
+    def set_of_sums():
+        return [unit_name for unit_name in units if unit_name[0] == "r"]
+
     def point(name):
-        for unit_name, stage in TABLE.get(name, ()):
+        listed = TABLE.get(name, ())
+        for place, (unit_name, stage) in enumerate(listed):
+            if name == LAST_POINT and place == len(listed) - 2:
+                for other in set_of_sums():
+                    if other not in (unit_name, listed[-1][0]):
+                        rs_sent(units[other])
             unit = units[unit_name]
             if unit_name[0] == "a":
                 ag_stage(unit, stage)
@@ -1086,10 +1095,9 @@
     for k in range(n_z):
         gsmalls[k] = gsmalls[k] + gather_back(up_sums[k], 96).reshape(2, 2, 2, 8, 128)
 
-    point("end")
-    for name, unit in units.items():
-        if name[0] == "r":
-            rs_sent(unit)
+    point(LAST_POINT)
+    for unit_name in dict(TABLE[LAST_POINT][-2:]):
+        rs_sent(units[unit_name])
     out_copy.wait()
     tgrad_copy.wait()
     do_all(last_copies, "wait")

time: 128 us -> 128 us (level)
  no operation moved by 1% of the time
where the time goes in v8:
time: 128 us
  Pallas kernels  127 us (99%)
    pallas_call x1, Pallas kernels, by_kernel(): pl.pallas_call(layer_kernel, out_shape=(shape((count, width), BF16), shap...  124 us
    pallas_call x1, Pallas kernels, by_kernel(): pl.pallas_call(hand_over, out_shape=tuple((shape(a.shape, a.dtype) for a...  3.42 us

profile of v8, /device:TPU:0, one launch (start us, length us, event | category | flops | bytes accessed | tf_op | source)
XLA Modules:
  0.0 128.1 jit_solution(4032438464881017020)
XLA Ops:
  0.7 123.9 %shard_map.254 = (bf16[512,768]{1,0:T(8,128)(2,1)}, f32[512,768]{1,0:T(8,128)}, f32[24,2304]{1,0:T(8,128)}, f32[24,768]{1,0:T(8,128)}, f32[24,3072]{1,0:T(8,128)}, /*index=5*/f32[96,768]{1,0:T(8,128)}, f32[8,128]{1,0:T(8,128)}) custom-call(s32[1,3]{1,0:T(1,128)} %clip_ref.1, bf16[512,768]{1,0:T(8,128)(2,1)} %tok_ref.1, bf16[512,768]{1,0:T(8,128)(2,1)} %cot_ref.1, ...), custom_call_target="tpu_custom_call" | custom-call | tf_op jit(solution)/shard_map/pallas_call | solution.py:1175
  124.5 3.4 %shard_map.255 = (bf16[512,768]{1,0:T(8,128)(2,1)}, f32[512,768]{1,0:T(8,128)}, f32[24,2304]{1,0:T(8,128)}, f32[24,768]{1,0:T(8,128)}, f32[24,3072]{1,0:T(8,128)...) custom-call(f32[8,128]{1,0:T(8,128)} %get-tuple-element.35.refs_0_, ...), custom_call_target="tpu_custom_call" | custom-call | tf_op jit(solution)/shard_map/pallas_call | solution.py:1192
